TPU v7x, 32 devices: a whole 2x2x4 slice. The times are simulated.
32 devices in a mesh: gx: 8 (over z, x), gy: 4 (over y, core).
Axes of the slice: x: 2, y: 2, z: 4, core: 2. Of those that a mesh axis runs over, the one named last changes fastest.
Arguments:
- eigen: float32 [256, 256, 256], P('gx', 'gy'), may hold values from -6 to 6
- seg_vec: float32 [6, 8, 4, 2048], P(None, 'gx', 'gy'), may hold values from -5 to 5
- seg_off: float32 [3, 8, 4, 2048], P(None, 'gx', 'gy'), may hold values from 0 to 1
- seg_cell: int32 [8, 4, 2048], P('gx', 'gy'), may hold values from 0 to 524287
- blk_count: int32 [8, 4, 16], P('gx', 'gy'), may hold values from 0 to 128, as said below
- pair_list: int32 [8, 4, 16, 8], P('gx', 'gy'), may hold values from 0 to 143, as said below
Outputs:
- stress_field: float32 [256, 256, 256], P('gx', 'gy')
- seg_force: float32 [3, 8, 4, 2048], P(None, 'gx', 'gy')
Inputs may be any that keep to these rules, and one draw needn't show every extreme that they name: `blk_count`: A block's live segments fill its first slots; at least one device holds 16 full blocks of 128; every device holds a block with segments. `pair_list`: the 8 entries of one block are distinct.
All inputs are finite; a program needn't handle non-finite values.
Results may differ from a plain program's by a relative error of at most 0.0003.
Values sent between devices are 32-bit elements; how exact they have to be, the bound alone decides.
No kernel may reach another device: no remote copies, remote signals or barrier semaphores. Data moves between devices by JAX's collectives and lax.ppermute only.
A program may use at most 64 MiB of HBM per device.

v0:
```python
import math

import jax
import jax.numpy as jnp
from jax import lax
from jax.sharding import PartitionSpec as P

nu_copper = 0.34
core_sq = 4.0
pair_scale = 4.0


def extended(block, sides, width):
    for axis, dim in sides:
        count = lax.axis_size(axis)
        forward = [(i, i + 1) for i in range(count - 1)]
        forward.append((count - 1, 0))
        backward = [(target, source) for source, target in forward]
        low = lax.ppermute(
            lax.slice_in_dim(block, block.shape[dim] - width, None, axis=dim), axis, forward
        )
        high = lax.ppermute(lax.slice_in_dim(block, 0, width, axis=dim), axis, backward)
        block = jnp.concatenate([low, block, high], axis=dim)
    return block


def wave_tables(length):
    steps = jnp.arange(length, dtype=jnp.int32)
    phase = steps[:, None] * steps[None, :] % length
    angle = phase.astype(jnp.float32) * (2.0 * math.pi / length)
    return (jnp.cos(angle), jnp.sin(angle))


def product(form, left, table):
    return jnp.einsum(form, left, table, precision=lax.Precision.HIGHEST)


def forward(real_part, imag_part, form, cos_table, sin_table):
    first = product(form, real_part, cos_table) + product(form, imag_part, sin_table)
    second = product(form, imag_part, cos_table) - product(form, real_part, sin_table)
    return jnp.stack([first, second])


def backward(real_part, imag_part, form, cos_table, sin_table):
    first = product(form, real_part, cos_table) - product(form, imag_part, sin_table)
    second = product(form, real_part, sin_table) + product(form, imag_part, cos_table)
    return jnp.stack([first, second])


def wave_sq(freq, length):
    sine = 2.0 * jnp.sin(math.pi * freq.astype(jnp.float32) / length)
    return sine * sine


def multiplier(wave_x, wave_y, wave_z, anchor):
    total = wave_x + wave_y + wave_z
    safe = jnp.where(anchor, 1.0, total)
    return -2.0 * (
        1.0 - (wave_x + wave_z) / safe + 2.0 * wave_x * wave_z / ((1.0 - nu_copper) * safe * safe)
    )


def block_force(own_data, far_data, tau_own):
    deltas = [own_data[k][:, None] - far_data[k][None, :] for k in range(3)]
    dist_sq = deltas[0] * deltas[0] + deltas[1] * deltas[1] + deltas[2] * deltas[2] + core_sq
    inverse = 1.0 / jnp.sqrt(dist_sq)
    inv_three = inverse * inverse * inverse
    inv_five = inv_three * inverse * inverse
    burg_dot = (
        own_data[3][:, None] * far_data[3][None, :]
        + own_data[4][:, None] * far_data[4][None, :]
        + own_data[5][:, None] * far_data[5][None, :]
    )
    line_dot = (
        own_data[6][:, None] * far_data[6][None, :]
        + own_data[7][:, None] * far_data[7][None, :]
        + own_data[8][:, None] * far_data[8][None, :]
    )
    burg_own = (
        own_data[3][:, None] * deltas[0]
        + own_data[4][:, None] * deltas[1]
        + own_data[5][:, None] * deltas[2]
    )
    burg_far = (
        far_data[3][None, :] * deltas[0]
        + far_data[4][None, :] * deltas[1]
        + far_data[5][None, :] * deltas[2]
    )
    weight = line_dot * (burg_dot * inv_three - 3.0 * burg_own * burg_far * inv_five)
    pair_pull = jnp.stack([jnp.sum(weight * deltas[k], axis=1) for k in range(3)])
    burgers = own_data[3:6]
    tangent = own_data[6:9]
    glide_dir = jnp.stack(
        [
            burgers[1] * tangent[2] - burgers[2] * tangent[1],
            burgers[2] * tangent[0] - burgers[0] * tangent[2],
            burgers[0] * tangent[1] - burgers[1] * tangent[0],
        ]
    )
    return pair_scale * pair_pull + tau_own[None, :] * glide_dir


def per_device(eigen, seg_vec, seg_off, seg_cell, blk_count, pair_list):
    plane_x, plane_y, length = eigen.shape
    groups_x = lax.axis_size("gx")
    groups_y = lax.axis_size("gy")
    cos_table, sin_table = wave_tables(length)
    scale = 1.0 / float(length) ** 3
    flat = eigen.reshape(plane_x * plane_y, length)
    zeta = jnp.stack(
        [product("mz,zk->km", flat, cos_table), -product("mz,zk->km", flat, sin_table)]
    )
    depth_z = length // groups_x
    width_x = length // groups_y
    swapped = lax.all_to_all(zeta, "gx", split_axis=1, concat_axis=2, tiled=True).reshape(
        2, depth_z, length, plane_y
    )
    along_x = forward(swapped[0], swapped[1], "zxy,xk->kzy", cos_table, sin_table).reshape(
        2, length, depth_z * plane_y
    )
    turned = lax.all_to_all(along_x, "gy", split_axis=1, concat_axis=2, tiled=True).reshape(
        2, width_x, groups_y, depth_z, plane_y
    )
    cos_y = cos_table.reshape(groups_y, plane_y, length)
    sin_y = sin_table.reshape(groups_y, plane_y, length)
    spectrum = forward(turned[0], turned[1], "ksqy,syl->kql", cos_y, sin_y)
    freq_x = lax.axis_index("gy") * width_x + jnp.arange(width_x, dtype=jnp.int32)
    freq_z = lax.axis_index("gx") * depth_z + jnp.arange(depth_z, dtype=jnp.int32)
    freq_y = jnp.arange(length, dtype=jnp.int32)
    anchor = (
        (freq_x[:, None, None] == 0) & (freq_z[None, :, None] == 0) & (freq_y[None, None, :] == 0)
    )
    gain = (
        multiplier(
            wave_sq(freq_x, length)[:, None, None],
            wave_sq(freq_y, length)[None, None, :],
            wave_sq(freq_z, length)[None, :, None],
            anchor,
        )
        * scale
    )
    spectrum = spectrum * gain[None]
    back_y = backward(spectrum[0], spectrum[1], "kql,yl->ykq", cos_table, sin_table).reshape(
        2, length, width_x * depth_z
    )
    returned = lax.all_to_all(back_y, "gy", split_axis=1, concat_axis=2, tiled=True).reshape(
        2, plane_y, length, depth_z
    )
    back_x = backward(returned[0], returned[1], "ykq,xk->xyq", cos_table, sin_table).reshape(
        2, length, plane_y * depth_z
    )
    landed = lax.all_to_all(back_x, "gx", split_axis=1, concat_axis=2, tiled=True).reshape(
        2, plane_x, groups_x, plane_y, depth_z
    )
    cos_z = cos_table.reshape(groups_x, depth_z, length)
    sin_z = sin_table.reshape(groups_x, depth_z, length)
    stress = product("xsyq,sqz->xyz", landed[0], cos_z) - product("xsyq,sqz->xyz", landed[1], sin_z)
    cells = seg_cell[0, 0]
    seg_total = cells.shape[0]
    block_total = blk_count.shape[2]
    width = seg_total // block_total
    coord_z = cells % length
    coord_y = cells // length % plane_y
    coord_x = cells // (length * plane_y)
    position = jnp.stack([coord_x, coord_y, coord_z]).astype(jnp.float32) + seg_off[:, 0, 0]
    counts = blk_count[0, 0]
    live = (
        (jnp.arange(width, dtype=jnp.int32)[None, :] < counts[:, None])
        .reshape(seg_total)
        .astype(jnp.float32)
    )
    source = jnp.concatenate(
        [position, seg_vec[0:3, 0, 0] * live[None, :], seg_vec[3:6, 0, 0]], axis=0
    )
    nearby = extended(source[:, None, None, :], (("gx", 1), ("gy", 2)), 1)
    shift = (jnp.arange(3, dtype=jnp.int32) - 1).astype(jnp.float32)
    nearby = (
        nearby.at[0].add(shift[:, None, None] * plane_x).at[1].add(shift[None, :, None] * plane_y)
    )
    source_pool = nearby.reshape(9, 9 * block_total, width)
    sampled = stress.reshape(-1)[cells]
    own_blocks = source.reshape(9, block_total, width).transpose(1, 0, 2)
    tau_blocks = sampled.reshape(block_total, width)

    def one_block(inputs):
        own_data, partner_ids, count, tau_own = inputs
        far_data = source_pool[:, partner_ids].reshape(9, -1)
        return block_force(own_data, far_data, tau_own)

    forces = lax.map(one_block, (own_blocks, pair_list[0, 0], counts, tau_blocks))
    seg_force = forces.transpose(1, 0, 2).reshape(3, 1, 1, seg_total)
    return (stress, seg_force)


def solution(mesh):
    return jax.shard_map(
        per_device,
        mesh=mesh,
        in_specs=(
            P("gx", "gy", None),
            P(None, "gx", "gy", None),
            P(None, "gx", "gy", None),
            P("gx", "gy", None),
            P("gx", "gy", None),
            P("gx", "gy", None, None),
        ),
        out_specs=(P("gx", "gy", None), P(None, "gx", "gy", None)),
        check_vma=False,
    )
```

profile of v0, /device:TPU:11, one launch (start us, length us, event | category | flops | bytes accessed | tf_op | source)
XLA Modules:
  0.0 599.2 jit_solution(18181618794963317839)
XLA Ops:
  2.2 4.4 convolution_bitcast_fusion
  6.6 4.4 fusion.27
  15.0 95.6 %all_to_all.60 = f32[2,256,2048]{2,0,1:T(2,128)S(1)} all-to-all(f32[2,256,2048]{2,0,1:T(2,128)S(1)} %copy.124), channel_id=1, replica_groups=mesh['gx'=8,'gy'=4] {'gx'}, dimensions={1} | all-to-all | bytes 8388608 | tf_op jit(solution)/shard_map/all_to_all | solution.py:115
  120.4 4.2 fusion.111
  124.7 4.2 fusion.100
  128.8 4.9 squeeze.85
  145.7 6.2 %copy.130 = f32[1,256,2048]{2,0,1:T(1,128)} copy(f32[1,256,2048]{1,2,0:T(8,128)} %bitcast.357) | data formatting | bytes 4194304 | tf_op jit(solution)/shard_map/stack | solution.py:41
  155.2 6.3 %copy.131 = f32[1,256,2048]{2,0,1:T(1,128)} copy(f32[1,256,2048]{1,2,0:T(8,128)} %bitcast.358) | data formatting | bytes 4194304 | tf_op jit(solution)/shard_map/stack | solution.py:41
  161.5 7.3 %pad_maximum_fusion.1 = f32[2,256,2048]{2,0,1:T(2,128)} fusion(f32[1,256,2048]{2,0,1:T(1,128)} %copy.131, f32[1,256,2048]{2,0,1:T(1,128)S(1)} %copy-done.10), kind=kLoop, calls=%fused_computation.66 | loop fusion | flops 1048576 | bytes 8388608 | tf_op jit(solution)/shard_map/stack | solution.py:41
  168.8 7.2 %all-to-all-start.1 = ((f32[2,256,2048]{2,0,1:T(2,128)}), f32[2,256,2048]{2,0,1:T(2,128)}, u32[]{:S(2)}, u32[]{:S(2)}) async-start(f32[2,256,2048]{2,0,1:T(2,128)} %pad_maximum_fusion.1), calls=%async_computation.1 | async-start | bytes 8388608 | tf_op jit(solution)/shard_map/all_to_all | solution.py:121
  179.0 44.3 %all-to-all-done.1 = f32[2,256,2048]{2,0,1:T(2,128)} async-done(((f32[2,256,2048]{2,0,1:T(2,128)}), f32[2,256,2048]{2,0,1:T(2,128)}, u32[]{:S(2)}, u32[]{:S(2)}) %all-to-all-start.1) | async-done | bytes 4194336 | tf_op jit(solution)/shard_map/all_to_all | solution.py:121
  223.3 4.6 copy.132
  240.8 8.1 %fusion.68 = f32[64,32,256,1]{2,1,3,0:T(8,128)S(1)} fusion(f32[64,4,32,64]{3,2,1,0:T(8,128)} %squeeze.87, s32[4,64]{1,0:T(4,128)S(1)} %multiply_add_fusion.1), kind=kOutput, calls=%fused_computation.129 | convolution fusion | flops 1611530240 | bytes 4195328 | tf_op jit(solution)/shard_map/ksqy,syl->kql/dot_general | solution.py:35
  248.8 4.7 fusion.66
  253.5 4.5 fusion.32
  258.0 5.2 fusion.31
  284.6 7.4 %copy.141 = f32[2,256,2048]{2,0,1:T(2,128)} copy(f32[2,256,2048]{1,2,0:T(8,128)} %pad_maximum_fusion.2) | data formatting | bytes 8388608 | tf_op jit(solution)/shard_map/stack | solution.py:47
  292.0 52.0 %all_to_all.61 = f32[2,256,2048]{2,0,1:T(2,128)S(1)} all-to-all(f32[2,256,2048]{2,0,1:T(2,128)} %copy.141), channel_id=1, replica_groups=mesh['gx'=8,'gy'=4] {'gy'}, dimensions={1} | all-to-all | bytes 8388608 | tf_op jit(solution)/shard_map/all_to_all | solution.py:146
  354.3 4.2 fusion.71
  358.5 4.2 fusion.59
  370.4 4.6 convolution_subtract_fusion
  383.1 7.3 %copy.151 = f32[2,256,2048]{2,0,1:T(2,128)} copy(f32[2,256,2048]{1,2,0:T(8,128)} %pad_maximum_fusion.3) | data formatting | bytes 8388608 | tf_op jit(solution)/shard_map/stack | solution.py:47
  390.5 6.5 %all-to-all-start.3 = ((f32[2,256,2048]{2,0,1:T(2,128)}), f32[2,256,2048]{2,0,1:T(2,128)}, u32[]{:S(2)}, u32[]{:S(2)}) async-start(f32[2,256,2048]{2,0,1:T(2,128)} %copy.151), calls=%async_computation.3 | async-start | bytes 8388608 | tf_op jit(solution)/shard_map/all_to_all | solution.py:152
  399.0 91.3 %collective-permute-done = f32[9,1,1,2048]{3,0,2,1:T(8,128)S(1)} collective-permute-done((f32[9,1,1,2048]{3,0,2,1:T(8,128)S(1)}, f32[9,1,1,2048]{3,0,2,1:T(8,128)S(1)}, u32[]{:S(2)}, u32[]{:S(2)}) %collective-permute-start) | collective-permute-done | bytes 73760 | tf_op jit(solution)/shard_map/ppermute | solution.py:19
  493.2 7.3 %collective-permute-done.2 = f32[9,3,1,2048]{3,0,2,1:T(8,128)S(1)} collective-permute-done((f32[9,3,1,2048]{3,0,2,1:T(8,128)S(1)}, f32[9,3,1,2048]{3,0,2,1:T(8,128)S(1)}, u32[]{:S(2)}, u32[]{:S(2)}) %collective-permute-start.2) | collective-permute-done | bytes 221216 | tf_op jit(solution)/shard_map/ppermute | solution.py:19
  507.4 4.6 copy.152
  513.6 6.3 %reshape.1054 = f32[32,8,64,32]{3,2,0,1:T(8,128)} reshape(f32[1,32,8,2048]{3,1,2,0:T(8,128)} %get-tuple-element.127) | data formatting | bytes 4194304 | tf_op jit(solution)/shard_map/squeeze | solution.py:157
  520.0 4.8 reshape.1055
  524.7 9.0 %fusion.57 = f32[32,64,256,1]{2,1,0,3:T(8,128)S(1)} fusion(f32[32,8,64,32]{3,2,0,1:T(8,128)} %reshape.1054, s32[8,32]{1,0:T(8,128)S(1)} %multiply_add_fusion), kind=kOutput, calls=%fused_computation.118 | convolution fusion | flops 1611530240 | bytes 4195328 | tf_op jit(solution)/shard_map/xsyq,sqz->xyz/dot_general | solution.py:35
  533.8 7.8 %bitcast_subtract_fusion = f32[32,64,256]{2,1,0:T(8,128)S(1)} fusion(f32[32,64,256,1]{2,1,0,3:T(8,128)S(1)} %fusion.57, f32[32,8,64,32]{3,2,0,1:T(8,128)S(1)} %copy-done.4, s32[8,32]{1,0:T(8,128)S(1)} %multiply_add_fusion), kind=kOutput, calls=%fused_computation.80 | convolution fusion | flops 1612054528 | bytes 6292480 | tf_op jit(solution)/shard_map/xsyq,sqz->xyz/dot_general | solution.py:35
  544.0 24.5 %gather_fusion.1 = f32[2048]{0:T(1024)S(1)} fusion(f32[524288]{0:T(1024)} %bitcast.341, s32[2048]{0:T(1024)S(1)} %broadcast_clamp_fusion), kind=kCustom, calls=%fused_computation.1 | custom fusion | bytes 24576 | tf_op jit(solution)/shard_map/gather | solution.py:181
  568.5 29.8 %while.12 = (s32[]{:T(128)}, f32[16,3,128]{2,1,0:T(4,128)S(1)}, f32[16,9,128]{2,0,1:T(8,128)S(1)}, s32[16,8]{1,0:T(8,128)S(1)}, f32[9,144,128]{2,0,1:T(8,128)S(1...) while((s32[]{:T(128)}, f32[16,3,128]{2,1,0:T(4,128)S(1)}, ...), condition=%wide.region_4.5_spmd, body=%wide.region_0.4_spmd.sunk | while | flops 5902754 | bytes 215469 | solution.py:190
  (290 shorter events, 138.8 us)
Async XLA Ops:
  0.6 1.6 copy-start
  139.9 4.2 copy-start.7
  145.7 6.2 %copy-start.6 = (f32[256,2048]{0,1:S(1)}, f32[256,2048]{0,1}, u32[]{:S(2)}) copy-start(f32[256,2048]{0,1} %fusion.100) | copy-start | bytes 6291460
  155.2 6.3 %copy-start.10 = (f32[1,256,2048]{2,0,1:T(1,128)S(1)}, f32[1,256,2048]{2,0,1:T(1,128)}, u32[]{:S(2)}) copy-start(f32[1,256,2048]{2,0,1:T(1,128)} %copy.130) | copy-start | bytes 6291460
  168.8 54.5 %all-to-all-start.1 = ((f32[2,256,2048]{2,0,1:T(2,128)}), f32[2,256,2048]{2,0,1:T(2,128)}, u32[]{:S(2)}, u32[]{:S(2)}) async-start(f32[2,256,2048]{2,0,1:T(2,128)} %pad_maximum_fusion.1), calls=%async_computation.1 | async-start | bytes 8388608 | tf_op jit(solution)/shard_map/all_to_all | solution.py:121
  240.7 8.1 %copy-start.3 = (f32[64,4,32,64]{3,2,1,0:T(8,128)S(1)}, f32[64,4,32,64]{3,2,1,0:T(8,128)}, u32[]{:S(2)}) copy-start(f32[64,4,32,64]{3,2,1,0:T(8,128)} %squeeze.88) | copy-start | bytes 6291460
  253.5 4.5 copy-start.2
  258.0 5.2 copy-start.5
  375.0 1.6 copy-start.8
  390.4 6.5 %copy-start.13 = (f32[6,1,1,2048]{3,2,1,0:T(1,128)S(1)}, f32[6,1,1,2048]{3,2,1,0:T(1,128)}, u32[]{:S(2)}) copy-start(f32[6,1,1,2048]{3,2,1,0:T(1,128)} %param.13) | copy-start | bytes 147460
  390.4 6.6 %copy-start.15 = (s32[1,1,16]{2,1,0:T(1,128)S(1)}, s32[1,1,16]{2,1,0:T(1,128)}, u32[]{:S(2)}) copy-start(s32[1,1,16]{2,1,0:T(1,128)} %param.16) | copy-start | bytes 196
  390.4 6.6 %copy-start.12 = (s32[1,1,2048]{2,1,0:T(1,128)S(1)}, s32[1,1,2048]{2,1,0:T(1,128)}, u32[]{:S(2)}) copy-start(s32[1,1,2048]{2,1,0:T(1,128)} %param.15) | copy-start | bytes 24580
  390.4 6.8 %copy-start.11 = (f32[3,1,1,2048]{3,2,1,0:T(1,128)S(1)}, f32[3,1,1,2048]{3,2,1,0:T(1,128)}, u32[]{:S(2)}) copy-start(f32[3,1,1,2048]{3,2,1,0:T(1,128)} %param.14) | copy-start | bytes 73732
  390.4 8.4 %copy-start.14 = (s32[1,1,16,8]{2,3,1,0:T(8,128)S(1)}, s32[1,1,16,8]{2,3,1,0:T(8,128)}, u32[]{:S(2)}) copy-start(s32[1,1,16,8]{2,3,1,0:T(8,128)} %param.17) | copy-start | bytes 1540
  390.5 117.0 %all-to-all-start.3 = ((f32[2,256,2048]{2,0,1:T(2,128)}), f32[2,256,2048]{2,0,1:T(2,128)}, u32[]{:S(2)}, u32[]{:S(2)}) async-start(f32[2,256,2048]{2,0,1:T(2,128)} %copy.151), calls=%async_computation.3 | async-start | bytes 8388608 | tf_op jit(solution)/shard_map/all_to_all | solution.py:152
  397.3 93.0 %collective-permute-start = (f32[9,1,1,2048]{3,0,2,1:T(8,128)S(1)}, f32[9,1,1,2048]{3,0,2,1:T(8,128)S(1)}, u32[]{:S(2)}, u32[]{:S(2)}) collective-permute-start(f32[9,1,1,2048]{3,0,2,1:T(8,128)S(1)} %maximum_bitcast_fusion), channel_id=1, source_target_pairs={{0,4},{4,8},{8,12},{12,16},{16,20},{20,24},{24,28},{28,0},{1,5},{5... | collective-permute-start | bytes 221192 | tf_op jit(solution)/shard_map/ppermute | solution.py:19
  398.6 92.0 %collective-permute-start.1 = (f32[9,1,1,2048]{3,0,2,1:T(8,128)S(1)}, f32[9,1,1,2048]{3,0,2,1:T(8,128)S(1)}, u32[]{:S(2)}, u32[]{:S(2)}) collective-permute-start(f32[9,1,1,2048]{3,0,2,1:T(8,128)S(1)} %maximum_bitcast_fusion), channel_id=1, source_target_pairs={{4,0},{8,4},{12,8},{16,12},{20,16},{24,20},{28,24},{0,28},{5,1},{9... | collective-permute-start | bytes 221192 | tf_op jit(solution)/shard_map/ppermute | solution.py:22
  490.5 10.0 %collective-permute-start.2 = (f32[9,3,1,2048]{3,0,2,1:T(8,128)S(1)}, f32[9,3,1,2048]{3,0,2,1:T(8,128)S(1)}, u32[]{:S(2)}, u32[]{:S(2)}) collective-permute-start(f32[9,3,1,2048]{3,0,2,1:T(8,128)S(1)} %pad_maximum_fusion.5), channel_id=1, source_target_pairs={{0,1},{1,2},{2,3},{3,0},{4,5},{5,6},{6,7},{7,4},{8,9},{9,10},{10,1... | collective-permute-start | bytes 663560 | tf_op jit(solution)/shard_map/ppermute | solution.py:19
  493.2 10.3 %collective-permute-start.3 = (f32[9,3,1,2048]{3,0,2,1:T(8,128)S(1)}, f32[9,3,1,2048]{3,0,2,1:T(8,128)S(1)}, u32[]{:S(2)}, u32[]{:S(2)}) collective-permute-start(f32[9,3,1,2048]{3,0,2,1:T(8,128)S(1)} %pad_maximum_fusion.5), channel_id=1, source_target_pairs={{1,0},{2,1},{3,2},{0,3},{5,4},{6,5},{7,6},{4,7},{9,8},{10,9},{11,1... | collective-permute-start | bytes 663560 | tf_op jit(solution)/shard_map/ppermute | solution.py:22
  524.7 9.0 %copy-start.4 = (f32[32,8,64,32]{3,2,0,1:T(8,128)S(1)}, f32[32,8,64,32]{3,2,0,1:T(8,128)}, u32[]{:S(2)}) copy-start(f32[32,8,64,32]{3,2,0,1:T(8,128)} %reshape.1055) | copy-start | bytes 6291460
  541.6 2.4 copy-start.9
  544.0 55.0 %copy-start.1 = (f32[32,64,256]{2,1,0:T(8,128)S(1)}, f32[32,64,256]{2,1,0:T(8,128)}, u32[]{:S(2)}) copy-start(f32[32,64,256]{2,1,0:T(8,128)} %param.12) | copy-start | bytes 6291460
where the time goes:
time: 610 us; the launch traced here: 599 us
  local copies, waits for them, and re-layouts  150 us (25%)
  blocking collectives  148 us (24%)
  waiting for transfers between devices  146 us (24%)
  matrix products  94.6 us (16%)
  other arithmetic  40.6 us (7%)
  starting transfers between devices  17.8 us (3%)
    ppermute x2, waiting for transfers between devices, extended(): lax.ppermute(lax.slice_in_dim(block, block.shape[dim] - width, None, axis...  98.6 us
    all_to_all x1, blocking collectives, per_device(): lax.all_to_all(zeta, 'gx', split_axis=1, concat_axis=2, tiled=True)  95.6 us
    dot_general x16, matrix products, product(): return jnp.einsum(form, left, table, precision=lax.Precision.HIGHEST)  79.2 us
    all_to_all x1, blocking collectives, per_device(): lax.all_to_all(back_y, 'gy', split_axis=1, concat_axis=2, tiled=True)  52 us
    all_to_all x1, waiting for transfers between devices, per_device(): lax.all_to_all(along_x, 'gy', split_axis=1, concat_axis=2, tiled=True)  44.3 us
    gather x1, local copies, waits for them, and re-layouts, per_device(): sampled = stress.reshape(-1)[cells]  24.5 us
    reduce_sum x16, other arithmetic, block_force(): jnp.sum(weight * deltas[k], axis=1)  17.3 us
    unnamed x4, matrix products  15.4 us
  transfers between devices with their start and end apart: 6, of which 5 were waited for; matrix products, arithmetic and copies ran while one was open for 1% of the time, Pallas kernels for 0%

commit v1 on v0

v1 whole, which is shorter than its diff:
```python
import math

import jax
import jax.numpy as jnp
import numpy as np
from jax import lax
from jax.experimental import pallas as pl
from jax.experimental.pallas import tpu as pltpu
from jax.sharding import PartitionSpec as P

nu_copper = 0.34
core_sq = 4.0
pair_scale = 4.0
CHUNKS = 2
VMEM_LIMIT = 48 * 1024 * 1024


def hartley_table(length):
    phase = np.outer(np.arange(length), np.arange(length)) % length
    angle = phase * (2.0 * math.pi / length)
    return ((np.cos(angle) + np.sin(angle)) / math.sqrt(length)).astype(np.float32)


def line_tables(length, plane_x):
    freq = np.arange(length, dtype=np.float64)
    wave = (2.0 * np.sin(math.pi * freq / length)) ** 2
    wave_z = wave[:, None]
    wave_y = wave[None, :]
    total = wave_y + wave_z
    zero = total == 0.0
    safe = np.where(zero, 1.0, total)
    ratio = 1.0 / (1.0 + safe / 2.0 + np.sqrt(safe + safe * safe / 4.0))
    ratio = ratio.astype(np.float32).astype(np.float64)
    elastic = 2.0 / (1.0 - nu_copper)
    gap = 1.0 - ratio * ratio
    green = ratio / gap
    first = -2.0 * (wave_y + elastic * wave_z) * green
    second = 2.0 * elastic * wave_z * safe * green * green
    weight_two = second
    weight_one = first + second * 2.0 * ratio * ratio / gap
    weight_zero = -first - second * (1.0 + ratio * ratio) / gap
    lap = ratio**length
    wrap_one = 1.0 / (1.0 - lap)
    wrap_two = length * lap / (1.0 - lap) ** 2
    leap = ratio**plane_x
    mask = np.where(zero, 0.0, 1.0)
    ratio = np.where(zero, 1.0, ratio)
    leap = np.where(zero, 1.0, leap)
    weight_zero = np.where(zero, 0.0, weight_zero)
    weight_one = np.where(zero, -1.0 / length, weight_one)
    weight_two = np.where(zero, 0.0, weight_two)
    wrap_one = np.where(zero, 1.0, wrap_one)
    wrap_two = np.where(zero, 0.0, wrap_two)
    tables = [ratio, leap, mask, weight_zero, weight_one, weight_two, wrap_one, wrap_two]
    return np.stack([t.astype(np.float32) for t in tables])


def halves(value):
    high = value.astype(jnp.bfloat16)
    low = (value - high.astype(jnp.float32)).astype(jnp.bfloat16)
    return high, low


def three_dots(left, right, dims):
    def one(a, b):
        return lax.dot_general(a, b, (dims, ((), ())), preferred_element_type=jnp.float32)

    return one(left[0], right[0]) + one(left[0], right[1]) + one(left[1], right[0])


def whole(memory=pltpu.VMEM):
    return pl.BlockSpec(memory_space=memory)


def params():
    return pltpu.CompilerParams(vmem_limit_bytes=VMEM_LIMIT)


def z_forward(field, table, me, groups, chunk, rows):
    cells, length = field.shape
    per = length // groups
    tile = min(512, cells)

    def kernel(me_ref, field_ref, table_ref, *outs):
        own = me_ref[0]
        picked = [
            table_ref[pl.ds(pl.multiple_of((own ^ d) * per + chunk * rows, 8), rows), :]
            for d in range(groups)
        ]
        left = halves(jnp.concatenate(picked, axis=0))
        right = halves(field_ref[...])
        result = three_dots(left, right, ((1,), (1,)))
        for d in range(groups):
            outs[d][...] = result[d * rows : (d + 1) * rows]

    return pl.pallas_call(
        kernel,
        grid=(cells // tile,),
        in_specs=[
            pl.BlockSpec(memory_space=pltpu.SMEM),
            pl.BlockSpec((tile, length), lambda i: (i, 0)),
            pl.BlockSpec((length, length), lambda i: (0, 0)),
        ],
        out_specs=[pl.BlockSpec((rows, tile), lambda i: (0, i))] * groups,
        out_shape=[jax.ShapeDtypeStruct((rows, cells), jnp.float32)] * groups,
        compiler_params=params(),
        cost_estimate=pl.CostEstimate(
            flops=6 * cells * length * rows * groups, bytes_accessed=8 * cells * length, transcendentals=0
        ),
        name="z_forward",
    )(me, field, table)


def y_rows(table_ref, own, groups, plane_y):
    picked = [
        table_ref[pl.ds(pl.multiple_of((own ^ d) * plane_y, 8), plane_y), :] for d in range(groups)
    ]
    return halves(jnp.concatenate(picked, axis=0))


def y_forward(parts, table, lines, me, chunk, rows, plane_x, plane_y):
    groups = len(parts)
    length = table.shape[0]
    per = length // groups

    def kernel(me_ref, *refs):
        part_refs = refs[:groups]
        table_ref, lines_ref, spec_ref, ends_ref, gathered = refs[groups:]
        own = me_ref[0]
        right = y_rows(table_ref, own, groups, plane_y)
        for x in range(plane_x):
            gathered[x * rows : (x + 1) * rows, :] = jnp.concatenate(
                [ref[:, x * plane_y : (x + 1) * plane_y] for ref in part_refs], axis=1
            )
        result = three_dots(halves(gathered[...]), right, ((1,), (0,)))
        gathered[...] = result
        first = pl.multiple_of(own * per + chunk * rows, 8)
        ratio = lines_ref[0, pl.ds(first, rows), :]
        mask = lines_ref[2, pl.ds(first, rows), :]
        for g in range(0, rows, 8):
            step = ratio[g : g + 8]
            keep = mask[g : g + 8]
            zero = jnp.zeros_like(step)
            one, two = zero, zero
            for x in range(plane_x):
                value = gathered[x * rows + g : x * rows + g + 8, :]
                one = value + step * one
                two = one + step * two
                spec_ref[x, g : g + 8, :] = value * keep
            ends_ref[0, g : g + 8, :] = one
            ends_ref[1, g : g + 8, :] = two
            one, two = zero, zero
            for x in reversed(range(plane_x)):
                value = gathered[x * rows + g : x * rows + g + 8, :]
                one = value + step * one
                two = one + step * two
            ends_ref[2, g : g + 8, :] = one
            ends_ref[3, g : g + 8, :] = two

    return pl.pallas_call(
        kernel,
        in_specs=[whole(pltpu.SMEM)] + [whole()] * (groups + 2),
        out_specs=[whole(), whole()],
        out_shape=[
            jax.ShapeDtypeStruct((plane_x, rows, length), jnp.float32),
            jax.ShapeDtypeStruct((4, rows, length), jnp.float32),
        ],
        scratch_shapes=[pltpu.VMEM((plane_x * rows, length), jnp.float32)],
        compiler_params=params(),
        cost_estimate=pl.CostEstimate(
            flops=6 * plane_x * rows * length * length,
            bytes_accessed=8 * plane_x * rows * length,
            transcendentals=0,
        ),
        name="y_forward",
    )(me, *parts, table, lines)


def y_backward(spec, ends, table, lines, me, chunk, groups, plane_y):
    plane_x, rows, length = spec.shape
    per = length // groups
    blocks = len(ends)

    def kernel(me_ref, spec_ref, *refs):
        ends_refs = refs[:blocks]
        table_ref, lines_ref = refs[blocks : blocks + 2]
        outs = refs[blocks + 2 : blocks + 2 + groups]
        work = refs[blocks + 2 + groups]
        own = me_ref[0]
        right = y_rows(table_ref, own, groups, plane_y)
        first = pl.multiple_of(own * per + chunk * rows, 8)
        for g in range(0, rows, 8):
            at = pl.ds(pl.multiple_of(first + g, 8), 8)
            step, leap = lines_ref[0, at, :], lines_ref[1, at, :]
            wrap_one, wrap_two = lines_ref[6, at, :], lines_ref[7, at, :]
            carries = []
            for side in (0, 1):
                one = jnp.zeros_like(step)
                two = jnp.zeros_like(step)
                for distance in reversed(range(1, blocks + 1)):
                    source = distance % blocks if side == 0 else (blocks - distance) % blocks
                    ref = ends_refs[source]
                    two = ref[2 * side + 1, g : g + 8, :] + leap * (two + float(plane_x) * one)
                    one = ref[2 * side, g : g + 8, :] + leap * one
                carries.append((one * wrap_one, two * wrap_one + wrap_two * one))
            weight_zero, weight_one, weight_two = lines_ref[3, at, :], lines_ref[4, at, :], lines_ref[5, at, :]
            one, two = carries[0]
            for x in range(plane_x):
                value = spec_ref[x, g : g + 8, :]
                one = value + step * one
                two = one + step * two
                work[x * rows + g : x * rows + g + 8, :] = (
                    weight_zero * value + weight_one * one + weight_two * two
                )
            one, two = carries[1]
            for x in reversed(range(plane_x)):
                value = spec_ref[x, g : g + 8, :]
                one = value + step * one
                two = one + step * two
                work[x * rows + g : x * rows + g + 8, :] += weight_one * one + weight_two * two
        work[...] = three_dots(halves(work[...]), right, ((1,), (1,)))
        pack = max(1, 128 // plane_y)
        for x in range(0, plane_x, pack):
            for d in range(groups):
                outs[d][:, x * plane_y : (x + pack) * plane_y] = jnp.concatenate(
                    [
                        work[(x + k) * rows : (x + k + 1) * rows, d * plane_y : (d + 1) * plane_y]
                        for k in range(pack)
                    ],
                    axis=1,
                )

    return pl.pallas_call(
        kernel,
        in_specs=[whole(pltpu.SMEM)] + [whole()] * (blocks + 3),
        out_specs=[whole()] * groups,
        out_shape=[jax.ShapeDtypeStruct((rows, plane_x * plane_y), jnp.float32)] * groups,
        scratch_shapes=[pltpu.VMEM((plane_x * rows, length), jnp.float32)],
        compiler_params=params(),
        cost_estimate=pl.CostEstimate(
            flops=6 * plane_x * rows * length * length,
            bytes_accessed=8 * plane_x * rows * length,
            transcendentals=0,
        ),
        name="y_backward",
    )(me, spec, *ends, table, lines)


def z_backward(parts, table, cells, pull, vectors, me, groups, chunks, rows):
    cell_total = parts[0].shape[1]
    length = table.shape[0]
    per = length // groups
    seg_total = cells.shape[1]
    blocks, width = pull.shape[1:]
    tile = min(512, cell_total)
    steps = cell_total // tile

    def kernel(me_ref, *refs):
        part_refs = refs[: chunks * groups]
        table_ref, cells_ref, pull_ref, vectors_ref, stress_ref, force_ref, samples = refs[chunks * groups :]
        own = me_ref[0]
        i = pl.program_id(0)
        picked = [
            table_ref[pl.ds(pl.multiple_of((own ^ d) * per + c * rows, 8), rows), :]
            for c in range(chunks)
            for d in range(groups)
        ]
        picked = jnp.concatenate(picked, axis=0)
        right = halves(picked)
        stack = jnp.concatenate([ref[...] for ref in part_refs], axis=0)
        left = halves(stack)
        stress_ref[...] = three_dots(left, right, ((0,), (0,)))
        place = cells_ref[...] // length - i * tile
        hot = (lax.broadcasted_iota(jnp.int32, (tile, seg_total), 0) == place).astype(jnp.bfloat16)
        found = jnp.dot(left[0], hot, preferred_element_type=jnp.float32) + jnp.dot(
            left[1], hot, preferred_element_type=jnp.float32
        )

        @pl.when(i == 0)
        def _():
            samples[...] = found

        @pl.when(i > 0)
        def _():
            samples[...] += found

        @pl.when(i == steps - 1)
        def _():
            depth = cells_ref[...] % length
            hot_z = (lax.broadcasted_iota(jnp.int32, (length, seg_total), 0) == depth).astype(jnp.bfloat16)
            factor = jnp.dot(right[0], hot_z, preferred_element_type=jnp.float32) + jnp.dot(
                right[1], hot_z, preferred_element_type=jnp.float32
            )
            tau = jnp.sum(samples[...] * factor, axis=0, keepdims=True)
            tau = jnp.concatenate([tau[:, b * width : (b + 1) * width] for b in range(blocks)], axis=0)
            b0, b1, b2, t0, t1, t2 = (vectors_ref[k] for k in range(6))
            force_ref[0] = pull_ref[0] + tau * (b1 * t2 - b2 * t1)
            force_ref[1] = pull_ref[1] + tau * (b2 * t0 - b0 * t2)
            force_ref[2] = pull_ref[2] + tau * (b0 * t1 - b1 * t0)

    return pl.pallas_call(
        kernel,
        grid=(steps,),
        in_specs=[whole(pltpu.SMEM)]
        + [pl.BlockSpec((rows, tile), lambda i: (0, i))] * (chunks * groups)
        + [
            pl.BlockSpec((length, length), lambda i: (0, 0)),
            pl.BlockSpec((1, seg_total), lambda i: (0, 0)),
            pl.BlockSpec((3, blocks, width), lambda i: (0, 0, 0)),
            pl.BlockSpec((6, blocks, width), lambda i: (0, 0, 0)),
        ],
        out_specs=[
            pl.BlockSpec((tile, length), lambda i: (i, 0)),
            pl.BlockSpec((3, blocks, width), lambda i: (0, 0, 0)),
        ],
        out_shape=[
            jax.ShapeDtypeStruct((cell_total, length), jnp.float32),
            jax.ShapeDtypeStruct((3, blocks, width), jnp.float32),
        ],
        scratch_shapes=[pltpu.VMEM((length, seg_total), jnp.float32)],
        compiler_params=params(),
        cost_estimate=pl.CostEstimate(
            flops=10 * cell_total * length * length, bytes_accessed=8 * cell_total * length, transcendentals=0
        ),
        name="z_backward",
    )(me, *parts, table, cells, pull, vectors)


def pair_pull(pool, pairs, lively, shifts, first, count):
    devices = len(pool)
    rows, blocks, width = pool[0].shape
    partners = pairs.shape[1]

    def kernel(pairs_ref, lively_ref, *refs):
        pool_refs = refs[:devices]
        out_ref, far, near, total = refs[devices:]
        for d in range(devices):
            for k in range(rows):
                value = pool_refs[d][k]
                if k < 2 and shifts[d][k] != 0.0:
                    value = value + shifts[d][k]
                far[(d * rows + k) * blocks : (d * rows + k + 1) * blocks, :] = value
        home = devices // 2 * rows * blocks

        def one_block(index, carry):
            b = first + index
            own = [far[pl.ds(home + k * blocks + b, 1), :] for k in range(rows)]
            own = jnp.concatenate(own + [jnp.zeros((16 - rows, width), jnp.float32)], axis=0)
            own = own.T
            for k in range(rows):
                near[k] = jnp.broadcast_to(own[:, k : k + 1], (width, width))
            total[...] = jnp.zeros_like(total)

            def one_partner(p, carry):
                number = pairs_ref[b, p]

                @pl.when(lively_ref[number] > 0)
                def _():
                    base = (number // blocks) * (rows * blocks) + number % blocks
                    other = [
                        jnp.broadcast_to(far[pl.ds(base + k * blocks, 1), :], (8, width)) for k in range(rows)
                    ]
                    for t in range(0, width, 8):
                        mine = [near[k, t : t + 8, :] for k in range(rows)]
                        dx, dy, dz = (mine[k] - other[k] for k in range(3))
                        inverse = lax.rsqrt(dx * dx + dy * dy + dz * dz + core_sq)
                        squared = inverse * inverse
                        burg_dot = mine[3] * other[3] + mine[4] * other[4] + mine[5] * other[5]
                        line_dot = mine[6] * other[6] + mine[7] * other[7] + mine[8] * other[8]
                        burg_own = mine[3] * dx + mine[4] * dy + mine[5] * dz
                        burg_far = other[3] * dx + other[4] * dy + other[5] * dz
                        weight = (line_dot * (squared * inverse)) * (
                            burg_dot - (3.0 * squared) * (burg_own * burg_far)
                        )
                        total[0, t : t + 8, :] += weight * dx
                        total[1, t : t + 8, :] += weight * dy
                        total[2, t : t + 8, :] += weight * dz

                return carry

            lax.fori_loop(0, partners, one_partner, 0)
            for k in range(3):
                summed = jnp.sum(total[k].T, axis=0, keepdims=True)
                out_ref[k, pl.ds(index, 1), :] = pair_scale * summed
            return carry

        lax.fori_loop(0, count, one_block, 0)

    return pl.pallas_call(
        kernel,
        in_specs=[whole(pltpu.SMEM)] * 2 + [whole()] * devices,
        out_specs=whole(),
        out_shape=jax.ShapeDtypeStruct((3, count, width), jnp.float32),
        scratch_shapes=[
            pltpu.VMEM((devices * rows * blocks, width), jnp.float32),
            pltpu.VMEM((rows, width, width), jnp.float32),
            pltpu.VMEM((3, width, width), jnp.float32),
        ],
        compiler_params=params(),
        cost_estimate=pl.CostEstimate(
            flops=50 * count * partners * width * width,
            bytes_accessed=4 * devices * rows * blocks * width,
            transcendentals=count * partners * width * width,
        ),
        name="pair_pull",
    )(pairs, lively, *pool)


def per_device(eigen, seg_vec, seg_off, seg_cell, blk_count, pair_list):
    plane_x, plane_y, length = eigen.shape
    groups_x = lax.axis_size("gx")
    groups_y = lax.axis_size("gy")
    per = length // groups_y
    chunks = CHUNKS if per // CHUNKS >= 8 else 1
    rows = per // chunks
    me = lax.axis_index("gy").astype(jnp.int32).reshape(1)
    table = jnp.asarray(hartley_table(length))
    lines = jnp.asarray(line_tables(length, plane_x))

    seg_total = seg_cell.shape[2]
    block_total = blk_count.shape[2]
    width = seg_total // block_total
    cells = seg_cell.reshape(block_total, width)
    vectors = seg_vec.reshape(6, block_total, width)
    position = jnp.stack(
        [cells // (length * plane_y), cells // length % plane_y, cells % length]
    ).astype(jnp.float32) + seg_off.reshape(3, block_total, width)
    counts = blk_count.reshape(block_total)
    live = (jnp.arange(width, dtype=jnp.int32)[None, :] < counts[:, None]).astype(jnp.float32)
    live_vectors = jnp.concatenate([vectors[0:3] * live[None], vectors[3:6]], axis=0)
    source = jnp.concatenate([position, live_vectors], axis=0)

    field = eigen.reshape(plane_x * plane_y, length)
    sent = [z_forward(field, table, me, groups_y, c, rows) for c in range(chunks)]

    def swap(parts):
        return [parts[0]] + [
            lax.ppermute(parts[d], "gy", [(i, i ^ d) for i in range(groups_y)])
            for d in range(1, groups_y)
        ]

    arrived = [swap(parts) for parts in sent]

    pool, shifts = [], []
    for p in (-1, 0, 1):
        for q in (-1, 0, 1):
            shifts.append((float(p * plane_x), float(q * plane_y)))
            if p == 0 and q == 0:
                pool.append(source)
                continue
            route = [
                (((i + p) % groups_x) * groups_y + (j + q) % groups_y, i * groups_y + j)
                for i in range(groups_x)
                for j in range(groups_y)
            ]
            pool.append(lax.ppermute(source, ("gx", "gy"), route))
    lively = jnp.concatenate([jnp.any(part[3:6] != 0.0, axis=(0, 2)) for part in pool]).astype(jnp.int32)
    pairs = pair_list.reshape(block_total, pair_list.shape[3])
    pull = pair_pull(pool, pairs, lively, shifts, 0, block_total)

    returned = []
    for c in range(chunks):
        spec, ends = y_forward(arrived[c], table, lines, me, c, rows, plane_x, plane_y)
        all_ends = [ends] + [
            lax.ppermute(ends, "gx", [(i, (i + e) % groups_x) for i in range(groups_x)])
            for e in range(1, groups_x)
        ]
        returned.append(y_backward(spec, all_ends, table, lines, me, c, groups_y, plane_y))
    landed = [swap(parts) for parts in returned]
    flat = [part for parts in landed for part in parts]
    stress, force = z_backward(
        flat, table, seg_cell.reshape(1, seg_total), pull, live_vectors, me, groups_y, chunks, rows
    )
    return stress.reshape(eigen.shape), force.reshape(3, 1, 1, seg_total)


def solution(mesh):
    return jax.shard_map(
        per_device,
        mesh=mesh,
        in_specs=(
            P("gx", "gy", None),
            P(None, "gx", "gy", None),
            P(None, "gx", "gy", None),
            P("gx", "gy", None),
            P("gx", "gy", None),
            P("gx", "gy", None, None),
        ),
        out_specs=(P("gx", "gy", None), P(None, "gx", "gy", None)),
        check_vma=False,
    )
```

time: 610 us -> 124 us (0.20)
  the two profiles are of different devices: /device:TPU:11 before, /device:TPU:1 now
where the time goes in v1:
time: 124 us; the launch traced here: 123 us
  starting transfers between devices  49.3 us (40%)
  Pallas kernels  37.3 us (30%)
  waiting for transfers between devices  19.1 us (15%)
  local copies, waits for them, and re-layouts  9.66 us (8%)
  other arithmetic  6.33 us (5%)
    ppermute x14, starting transfers between devices, per_device(): lax.ppermute(ends, 'gx', [(i, (i + e) % groups_x) for i in range(groups_x)])  25.9 us
    pallas_call x1, Pallas kernels, pair_pull(): pl.pallas_call(kernel, in_specs=[whole(pltpu.SMEM)] * 2 + [whole()] * dev...  16.4 us
    ppermute x12, starting transfers between devices, swap(): lax.ppermute(parts[d], 'gy', [(i, i ^ d) for i in range(groups_y)])  12.2 us
    ppermute x14, waiting for transfers between devices, per_device(): lax.ppermute(ends, 'gx', [(i, (i + e) % groups_x) for i in range(groups_x)])  11.7 us
    ppermute x8, starting transfers between devices, per_device(): pool.append(lax.ppermute(source, ('gx', 'gy'), route))  11.3 us
    pallas_call x1, Pallas kernels, z_backward(): pl.pallas_call(kernel, grid=(steps,), in_specs=[whole(pltpu.SMEM)] + [pl....  9.88 us
    unnamed x44, local copies, waits for them, and re-layouts  7.96 us
    ppermute x12, waiting for transfers between devices, swap(): lax.ppermute(parts[d], 'gy', [(i, i ^ d) for i in range(groups_y)])  5.77 us
  transfers between devices with their start and end apart: 34, of which 8 were waited for; matrix products, arithmetic and copies ran while one was open for 4% of the time, Pallas kernels for 22%

profile of v1, /device:TPU:1, one launch (start us, length us, event | category | flops | bytes accessed | tf_op | source)
XLA Modules:
  0.0 122.6 jit_solution(10672943983739060774)
XLA Ops:
  3.7 5.7 %collective-permute-start.33 = (f32[9,16,128]{2,1,0:T(8,128)S(1)}, f32[9,16,128]{2,1,0:T(8,128)S(1)}, u32[]{:S(2)}, u32[]{:S(2)}) collective-permute-start(f32[9,16,128]{2,1,0:T(8,128)S(1)} %pad_maximum_fusion.refs_4_), channel_id=1, source_target_pairs={{5,0},{6,1},{7,2},{4,3},{9,4},{10,5},{11,6},{8,7},{13,8},{14,9},{1... | collective-permute-start | bytes 221192 | tf_op jit(solution)/shard_map/ppermute | solution.py:456
  10.6 1.6 %copy-done.3 = f32[32,64,256]{2,1,0:T(8,128)S(1)} copy-done((f32[32,64,256]{2,1,0:T(8,128)S(1)}, f32[32,64,256]{2,1,0:T(8,128)}, u32[]{:S(2)}) %copy-start.3) | copy-done | bytes 2097176
  12.2 1.7 %z_forward.3 = (f32[32,2048]{1,0:T(8,128)S(1)}, f32[32,2048]{1,0:T(8,128)S(1)}, f32[32,2048]{1,0:T(8,128)S(1)}, f32[32,2048]{1,0:T(8,128)S(1)}) custom-call(s32[1]{0:T(128)} %bitcast.me_ref, f32[2048,256]{1,0:T(8,128)S(1)} %bitcast.18, f32[256,256]{1,0:T(8,128)S(1)} %copy-done.1), custom_call_target="tpu_custom_call" | custom-call | flops 402653184 | bytes 4194304 | tf_op jit(solution)/shard_map/z_forward/pallas_call | solution.py:96
  13.9 1.1 collective-permute-start.13
  15.4 1.3 %collective-permute-start.15 = (f32[32,2048]{1,0:T(8,128)S(1)}, f32[32,2048]{1,0:T(8,128)S(1)}, u32[]{:S(2)}, u32[]{:S(2)}) collective-permute-start(f32[32,2048]{1,0:T(8,128)S(1)} %get-tuple-element.37), channel_id=1, source_target_pairs={{0,3},{1,2},{2,1},{3,0},{4,7},{5,6},{6,5},{7,4},{8,11},{9,10},{10,... | collective-permute-start | bytes 786440 | tf_op jit(solution)/shard_map/ppermute | solution.py:438
  16.9 2.6 %z_forward.2 = (f32[32,2048]{1,0:T(8,128)S(1)}, f32[32,2048]{1,0:T(8,128)}, f32[32,2048]{1,0:T(8,128)}, f32[32,2048]{1,0:T(8,128)}) custom-call(s32[1]{0:T(128)} %bitcast.me_ref, f32[2048,256]{1,0:T(8,128)S(1)} %bitcast.19, f32[256,256]{1,0:T(8,128)S(1)} %copy-done.1), custom_call_target="tpu_custom_call" | custom-call | flops 402653184 | bytes 4194304 | tf_op jit(solution)/shard_map/z_forward/pallas_call | solution.py:96
  19.5 1.1 collective-permute-start.31
  22.4 1.5 %collective-permute-done.31.refs_6_ = f32[9,16,128]{2,1,0:T(8,128)S(1)} collective-permute-done((f32[9,16,128]{2,1,0:T(8,128)S(1)}, f32[9,16,128]{2,1,0:T(8,128)S(1)}, u32[]{:S(2)}, u32[]{:S(2)}) %collective-permute-start.31) | collective-permute-done | bytes 73760 | tf_op jit(solution)/shard_map/ppermute | solution.py:456
  23.9 1.3 %collective-permute-start.30 = (f32[9,16,128]{2,1,0:T(8,128)S(1)}, f32[9,16,128]{2,1,0:T(8,128)}, u32[]{:S(2)}, u32[]{:S(2)}) collective-permute-start(f32[9,16,128]{2,1,0:T(8,128)S(1)} %pad_maximum_fusion.refs_4_), channel_id=1, source_target_pairs={{1,0},{2,1},{3,2},{0,3},{5,4},{6,5},{7,6},{4,7},{9,8},{10,9},{11,1... | collective-permute-start | bytes 221192 | tf_op jit(solution)/shard_map/ppermute | solution.py:456
  27.4 2.9 %collective-permute-done.15.refs_3_ = f32[32,2048]{1,0:T(8,128)S(1)} collective-permute-done((f32[32,2048]{1,0:T(8,128)S(1)}, f32[32,2048]{1,0:T(8,128)S(1)}, u32[]{:S(2)}, u32[]{:S(2)}) %collective-permute-start.15) | collective-permute-done | bytes 262176 | tf_op jit(solution)/shard_map/ppermute | solution.py:438
  34.6 1.6 %collective-permute-start.22 = (f32[4,32,256]{2,1,0:T(8,128)S(1)}, f32[4,32,256]{2,1,0:T(8,128)S(1)}, u32[]{:S(2)}, u32[]{:S(2)}) collective-permute-start(f32[4,32,256]{2,1,0:T(8,128)S(1)} %get-tuple-element.39.refs_0_), channel_id=1, source_target_pairs={{0,28},{4,0},{8,4},{12,8},{16,12},{20,16},{24,20},{28,24},{1,29},{... | collective-permute-start | bytes 393224 | tf_op jit(solution)/shard_map/ppermute | solution.py:465
  37.2 2.4 %collective-permute-start.19 = (f32[4,32,256]{2,1,0:T(8,128)S(1)}, f32[4,32,256]{2,1,0:T(8,128)S(1)}, u32[]{:S(2)}, u32[]{:S(2)}) collective-permute-start(f32[4,32,256]{2,1,0:T(8,128)S(1)} %get-tuple-element.39.refs_0_), channel_id=1, source_target_pairs={{0,16},{4,20},{8,24},{12,28},{16,0},{20,4},{24,8},{28,12},{1,17},{... | collective-permute-start | bytes 393224 | tf_op jit(solution)/shard_map/ppermute | solution.py:465
  39.6 2.8 %collective-permute-done.2.refs_3_ = f32[32,2048]{1,0:T(8,128)} collective-permute-done((f32[32,2048]{1,0:T(8,128)}, f32[32,2048]{1,0:T(8,128)}, u32[]{:S(2)}, u32[]{:S(2)}) %collective-permute-start.2) | collective-permute-done | bytes 262176 | tf_op jit(solution)/shard_map/ppermute | solution.py:438
  42.4 1.8 %y_forward.2 = (f32[32,32,256]{2,1,0:T(8,128)S(1)}, f32[4,32,256]{2,1,0:T(8,128)S(1)}) custom-call(s32[1]{0:T(128)} %bitcast.me_ref, f32[32,2048]{1,0:T(8,128)S(1)} %get-tuple-element.24.refs_0_, f32[32,2048]{1,0:T(8,128)S(1)} %collective-permute-done.refs_1_, f32[32,2048]{1,0:T(8,128)} %collective-permute-done.1.refs_2_, ...), custom_call_target="tpu_custom_call" | custom-call | flops 402653184 | bytes 2097152 | tf_op jit(solution)/shard_map/y_forward/pallas_call | solution.py:160
  44.8 1.1 collective-permute-start.16
  45.9 9.7 %collective-permute-start.9 = (f32[4,32,256]{2,1,0:T(8,128)S(1)}, f32[4,32,256]{2,1,0:T(8,128)S(1)}, u32[]{:S(2)}, u32[]{:S(2)}) collective-permute-start(f32[4,32,256]{2,1,0:T(8,128)S(1)} %get-tuple-element.29.refs_0_), channel_id=1, source_target_pairs={{0,28},{4,0},{8,4},{12,8},{16,12},{20,16},{24,20},{28,24},{1,29},{... | collective-permute-start | bytes 393224 | tf_op jit(solution)/shard_map/ppermute | solution.py:465
  55.8 1.3 %collective-permute-done.19.refs_4_ = f32[4,32,256]{2,1,0:T(8,128)S(1)} collective-permute-done((f32[4,32,256]{2,1,0:T(8,128)S(1)}, f32[4,32,256]{2,1,0:T(8,128)S(1)}, u32[]{:S(2)}, u32[]{:S(2)}) %collective-permute-start.19) | collective-permute-done | bytes 131104 | tf_op jit(solution)/shard_map/ppermute | solution.py:465
  57.5 2.0 %collective-permute-done.18.refs_3_ = f32[4,32,256]{2,1,0:T(8,128)S(1)} collective-permute-done((f32[4,32,256]{2,1,0:T(8,128)S(1)}, f32[4,32,256]{2,1,0:T(8,128)S(1)}, u32[]{:S(2)}, u32[]{:S(2)}) %collective-permute-start.18) | collective-permute-done | bytes 131104 | tf_op jit(solution)/shard_map/ppermute | solution.py:465
  59.5 5.1 %collective-permute-start.7 = (f32[4,32,256]{2,1,0:T(8,128)S(1)}, f32[4,32,256]{2,1,0:T(8,128)S(1)}, u32[]{:S(2)}, u32[]{:S(2)}) collective-permute-start(f32[4,32,256]{2,1,0:T(8,128)S(1)} %get-tuple-element.29.refs_0_), channel_id=1, source_target_pairs={{0,20},{4,24},{8,28},{12,0},{16,4},{20,8},{24,12},{28,16},{1,21},{... | collective-permute-start | bytes 393224 | tf_op jit(solution)/shard_map/ppermute | solution.py:465
  64.7 3.2 %collective-permute-start.6 = (f32[4,32,256]{2,1,0:T(8,128)S(1)}, f32[4,32,256]{2,1,0:T(8,128)S(1)}, u32[]{:S(2)}, u32[]{:S(2)}) collective-permute-start(f32[4,32,256]{2,1,0:T(8,128)S(1)} %get-tuple-element.29.refs_0_), channel_id=1, source_target_pairs={{0,16},{4,20},{8,24},{12,28},{16,0},{20,4},{24,8},{28,12},{1,17},{... | collective-permute-start | bytes 393224 | tf_op jit(solution)/shard_map/ppermute | solution.py:465
  68.0 2.0 %y_backward.3 = (f32[32,2048]{1,0:T(8,128)S(1)}, f32[32,2048]{1,0:T(8,128)S(1)}, f32[32,2048]{1,0:T(8,128)}, f32[32,2048]{1,0:T(8,128)}) custom-call(s32[1]{0:T(128)} %bitcast.me_ref, f32[32,32,256]{2,1,0:T(8,128)S(1)} %get-tuple-element.38.spec_ref, f32[4,32,256]{2,1,0:T(8,128)S(1)} %get-tuple-element.39.refs_0_, ...), custom_call_target="tpu_custom_call" | custom-call | flops 402653184 | bytes 2097152 | tf_op jit(solution)/shard_map/y_backward/pallas_call | solution.py:233
  70.0 1.6 %collective-permute-start.3 = (f32[4,32,256]{2,1,0:T(8,128)S(1)}, f32[4,32,256]{2,1,0:T(8,128)S(1)}, u32[]{:S(2)}, u32[]{:S(2)}) collective-permute-start(f32[4,32,256]{2,1,0:T(8,128)S(1)} %get-tuple-element.29.refs_0_), channel_id=1, source_target_pairs={{0,4},{4,8},{8,12},{12,16},{16,20},{20,24},{24,28},{28,0},{1,5},{5... | collective-permute-start | bytes 393224 | tf_op jit(solution)/shard_map/ppermute | solution.py:465
  71.6 1.7 %collective-permute-start.23 = (f32[32,2048]{1,0:T(8,128)S(1)}, f32[32,2048]{1,0:T(8,128)S(1)}, u32[]{:S(2)}, u32[]{:S(2)}) collective-permute-start(f32[32,2048]{1,0:T(8,128)S(1)} %get-tuple-element.41), channel_id=1, source_target_pairs={{0,1},{1,0},{2,3},{3,2},{4,5},{5,4},{6,7},{7,6},{8,9},{9,8},{10,11... | collective-permute-start | bytes 786440 | tf_op jit(solution)/shard_map/ppermute | solution.py:438
  74.1 6.3 %collective-permute-done.6.refs_4_ = f32[4,32,256]{2,1,0:T(8,128)S(1)} collective-permute-done((f32[4,32,256]{2,1,0:T(8,128)S(1)}, f32[4,32,256]{2,1,0:T(8,128)S(1)}, u32[]{:S(2)}, u32[]{:S(2)}) %collective-permute-start.6) | collective-permute-done | bytes 131104 | tf_op jit(solution)/shard_map/ppermute | solution.py:465
  80.5 2.5 %collective-permute-start.28 = (f32[9,16,128]{2,1,0:T(8,128)S(1)}, f32[9,16,128]{2,1,0:T(8,128)S(1)}, u32[]{:S(2)}, u32[]{:S(2)}) collective-permute-start(f32[9,16,128]{2,1,0:T(8,128)S(1)} %pad_maximum_fusion.refs_4_), channel_id=1, source_target_pairs={{29,0},{30,1},{31,2},{28,3},{1,4},{2,5},{3,6},{0,7},{5,8},{6,9},{7... | collective-permute-start | bytes 221192 | tf_op jit(solution)/shard_map/ppermute | solution.py:456
  83.0 2.0 %collective-permute-done.5.refs_3_ = f32[4,32,256]{2,1,0:T(8,128)S(1)} collective-permute-done((f32[4,32,256]{2,1,0:T(8,128)S(1)}, f32[4,32,256]{2,1,0:T(8,128)S(1)}, u32[]{:S(2)}, u32[]{:S(2)}) %collective-permute-start.5) | collective-permute-done | bytes 131104 | tf_op jit(solution)/shard_map/ppermute | solution.py:465
  85.9 2.1 %y_backward.2 = (f32[32,2048]{1,0:T(8,128)S(1)}, f32[32,2048]{1,0:T(8,128)}, f32[32,2048]{1,0:T(8,128)}, f32[32,2048]{1,0:T(8,128)}) custom-call(s32[1]{0:T(128)} %bitcast.me_ref, f32[32,32,256]{2,1,0:T(8,128)S(1)} %get-tuple-element.28.spec_ref, f32[4,32,256]{2,1,0:T(8,128)S(1)} %get-tuple-element.29.refs_0_, ...), custom_call_target="tpu_custom_call" | custom-call | flops 402653184 | bytes 2097152 | tf_op jit(solution)/shard_map/y_backward/pallas_call | solution.py:233
  88.7 2.1 %collective-permute-start.25 = (f32[32,2048]{1,0:T(8,128)}, f32[32,2048]{1,0:T(8,128)S(1)}, u32[]{:S(2)}, u32[]{:S(2)}) collective-permute-start(f32[32,2048]{1,0:T(8,128)} %get-tuple-element.43), channel_id=1, source_target_pairs={{0,3},{1,2},{2,1},{3,0},{4,7},{5,6},{6,5},{7,4},{8,11},{9,10},{10,... | collective-permute-start | bytes 786440 | tf_op jit(solution)/shard_map/ppermute | solution.py:438
  90.9 2.2 %collective-permute-start.10 = (f32[32,2048]{1,0:T(8,128)}, f32[32,2048]{1,0:T(8,128)S(1)}, u32[]{:S(2)}, u32[]{:S(2)}) collective-permute-start(f32[32,2048]{1,0:T(8,128)} %get-tuple-element.31), channel_id=1, source_target_pairs={{0,1},{1,0},{2,3},{3,2},{4,5},{5,4},{6,7},{7,6},{8,9},{9,8},{10,11... | collective-permute-start | bytes 786440 | tf_op jit(solution)/shard_map/ppermute | solution.py:438
  94.0 1.8 %collective-permute-start.12 = (f32[32,2048]{1,0:T(8,128)}, f32[32,2048]{1,0:T(8,128)S(1)}, u32[]{:S(2)}, u32[]{:S(2)}) collective-permute-start(f32[32,2048]{1,0:T(8,128)} %get-tuple-element.33), channel_id=1, source_target_pairs={{0,3},{1,2},{2,1},{3,0},{4,7},{5,6},{6,5},{7,4},{8,11},{9,10},{10,... | collective-permute-start | bytes 786440 | tf_op jit(solution)/shard_map/ppermute | solution.py:438
  96.2 16.4 %pair_pull.1.refs_10_ = f32[3,16,128]{2,1,0:T(8,128)S(1)} custom-call(s32[16,8]{1,0:T(8,128)S(1)} %copy.14.pairs_ref, s32[144]{0:T(256)S(1)} %convert_element_type.19.lively_ref, f32[9,16,128]{2,1,0:T(8,128)S(1)} %collective-permute-done.26.refs_0_, f32[9,16,128]{2,1,0:T(8,128)S(1)} %collective-permute-done.27.refs_1_, ...), custom_call_target="tpu_custom_call" | custom-call | flops 104857600 | bytes 663552 | tf_op jit(solution)/shard_map/pair_pull/pallas_call | solution.py:389
  112.7 9.9 %z_backward.1 = (f32[2048,256]{1,0:T(8,128)}, f32[3,16,128]{2,1,0:T(8,128)}) custom-call(s32[1]{0:T(128)} %bitcast.me_ref, f32[32,2048]{1,0:T(8,128)S(1)} %copy-done.18, f32[32,2048]{1,0:T(8,128)S(1)} %collective-permute-done.10.refs_1_, f32[32,2048]{1,0:T(8,128)S(1)} %collective-permute-done.11.refs_2_, f32[32,2048]{1,0:T(8,128)S(1)} %collective-permute-done.12.refs_3_, ...), custom_call_target="tpu_custom_call" | custom-call | flops 1342177280 | bytes 4194304 | tf_op jit(solution)/shard_map/z_backward/pallas_call | solution.py:301
  (110 shorter events, 19.1 us)
Async XLA Ops:
  3.7 15.8 %collective-permute-start.33 = (f32[9,16,128]{2,1,0:T(8,128)S(1)}, f32[9,16,128]{2,1,0:T(8,128)S(1)}, u32[]{:S(2)}, u32[]{:S(2)}) collective-permute-start(f32[9,16,128]{2,1,0:T(8,128)S(1)} %pad_maximum_fusion.refs_4_), channel_id=1, source_target_pairs={{5,0},{6,1},{7,2},{4,3},{9,4},{10,5},{11,6},{8,7},{13,8},{14,9},{1... | collective-permute-start | bytes 221192 | tf_op jit(solution)/shard_map/ppermute | solution.py:456
  9.4 11.2 %collective-permute-start.32 = (f32[9,16,128]{2,1,0:T(8,128)S(1)}, f32[9,16,128]{2,1,0:T(8,128)S(1)}, u32[]{:S(2)}, u32[]{:S(2)}) collective-permute-start(f32[9,16,128]{2,1,0:T(8,128)S(1)} %pad_maximum_fusion.refs_4_), channel_id=1, source_target_pairs={{4,0},{5,1},{6,2},{7,3},{8,4},{9,5},{10,6},{11,7},{12,8},{13,9},{1... | collective-permute-start | bytes 221192 | tf_op jit(solution)/shard_map/ppermute | solution.py:456
  13.9 11.3 %collective-permute-start.13 = (f32[32,2048]{1,0:T(8,128)S(1)}, f32[32,2048]{1,0:T(8,128)S(1)}, u32[]{:S(2)}, u32[]{:S(2)}) collective-permute-start(f32[32,2048]{1,0:T(8,128)S(1)} %get-tuple-element.35), channel_id=1, source_target_pairs={{0,1},{1,0},{2,3},{3,2},{4,5},{5,4},{6,7},{7,6},{8,9},{9,8},{10,11... | collective-permute-start | bytes 786440 | tf_op jit(solution)/shard_map/ppermute | solution.py:438
  15.0 10.7 %collective-permute-start.14 = (f32[32,2048]{1,0:T(8,128)S(1)}, f32[32,2048]{1,0:T(8,128)S(1)}, u32[]{:S(2)}, u32[]{:S(2)}) collective-permute-start(f32[32,2048]{1,0:T(8,128)S(1)} %get-tuple-element.36), channel_id=1, source_target_pairs={{0,2},{1,3},{2,0},{3,1},{4,6},{5,7},{6,4},{7,5},{8,10},{9,11},{10,... | collective-permute-start | bytes 786440 | tf_op jit(solution)/shard_map/ppermute | solution.py:438
  15.4 14.9 %collective-permute-start.15 = (f32[32,2048]{1,0:T(8,128)S(1)}, f32[32,2048]{1,0:T(8,128)S(1)}, u32[]{:S(2)}, u32[]{:S(2)}) collective-permute-start(f32[32,2048]{1,0:T(8,128)S(1)} %get-tuple-element.37), channel_id=1, source_target_pairs={{0,3},{1,2},{2,1},{3,0},{4,7},{5,6},{6,5},{7,4},{8,11},{9,10},{10,... | collective-permute-start | bytes 786440 | tf_op jit(solution)/shard_map/ppermute | solution.py:438
  21.2 15.0 %collective-permute-start = (f32[32,2048]{1,0:T(8,128)}, f32[32,2048]{1,0:T(8,128)S(1)}, u32[]{:S(2)}, u32[]{:S(2)}) collective-permute-start(f32[32,2048]{1,0:T(8,128)} %get-tuple-element.25), channel_id=1, source_target_pairs={{0,1},{1,0},{2,3},{3,2},{4,5},{5,4},{6,7},{7,6},{8,9},{9,8},{10,11... | collective-permute-start | bytes 786440 | tf_op jit(solution)/shard_map/ppermute | solution.py:438
  23.9 10.7 %collective-permute-start.30 = (f32[9,16,128]{2,1,0:T(8,128)S(1)}, f32[9,16,128]{2,1,0:T(8,128)}, u32[]{:S(2)}, u32[]{:S(2)}) collective-permute-start(f32[9,16,128]{2,1,0:T(8,128)S(1)} %pad_maximum_fusion.refs_4_), channel_id=1, source_target_pairs={{1,0},{2,1},{3,2},{0,3},{5,4},{6,5},{7,6},{4,7},{9,8},{10,9},{11,1... | collective-permute-start | bytes 221192 | tf_op jit(solution)/shard_map/ppermute | solution.py:456
  25.2 11.0 %collective-permute-start.29 = (f32[9,16,128]{2,1,0:T(8,128)S(1)}, f32[9,16,128]{2,1,0:T(8,128)}, u32[]{:S(2)}, u32[]{:S(2)}) collective-permute-start(f32[9,16,128]{2,1,0:T(8,128)S(1)} %pad_maximum_fusion.refs_4_), channel_id=1, source_target_pairs={{3,0},{0,1},{1,2},{2,3},{7,4},{4,5},{5,6},{6,7},{11,8},{8,9},{9,10... | collective-permute-start | bytes 221192 | tf_op jit(solution)/shard_map/ppermute | solution.py:456
  26.4 10.8 %collective-permute-start.1 = (f32[32,2048]{1,0:T(8,128)}, f32[32,2048]{1,0:T(8,128)}, u32[]{:S(2)}, u32[]{:S(2)}) collective-permute-start(f32[32,2048]{1,0:T(8,128)} %get-tuple-element.26), channel_id=1, source_target_pairs={{0,2},{1,3},{2,0},{3,1},{4,6},{5,7},{6,4},{7,5},{8,10},{9,11},{10,... | collective-permute-start | bytes 786440 | tf_op jit(solution)/shard_map/ppermute | solution.py:438
  31.0 11.4 %collective-permute-start.2 = (f32[32,2048]{1,0:T(8,128)}, f32[32,2048]{1,0:T(8,128)}, u32[]{:S(2)}, u32[]{:S(2)}) collective-permute-start(f32[32,2048]{1,0:T(8,128)} %get-tuple-element.27), channel_id=1, source_target_pairs={{0,3},{1,2},{2,1},{3,0},{4,7},{5,6},{6,5},{7,4},{8,11},{9,10},{10,... | collective-permute-start | bytes 786440 | tf_op jit(solution)/shard_map/ppermute | solution.py:438
  34.6 9.6 %collective-permute-start.22 = (f32[4,32,256]{2,1,0:T(8,128)S(1)}, f32[4,32,256]{2,1,0:T(8,128)S(1)}, u32[]{:S(2)}, u32[]{:S(2)}) collective-permute-start(f32[4,32,256]{2,1,0:T(8,128)S(1)} %get-tuple-element.39.refs_0_), channel_id=1, source_target_pairs={{0,28},{4,0},{8,4},{12,8},{16,12},{20,16},{24,20},{28,24},{1,29},{... | collective-permute-start | bytes 393224 | tf_op jit(solution)/shard_map/ppermute | solution.py:465
  36.2 8.6 %collective-permute-start.21 = (f32[4,32,256]{2,1,0:T(8,128)S(1)}, f32[4,32,256]{2,1,0:T(8,128)S(1)}, u32[]{:S(2)}, u32[]{:S(2)}) collective-permute-start(f32[4,32,256]{2,1,0:T(8,128)S(1)} %get-tuple-element.39.refs_0_), channel_id=1, source_target_pairs={{0,24},{4,28},{8,0},{12,4},{16,8},{20,12},{24,16},{28,20},{1,25},{... | collective-permute-start | bytes 393224 | tf_op jit(solution)/shard_map/ppermute | solution.py:465
  36.2 9.7 %collective-permute-start.20 = (f32[4,32,256]{2,1,0:T(8,128)S(1)}, f32[4,32,256]{2,1,0:T(8,128)S(1)}, u32[]{:S(2)}, u32[]{:S(2)}) collective-permute-start(f32[4,32,256]{2,1,0:T(8,128)S(1)} %get-tuple-element.39.refs_0_), channel_id=1, source_target_pairs={{0,20},{4,24},{8,28},{12,0},{16,4},{20,8},{24,12},{28,16},{1,21},{... | collective-permute-start | bytes 393224 | tf_op jit(solution)/shard_map/ppermute | solution.py:465
  37.2 19.9 %collective-permute-start.19 = (f32[4,32,256]{2,1,0:T(8,128)S(1)}, f32[4,32,256]{2,1,0:T(8,128)S(1)}, u32[]{:S(2)}, u32[]{:S(2)}) collective-permute-start(f32[4,32,256]{2,1,0:T(8,128)S(1)} %get-tuple-element.39.refs_0_), channel_id=1, source_target_pairs={{0,16},{4,20},{8,24},{12,28},{16,0},{20,4},{24,8},{28,12},{1,17},{... | collective-permute-start | bytes 393224 | tf_op jit(solution)/shard_map/ppermute | solution.py:465
  42.4 17.2 %collective-permute-start.18 = (f32[4,32,256]{2,1,0:T(8,128)S(1)}, f32[4,32,256]{2,1,0:T(8,128)S(1)}, u32[]{:S(2)}, u32[]{:S(2)}) collective-permute-start(f32[4,32,256]{2,1,0:T(8,128)S(1)} %get-tuple-element.39.refs_0_), channel_id=1, source_target_pairs={{0,12},{4,16},{8,20},{12,24},{16,28},{20,0},{24,4},{28,8},{1,13},{... | collective-permute-start | bytes 393224 | tf_op jit(solution)/shard_map/ppermute | solution.py:465
  44.2 20.5 %collective-permute-start.17 = (f32[4,32,256]{2,1,0:T(8,128)S(1)}, f32[4,32,256]{2,1,0:T(8,128)S(1)}, u32[]{:S(2)}, u32[]{:S(2)}) collective-permute-start(f32[4,32,256]{2,1,0:T(8,128)S(1)} %get-tuple-element.39.refs_0_), channel_id=1, source_target_pairs={{0,8},{4,12},{8,16},{12,20},{16,24},{20,28},{24,0},{28,4},{1,9},{5... | collective-permute-start | bytes 393224 | tf_op jit(solution)/shard_map/ppermute | solution.py:465
  44.8 23.1 %collective-permute-start.16 = (f32[4,32,256]{2,1,0:T(8,128)S(1)}, f32[4,32,256]{2,1,0:T(8,128)S(1)}, u32[]{:S(2)}, u32[]{:S(2)}) collective-permute-start(f32[4,32,256]{2,1,0:T(8,128)S(1)} %get-tuple-element.39.refs_0_), channel_id=1, source_target_pairs={{0,4},{4,8},{8,12},{12,16},{16,20},{20,24},{24,28},{28,0},{1,5},{5... | collective-permute-start | bytes 393224 | tf_op jit(solution)/shard_map/ppermute | solution.py:465
  45.9 22.0 %collective-permute-start.9 = (f32[4,32,256]{2,1,0:T(8,128)S(1)}, f32[4,32,256]{2,1,0:T(8,128)S(1)}, u32[]{:S(2)}, u32[]{:S(2)}) collective-permute-start(f32[4,32,256]{2,1,0:T(8,128)S(1)} %get-tuple-element.29.refs_0_), channel_id=1, source_target_pairs={{0,28},{4,0},{8,4},{12,8},{16,12},{20,16},{24,20},{28,24},{1,29},{... | collective-permute-start | bytes 393224 | tf_op jit(solution)/shard_map/ppermute | solution.py:465
  57.1 12.9 %collective-permute-start.8 = (f32[4,32,256]{2,1,0:T(8,128)S(1)}, f32[4,32,256]{2,1,0:T(8,128)S(1)}, u32[]{:S(2)}, u32[]{:S(2)}) collective-permute-start(f32[4,32,256]{2,1,0:T(8,128)S(1)} %get-tuple-element.29.refs_0_), channel_id=1, source_target_pairs={{0,24},{4,28},{8,0},{12,4},{16,8},{20,12},{24,16},{28,20},{1,25},{... | collective-permute-start | bytes 393224 | tf_op jit(solution)/shard_map/ppermute | solution.py:465
  59.5 12.1 %collective-permute-start.7 = (f32[4,32,256]{2,1,0:T(8,128)S(1)}, f32[4,32,256]{2,1,0:T(8,128)S(1)}, u32[]{:S(2)}, u32[]{:S(2)}) collective-permute-start(f32[4,32,256]{2,1,0:T(8,128)S(1)} %get-tuple-element.29.refs_0_), channel_id=1, source_target_pairs={{0,20},{4,24},{8,28},{12,0},{16,4},{20,8},{24,12},{28,16},{1,21},{... | collective-permute-start | bytes 393224 | tf_op jit(solution)/shard_map/ppermute | solution.py:465
  64.7 15.7 %collective-permute-start.6 = (f32[4,32,256]{2,1,0:T(8,128)S(1)}, f32[4,32,256]{2,1,0:T(8,128)S(1)}, u32[]{:S(2)}, u32[]{:S(2)}) collective-permute-start(f32[4,32,256]{2,1,0:T(8,128)S(1)} %get-tuple-element.29.refs_0_), channel_id=1, source_target_pairs={{0,16},{4,20},{8,24},{12,28},{16,0},{20,4},{24,8},{28,12},{1,17},{... | collective-permute-start | bytes 393224 | tf_op jit(solution)/shard_map/ppermute | solution.py:465
  67.9 17.0 %collective-permute-start.5 = (f32[4,32,256]{2,1,0:T(8,128)S(1)}, f32[4,32,256]{2,1,0:T(8,128)S(1)}, u32[]{:S(2)}, u32[]{:S(2)}) collective-permute-start(f32[4,32,256]{2,1,0:T(8,128)S(1)} %get-tuple-element.29.refs_0_), channel_id=1, source_target_pairs={{0,12},{4,16},{8,20},{12,24},{16,28},{20,0},{24,4},{28,8},{1,13},{... | collective-permute-start | bytes 393224 | tf_op jit(solution)/shard_map/ppermute | solution.py:465
  67.9 17.0 %collective-permute-start.4 = (f32[4,32,256]{2,1,0:T(8,128)S(1)}, f32[4,32,256]{2,1,0:T(8,128)S(1)}, u32[]{:S(2)}, u32[]{:S(2)}) collective-permute-start(f32[4,32,256]{2,1,0:T(8,128)S(1)} %get-tuple-element.29.refs_0_), channel_id=1, source_target_pairs={{0,8},{4,12},{8,16},{12,20},{16,24},{20,28},{24,0},{28,4},{1,9},{5... | collective-permute-start | bytes 393224 | tf_op jit(solution)/shard_map/ppermute | solution.py:465
  70.0 15.8 %collective-permute-start.3 = (f32[4,32,256]{2,1,0:T(8,128)S(1)}, f32[4,32,256]{2,1,0:T(8,128)S(1)}, u32[]{:S(2)}, u32[]{:S(2)}) collective-permute-start(f32[4,32,256]{2,1,0:T(8,128)S(1)} %get-tuple-element.29.refs_0_), channel_id=1, source_target_pairs={{0,4},{4,8},{8,12},{12,16},{16,20},{20,24},{24,28},{28,0},{1,5},{5... | collective-permute-start | bytes 393224 | tf_op jit(solution)/shard_map/ppermute | solution.py:465
  71.6 21.6 %collective-permute-start.23 = (f32[32,2048]{1,0:T(8,128)S(1)}, f32[32,2048]{1,0:T(8,128)S(1)}, u32[]{:S(2)}, u32[]{:S(2)}) collective-permute-start(f32[32,2048]{1,0:T(8,128)S(1)} %get-tuple-element.41), channel_id=1, source_target_pairs={{0,1},{1,0},{2,3},{3,2},{4,5},{5,4},{6,7},{7,6},{8,9},{9,8},{10,11... | collective-permute-start | bytes 786440 | tf_op jit(solution)/shard_map/ppermute | solution.py:438
  80.5 8.3 %collective-permute-start.28 = (f32[9,16,128]{2,1,0:T(8,128)S(1)}, f32[9,16,128]{2,1,0:T(8,128)S(1)}, u32[]{:S(2)}, u32[]{:S(2)}) collective-permute-start(f32[9,16,128]{2,1,0:T(8,128)S(1)} %pad_maximum_fusion.refs_4_), channel_id=1, source_target_pairs={{29,0},{30,1},{31,2},{28,3},{1,4},{2,5},{3,6},{0,7},{5,8},{6,9},{7... | collective-permute-start | bytes 221192 | tf_op jit(solution)/shard_map/ppermute | solution.py:456
  85.0 8.3 %collective-permute-start.26 = (f32[9,16,128]{2,1,0:T(8,128)S(1)}, f32[9,16,128]{2,1,0:T(8,128)S(1)}, u32[]{:S(2)}, u32[]{:S(2)}) collective-permute-start(f32[9,16,128]{2,1,0:T(8,128)S(1)} %pad_maximum_fusion.refs_4_), channel_id=1, source_target_pairs={{31,0},{28,1},{29,2},{30,3},{3,4},{0,5},{1,6},{2,7},{7,8},{4,9},{5... | collective-permute-start | bytes 221192 | tf_op jit(solution)/shard_map/ppermute | solution.py:456
  85.8 26.8 %collective-permute-start.24 = (f32[32,2048]{1,0:T(8,128)}, f32[32,2048]{1,0:T(8,128)}, u32[]{:S(2)}, u32[]{:S(2)}) collective-permute-start(f32[32,2048]{1,0:T(8,128)} %get-tuple-element.42), channel_id=1, source_target_pairs={{0,2},{1,3},{2,0},{3,1},{4,6},{5,7},{6,4},{7,5},{8,10},{9,11},{10,... | collective-permute-start | bytes 786440 | tf_op jit(solution)/shard_map/ppermute | solution.py:438
  88.7 23.9 %collective-permute-start.25 = (f32[32,2048]{1,0:T(8,128)}, f32[32,2048]{1,0:T(8,128)S(1)}, u32[]{:S(2)}, u32[]{:S(2)}) collective-permute-start(f32[32,2048]{1,0:T(8,128)} %get-tuple-element.43), channel_id=1, source_target_pairs={{0,3},{1,2},{2,1},{3,0},{4,7},{5,6},{6,5},{7,4},{8,11},{9,10},{10,... | collective-permute-start | bytes 786440 | tf_op jit(solution)/shard_map/ppermute | solution.py:438
  90.9 21.8 %collective-permute-start.10 = (f32[32,2048]{1,0:T(8,128)}, f32[32,2048]{1,0:T(8,128)S(1)}, u32[]{:S(2)}, u32[]{:S(2)}) collective-permute-start(f32[32,2048]{1,0:T(8,128)} %get-tuple-element.31), channel_id=1, source_target_pairs={{0,1},{1,0},{2,3},{3,2},{4,5},{5,4},{6,7},{7,6},{8,9},{9,8},{10,11... | collective-permute-start | bytes 786440 | tf_op jit(solution)/shard_map/ppermute | solution.py:438
  93.2 19.5 %collective-permute-start.11 = (f32[32,2048]{1,0:T(8,128)}, f32[32,2048]{1,0:T(8,128)S(1)}, u32[]{:S(2)}, u32[]{:S(2)}) collective-permute-start(f32[32,2048]{1,0:T(8,128)} %get-tuple-element.32), channel_id=1, source_target_pairs={{0,2},{1,3},{2,0},{3,1},{4,6},{5,7},{6,4},{7,5},{8,10},{9,11},{10,... | collective-permute-start | bytes 786440 | tf_op jit(solution)/shard_map/ppermute | solution.py:438
  94.0 18.8 %collective-permute-start.12 = (f32[32,2048]{1,0:T(8,128)}, f32[32,2048]{1,0:T(8,128)S(1)}, u32[]{:S(2)}, u32[]{:S(2)}) collective-permute-start(f32[32,2048]{1,0:T(8,128)} %get-tuple-element.33), channel_id=1, source_target_pairs={{0,3},{1,2},{2,1},{3,0},{4,7},{5,6},{6,5},{7,4},{8,11},{9,10},{10,... | collective-permute-start | bytes 786440 | tf_op jit(solution)/shard_map/ppermute | solution.py:438
  (24 other events, 244.0 us)

commit v2 on v1

v2 whole, which is shorter than its diff:
```python
import math

import jax
import jax.numpy as jnp
import numpy as np
from jax import lax
from jax.experimental import pallas as pl
from jax.experimental.pallas import tpu as pltpu
from jax.sharding import PartitionSpec as P

nu_copper = 0.34
core_sq = 4.0
pair_scale = 4.0
CHUNKS = 2
VMEM_LIMIT = 24 * 1024 * 1024


def hartley_table(length):
    phase = np.outer(np.arange(length), np.arange(length)) % length
    angle = phase * (2.0 * math.pi / length)
    return ((np.cos(angle) + np.sin(angle)) / math.sqrt(length)).astype(np.float32)


def line_tables(length, plane_x):
    freq = np.arange(length, dtype=np.float64)
    wave = (2.0 * np.sin(math.pi * freq / length)) ** 2
    wave_z = wave[:, None]
    wave_y = wave[None, :]
    total = wave_y + wave_z
    zero = total == 0.0
    safe = np.where(zero, 1.0, total)
    ratio = 1.0 / (1.0 + safe / 2.0 + np.sqrt(safe + safe * safe / 4.0))
    ratio = ratio.astype(np.float32).astype(np.float64)
    elastic = 2.0 / (1.0 - nu_copper)
    gap = 1.0 - ratio * ratio
    green = ratio / gap
    first = -2.0 * (wave_y + elastic * wave_z) * green
    second = 2.0 * elastic * wave_z * safe * green * green
    weight_two = second
    weight_one = first + second * 2.0 * ratio * ratio / gap
    weight_zero = -first - second * (1.0 + ratio * ratio) / gap
    lap = ratio**length
    wrap_one = 1.0 / (1.0 - lap)
    wrap_two = length * lap / (1.0 - lap) ** 2
    leap = ratio**plane_x
    mask = np.where(zero, 0.0, 1.0)
    ratio = np.where(zero, 1.0, ratio)
    leap = np.where(zero, 1.0, leap)
    weight_zero = np.where(zero, 0.0, weight_zero)
    weight_one = np.where(zero, -1.0 / length, weight_one)
    weight_two = np.where(zero, 0.0, weight_two)
    wrap_one = np.where(zero, 1.0, wrap_one)
    wrap_two = np.where(zero, 0.0, wrap_two)
    tables = [ratio, leap, mask, weight_zero, weight_one, weight_two, wrap_one, wrap_two]
    return np.stack([t.astype(np.float32) for t in tables])


def halves(value):
    high = value.astype(jnp.bfloat16)
    low = (value - high.astype(jnp.float32)).astype(jnp.bfloat16)
    return high, low


def three_dots(left, right, dims):
    def one(a, b):
        return lax.dot_general(a, b, (dims, ((), ())), preferred_element_type=jnp.float32)

    return one(left[0], right[0]) + one(left[0], right[1]) + one(left[1], right[0])


def whole(memory=pltpu.VMEM):
    return pl.BlockSpec(memory_space=memory)


def anywhere(count):
    return [pl.BlockSpec(memory_space=pl.ANY)] * count


def params():
    return pltpu.CompilerParams(vmem_limit_bytes=VMEM_LIMIT)


def z_forward(field, table, me, groups, chunk, rows, after):
    cells, length = field.shape
    per = length // groups
    tile = min(512, cells)

    def kernel(me_ref, field_ref, table_ref, *refs):
        outs = refs[-groups:]
        own = me_ref[0]
        picked = [
            table_ref[pl.ds(pl.multiple_of((own ^ d) * per + chunk * rows, 8), rows), :]
            for d in range(groups)
        ]
        left = halves(jnp.concatenate(picked, axis=0))
        right = halves(field_ref[...])
        result = three_dots(left, right, ((1,), (1,)))
        for d in range(groups):
            outs[d][...] = result[d * rows : (d + 1) * rows]

    return pl.pallas_call(
        kernel,
        grid=(cells // tile,),
        in_specs=[
            pl.BlockSpec(memory_space=pltpu.SMEM),
            pl.BlockSpec((tile, length), lambda i: (i, 0)),
            pl.BlockSpec((length, length), lambda i: (0, 0)),
        ]
        + anywhere(len(after)),
        out_specs=[pl.BlockSpec((rows, tile), lambda i: (0, i))] * groups,
        out_shape=[jax.ShapeDtypeStruct((rows, cells), jnp.float32)] * groups,
        compiler_params=params(),
        cost_estimate=pl.CostEstimate(
            flops=6 * cells * length * rows * groups, bytes_accessed=8 * cells * length, transcendentals=0
        ),
        name="z_forward",
    )(me, field, table, *after)


def y_rows(table_ref, own, groups, plane_y):
    picked = [
        table_ref[pl.ds(pl.multiple_of((own ^ d) * plane_y, 8), plane_y), :] for d in range(groups)
    ]
    return halves(jnp.concatenate(picked, axis=0))


def y_forward(parts, table, lines, me, chunk, rows, plane_x, plane_y, after):
    groups = len(parts)
    length = table.shape[0]
    per = length // groups

    def kernel(me_ref, *refs):
        part_refs = refs[:groups]
        table_ref, lines_ref = refs[groups : groups + 2]
        spec_ref, ends_ref, gathered = refs[-3:]
        own = me_ref[0]
        right = y_rows(table_ref, own, groups, plane_y)
        for x in range(plane_x):
            gathered[x * rows : (x + 1) * rows, :] = jnp.concatenate(
                [ref[:, x * plane_y : (x + 1) * plane_y] for ref in part_refs], axis=1
            )
        result = three_dots(halves(gathered[...]), right, ((1,), (0,)))
        gathered[...] = result
        first = pl.multiple_of(own * per + chunk * rows, 8)
        ratio = lines_ref[0, pl.ds(first, rows), :]
        mask = lines_ref[2, pl.ds(first, rows), :]
        for g in range(0, rows, 8):
            step = ratio[g : g + 8]
            keep = mask[g : g + 8]
            zero = jnp.zeros_like(step)
            one, two = zero, zero
            for x in range(plane_x):
                value = gathered[x * rows + g : x * rows + g + 8, :]
                one = value + step * one
                two = one + step * two
                spec_ref[x, g : g + 8, :] = value * keep
            ends_ref[0, g : g + 8, :] = one
            ends_ref[1, g : g + 8, :] = two
            one, two = zero, zero
            for x in reversed(range(plane_x)):
                value = gathered[x * rows + g : x * rows + g + 8, :]
                one = value + step * one
                two = one + step * two
            ends_ref[2, g : g + 8, :] = one
            ends_ref[3, g : g + 8, :] = two

    return pl.pallas_call(
        kernel,
        in_specs=[whole(pltpu.SMEM)] + [whole()] * (groups + 2) + anywhere(len(after)),
        out_specs=[whole(), whole()],
        out_shape=[
            jax.ShapeDtypeStruct((plane_x, rows, length), jnp.float32),
            jax.ShapeDtypeStruct((4, rows, length), jnp.float32),
        ],
        scratch_shapes=[pltpu.VMEM((plane_x * rows, length), jnp.float32)],
        compiler_params=params(),
        cost_estimate=pl.CostEstimate(
            flops=6 * plane_x * rows * length * length,
            bytes_accessed=8 * plane_x * rows * length,
            transcendentals=0,
        ),
        name="y_forward",
    )(me, *parts, table, lines, *after)


def leap_power(leap, exponent, top):
    result, factor, bit = None, leap, 1
    while bit < top:
        term = jnp.where((exponent & bit) != 0, factor, jnp.ones_like(factor))
        result = term if result is None else result * term
        factor = factor * factor
        bit *= 2
    return result


def join_ends(ends, other, lines, me, level, plane_x):
    rows, length = ends.shape[1:]

    def kernel(me_ref, ends_ref, other_ref, lines_ref, out_ref):
        first = pl.multiple_of(me_ref[2], 8)
        right_half = ((me_ref[1] >> level) & 1) == 1
        leap = lines_ref[1, pl.ds(first, rows), :]
        for _ in range(level):
            leap = leap * leap
        span = float(plane_x * 2**level)
        for side in (0, 1):
            mine = [ends_ref[2 * side + k] for k in range(2)]
            theirs = [other_ref[2 * side + k] for k in range(2)]
            nearest = right_half if side == 0 else jnp.logical_not(right_half)
            near = [jnp.where(nearest, mine[k], theirs[k]) for k in range(2)]
            away = [jnp.where(nearest, theirs[k], mine[k]) for k in range(2)]
            out_ref[2 * side] = near[0] + leap * away[0]
            out_ref[2 * side + 1] = near[1] + leap * (away[1] + span * away[0])

    return pl.pallas_call(
        kernel,
        in_specs=[whole(pltpu.SMEM)] + [whole()] * 3,
        out_specs=whole(),
        out_shape=jax.ShapeDtypeStruct(ends.shape, jnp.float32),
        compiler_params=params(),
        cost_estimate=pl.CostEstimate(
            flops=8 * rows * length, bytes_accessed=48 * rows * length, transcendentals=0
        ),
        name="join_ends",
    )(me, ends, other, lines)


def y_backward(spec, ends, others, table, lines, me, groups, plane_y, after):
    plane_x, rows, length = spec.shape
    levels = len(others)
    blocks = 2**levels

    def kernel(me_ref, spec_ref, ends_ref, *refs):
        other_refs = refs[:levels]
        table_ref, lines_ref = refs[levels : levels + 2]
        outs, work = refs[-1 - groups : -1], refs[-1]
        right = y_rows(table_ref, me_ref[0], groups, plane_y)
        place = me_ref[1]
        first = pl.multiple_of(me_ref[2], 8)
        gaps = ([], [])
        for level in range(levels):
            size = 2**level
            inside = place & (size - 1)
            on_right = ((place >> level) & 1) == 1
            wrap = blocks - 2 * size
            gaps[0].append(inside + jnp.where(on_right, 0, wrap))
            gaps[1].append(size - 1 - inside + jnp.where(on_right, wrap, 0))
        for g in range(0, rows, 8):
            at = pl.ds(pl.multiple_of(first + g, 8), 8)
            step, leap = lines_ref[0, at, :], lines_ref[1, at, :]
            wrap_one, wrap_two = lines_ref[6, at, :], lines_ref[7, at, :]
            power = jnp.ones_like(leap)
            for _ in range(blocks - 1):
                power = power * leap
            carries = []
            for side in (0, 1):
                far_one = ends_ref[2 * side, g : g + 8, :]
                far_two = ends_ref[2 * side + 1, g : g + 8, :]
                one = power * far_one
                two = power * (far_two + float(plane_x * (blocks - 1)) * far_one)
                for level in range(levels):
                    gap = gaps[side][level]
                    factor = leap_power(leap, gap, blocks)
                    far_one = other_refs[level][2 * side, g : g + 8, :]
                    far_two = other_refs[level][2 * side + 1, g : g + 8, :]
                    one = one + factor * far_one
                    two = two + factor * (far_two + (plane_x * gap).astype(jnp.float32) * far_one)
                carries.append((one * wrap_one, two * wrap_one + wrap_two * one))
            weight_zero, weight_one, weight_two = lines_ref[3, at, :], lines_ref[4, at, :], lines_ref[5, at, :]
            one, two = carries[0]
            for x in range(plane_x):
                value = spec_ref[x, g : g + 8, :]
                one = value + step * one
                two = one + step * two
                work[x * rows + g : x * rows + g + 8, :] = (
                    weight_zero * value + weight_one * one + weight_two * two
                )
            one, two = carries[1]
            for x in reversed(range(plane_x)):
                value = spec_ref[x, g : g + 8, :]
                one = value + step * one
                two = one + step * two
                work[x * rows + g : x * rows + g + 8, :] += weight_one * one + weight_two * two
        work[...] = three_dots(halves(work[...]), right, ((1,), (1,)))
        pack = max(1, 128 // plane_y)
        for x in range(0, plane_x, pack):
            for d in range(groups):
                outs[d][:, x * plane_y : (x + pack) * plane_y] = jnp.concatenate(
                    [
                        work[(x + k) * rows : (x + k + 1) * rows, d * plane_y : (d + 1) * plane_y]
                        for k in range(pack)
                    ],
                    axis=1,
                )

    return pl.pallas_call(
        kernel,
        in_specs=[whole(pltpu.SMEM)] + [whole()] * (levels + 4) + anywhere(len(after)),
        out_specs=[whole()] * groups,
        out_shape=[jax.ShapeDtypeStruct((rows, plane_x * plane_y), jnp.float32)] * groups,
        scratch_shapes=[pltpu.VMEM((plane_x * rows, length), jnp.float32)],
        compiler_params=params(),
        cost_estimate=pl.CostEstimate(
            flops=6 * plane_x * rows * length * length,
            bytes_accessed=8 * plane_x * rows * length,
            transcendentals=0,
        ),
        name="y_backward",
    )(me, spec, ends, *others, table, lines, *after)


def segment_rows(vectors, offsets, cells, counts, pairs, me, plane_y, length, after):
    blocks, width = cells.shape

    def kernel(counts_ref, me_ref, vectors_ref, offsets_ref, cells_ref, pairs_ref, after_ref, out_ref, places_ref):
        cell = cells_ref[...]
        out_ref[0] = (cell // (length * plane_y)).astype(jnp.float32) + offsets_ref[0]
        out_ref[1] = (cell // length % plane_y).astype(jnp.float32) + offsets_ref[1]
        out_ref[2] = (cell % length).astype(jnp.float32) + offsets_ref[2]
        lane = lax.broadcasted_iota(jnp.int32, (1, width), 1)
        for b in range(blocks):
            live = lane < counts_ref[b]
            for k in range(3):
                out_ref[3 + k, b : b + 1, :] = jnp.where(live, vectors_ref[k, b : b + 1, :], 0.0)
        for k in range(3):
            out_ref[6 + k] = vectors_ref[3 + k]
        number = pairs_ref[...]
        column = number // blocks % 3
        even = jnp.full_like(number, me_ref[0]) & 1 == 0
        slot = jnp.where(column == 1, 0, jnp.where((column == 2) == even, 1, 2))
        places_ref[...] = (slot * 3 + number // (3 * blocks)) * blocks + number % blocks

    return pl.pallas_call(
        kernel,
        in_specs=[whole(pltpu.SMEM)] * 2 + [whole()] * 4 + [pl.BlockSpec(memory_space=pl.ANY)],
        out_specs=[whole()] * 2,
        out_shape=[
            jax.ShapeDtypeStruct((9, blocks, width), jnp.float32),
            jax.ShapeDtypeStruct(pairs.shape, jnp.int32),
        ],
        compiler_params=params(),
        name="segment_rows",
    )(counts, me, vectors, offsets, cells, pairs, after)


def z_backward(parts, table, cells, me, groups, chunks, rows, pull, source):
    cell_total = parts[0].shape[1]
    length = table.shape[0]
    per = length // groups
    seg_total = cells.shape[1]
    blocks, width = pull.shape[1:]
    tile = min(512, cell_total)
    steps = cell_total // tile

    def kernel(me_ref, *refs):
        part_refs, refs = refs[: groups * chunks], refs[groups * chunks :]
        table_ref, cells_ref, pull_ref, source_ref, stress_ref, force_ref, field, sems = refs
        own = me_ref[0]
        picked = [
            table_ref[pl.ds(pl.multiple_of((own ^ d) * per + c * rows, 8), rows), :]
            for c in range(chunks)
            for d in range(groups)
        ]
        right = halves(jnp.concatenate(picked, axis=0))
        left = halves(jnp.concatenate([ref[...] for ref in part_refs], axis=0))
        writes = []
        for i in range(steps):
            at = slice(i * tile, (i + 1) * tile)
            field[at, :] = three_dots([half[:, at] for half in left], right, ((0,), (0,)))
            writes.append(pltpu.make_async_copy(field.at[at], stress_ref.at[at], sems.at[i]))
            writes[-1].start()
        both = jnp.concatenate(left, axis=0)
        place = cells_ref[...] // length
        depth = cells_ref[...] % length
        lane_tile = min(512, seg_total)
        taus = []
        for k in range(0, seg_total, lane_tile):
            at = slice(k, k + lane_tile)
            hot = jnp.where(
                lax.broadcasted_iota(jnp.int32, (cell_total, lane_tile), 0) == place[:, at], 1.0, 0.0
            ).astype(jnp.bfloat16)
            found = jnp.dot(both, hot, preferred_element_type=jnp.float32)
            hot_z = jnp.where(
                lax.broadcasted_iota(jnp.int32, (length, lane_tile), 0) == depth[:, at], 1.0, 0.0
            ).astype(jnp.bfloat16)
            factor = jnp.dot(jnp.concatenate(right, axis=0), hot_z, preferred_element_type=jnp.float32)
            tau = jnp.sum(
                (found[:length] + found[length:]) * (factor[:length] + factor[length:]), axis=0, keepdims=True
            )
            taus += [tau[:, j : j + width] for j in range(0, lane_tile, width)]
        tau = jnp.concatenate(taus, axis=0)
        b0, b1, b2, t0, t1, t2 = (source_ref[3 + k] for k in range(6))
        force_ref[0] = pull_ref[0] + tau * (b1 * t2 - b2 * t1)
        force_ref[1] = pull_ref[1] + tau * (b2 * t0 - b0 * t2)
        force_ref[2] = pull_ref[2] + tau * (b0 * t1 - b1 * t0)
        for write in writes:
            write.wait()

    return pl.pallas_call(
        kernel,
        in_specs=[whole(pltpu.SMEM)] + [whole()] * (groups * chunks + 4),
        out_specs=anywhere(1) + [whole()],
        out_shape=[
            jax.ShapeDtypeStruct((cell_total, length), jnp.float32),
            jax.ShapeDtypeStruct((3, blocks, width), jnp.float32),
        ],
        scratch_shapes=[pltpu.VMEM((cell_total, length), jnp.float32), pltpu.SemaphoreType.DMA((steps,))],
        compiler_params=params(),
        cost_estimate=pl.CostEstimate(
            flops=6 * cell_total * length * length, bytes_accessed=8 * cell_total * length, transcendentals=0
        ),
        name="z_backward",
    )(me, *parts, table, cells, pull, source)


def join_rows(low, own, high, after):
    rows = own.shape[0]

    def kernel(low_ref, own_ref, high_ref, after_ref, out_ref):
        out_ref[0:rows] = low_ref[...]
        out_ref[rows : 2 * rows] = own_ref[...]
        out_ref[2 * rows :] = high_ref[...]

    return pl.pallas_call(
        kernel,
        in_specs=[whole()] * 3 + anywhere(1),
        out_specs=whole(),
        out_shape=jax.ShapeDtypeStruct((3 * rows,) + own.shape[1:], jnp.float32),
        compiler_params=params(),
        name="join_rows",
    )(low, own, high, after)


def spread_rows(source, after):
    rows, blocks, width = source.shape

    def kernel(source_ref, *refs):
        near = refs[-1]
        spread_row = lax.broadcasted_iota(jnp.int32, (3 * rows, rows * width), 0) % rows
        spread_col = lax.broadcasted_iota(jnp.int32, (3 * rows, rows * width), 1) // width
        spread = (spread_row == spread_col).astype(jnp.bfloat16)
        for b in range(blocks):
            own = jnp.concatenate([source_ref[k, b : b + 1, :] for k in range(rows)], axis=0)
            high = own.astype(jnp.bfloat16).astype(jnp.float32)
            rest = own - high
            middle = rest.astype(jnp.bfloat16).astype(jnp.float32)
            split = jnp.concatenate([high, middle, rest - middle], axis=0).astype(jnp.bfloat16)
            near[b * width : (b + 1) * width, :] = lax.dot_general(
                split, spread, (((0,), (0,)), ((), ())), preferred_element_type=jnp.float32
            )

    return pl.pallas_call(
        kernel,
        in_specs=[whole()] + anywhere(len(after)),
        out_specs=whole(),
        out_shape=jax.ShapeDtypeStruct((blocks * width, rows * width), jnp.float32),
        compiler_params=params(),
        name="spread_rows",
    )(source, *after)


def gather_rows(trios, me, plane_x, plane_y):
    blocks, width = trios[0].shape[1:]
    rows = trios[0].shape[0] // 3
    stride = rows * blocks
    padded = (9 * blocks + 127) // 128 * 128

    def kernel(me_ref, *refs):
        trio_refs = refs[:3]
        far, marks, flags = refs[3:]
        toward = jnp.where(me_ref[0] & 1 == 1, -float(plane_y), float(plane_y))
        flags[...] = jnp.zeros_like(flags)
        for slot in range(3):
            for p in range(3):
                base = slot * 3 + p
                trio = trio_refs[slot]
                for k in range(rows):
                    value = trio[p * rows + k]
                    if k == 0 and p != 1:
                        value = value + float((p - 1) * plane_x)
                    if k == 1 and slot > 0:
                        value = value + (toward if slot == 1 else -toward)
                    at = base * stride + k * blocks
                    far[at : at + blocks, :] = value
                size = jnp.maximum(
                    jnp.maximum(jnp.abs(trio[p * rows + 3]), jnp.abs(trio[p * rows + 4])),
                    jnp.abs(trio[p * rows + 5]),
                )
                flags[base * blocks : (base + 1) * blocks, :] = (size > 0.0).astype(jnp.float32)
        marks[...] = lax.dot_general(
            jnp.ones((8, width), jnp.bfloat16),
            flags[...].astype(jnp.bfloat16),
            (((1,), (1,)), ((), ())),
            preferred_element_type=jnp.float32,
        ).astype(jnp.int32)

    return pl.pallas_call(
        kernel,
        in_specs=[whole(pltpu.SMEM)] + [whole()] * 3,
        out_specs=[whole()] * 2,
        out_shape=[
            jax.ShapeDtypeStruct((9 * stride, width), jnp.float32),
            jax.ShapeDtypeStruct((8, padded), jnp.int32),
        ],
        scratch_shapes=[pltpu.VMEM((padded, width), jnp.float32)],
        compiler_params=params(),
        name="gather_rows",
    )(me, *trios)


def pair_pull(near, far, marks, pairs, after):
    blocks, partners = pairs.shape
    width = near.shape[0] // blocks
    rows = near.shape[1] // width
    stride = rows * blocks

    def kernel(pairs_ref, marks_ref, near, far, *refs):
        out_ref, total = refs[-2:]
        total[...] = jnp.zeros_like(total)

        def one_block(b, carry):
            own_at = pl.multiple_of(b * width, width)

            def one_partner(p, carry):
                number = pairs_ref[b, p]

                @pl.when(marks_ref[0, number] > 0)
                def _():
                    first = number // blocks * stride + number % blocks
                    other = [
                        jnp.broadcast_to(far[pl.ds(first + k * blocks, 1), :], (8, width)) for k in range(rows)
                    ]
                    for t in range(0, width, 8):
                        at = pl.ds(pl.multiple_of(own_at + t, 8), 8)
                        mine = [near[at, k * width : (k + 1) * width] for k in range(rows)]
                        dx, dy, dz = (mine[k] - other[k] for k in range(3))
                        inverse = lax.rsqrt(dx * dx + dy * dy + dz * dz + core_sq)
                        squared = inverse * inverse
                        burg_dot = mine[3] * other[3] + mine[4] * other[4] + mine[5] * other[5]
                        line_dot = mine[6] * other[6] + mine[7] * other[7] + mine[8] * other[8]
                        burg_own = mine[3] * dx + mine[4] * dy + mine[5] * dz
                        burg_far = other[3] * dx + other[4] * dy + other[5] * dz
                        weight = (line_dot * (squared * inverse)) * (
                            burg_dot - (3.0 * squared) * (burg_own * burg_far)
                        )
                        total[0, at, :] += weight * dx
                        total[1, at, :] += weight * dy
                        total[2, at, :] += weight * dz

                return carry

            return lax.fori_loop(0, partners, one_partner, carry)

        lax.fori_loop(0, blocks, one_block, 0)
        ones = jnp.ones((8, width), jnp.bfloat16)
        dims = (((1,), (1,)), ((), ()))
        for k in range(3):
            high, low = halves(total[k])
            summed = lax.dot_general(ones, high, dims, preferred_element_type=jnp.float32) + lax.dot_general(
                ones, low, dims, preferred_element_type=jnp.float32
            )
            for b in range(blocks):
                out_ref[k, b : b + 1, :] = pair_scale * summed[0:1, b * width : (b + 1) * width]

    return pl.pallas_call(
        kernel,
        in_specs=[whole(pltpu.SMEM)] * 2 + [whole()] * 2 + anywhere(len(after)),
        out_specs=whole(),
        out_shape=jax.ShapeDtypeStruct((3, blocks, width), jnp.float32),
        scratch_shapes=[pltpu.VMEM((3, blocks * width, width), jnp.float32)],
        compiler_params=params(),
        cost_estimate=pl.CostEstimate(
            flops=50 * blocks * partners * width * width,
            bytes_accessed=36 * stride * width,
            transcendentals=blocks * partners * width * width,
        ),
        name="pair_pull",
    )(pairs, marks, near, far, *after)


def per_device(eigen, seg_vec, seg_off, seg_cell, blk_count, pair_list):
    plane_x, plane_y, length = eigen.shape
    groups_x = lax.axis_size("gx")
    groups_y = lax.axis_size("gy")
    per = length // groups_y
    chunks = CHUNKS if per // CHUNKS >= 8 else 1
    rows = per // chunks
    place_x = lax.axis_index("gx").astype(jnp.int32)
    place_y = lax.axis_index("gy").astype(jnp.int32)
    mes = [jnp.stack([place_y, place_x, place_y * per + c * rows]) for c in range(chunks)]
    me = mes[0]
    table = jnp.asarray(hartley_table(length))
    lines = jnp.asarray(line_tables(length, plane_x))

    def swap(parts):
        return [parts[0]] + [
            lax.ppermute(parts[d], "gy", [(i, i ^ d) for i in range(groups_y)])
            for d in range(1, groups_y)
        ]

    field = eigen.reshape(plane_x * plane_y, length)
    sent = []
    for c in range(chunks):
        sent.append(z_forward(field, table, me, groups_y, c, rows, sent[-1][:1] if sent else []))
    arrived = [swap(parts) for parts in sent]

    seg_total = seg_cell.shape[2]
    block_total = blk_count.shape[2]
    width = seg_total // block_total
    cells = seg_cell.reshape(block_total, width)
    source, pairs = segment_rows(
        seg_vec.reshape(6, block_total, width),
        seg_off.reshape(3, block_total, width),
        cells,
        blk_count.reshape(block_total),
        pair_list.reshape(block_total, pair_list.shape[3]),
        me,
        plane_y,
        length,
        sent[-1][0],
    )
    low = lax.ppermute(source, "gx", [(i, (i + 1) % groups_x) for i in range(groups_x)])
    high = lax.ppermute(source, "gx", [((i + 1) % groups_x, i) for i in range(groups_x)])

    near = spread_rows(source, [])

    forward = []
    for c in range(chunks):
        after = [low, high, near] if c == 0 else [forward[-1][1]]
        forward.append(y_forward(arrived[c], table, lines, me, c, rows, plane_x, plane_y, after))
    trio = join_rows(low, source, high, forward[-1][1])
    other = [(i, (i + 1 if i % 2 else i - 1) % groups_y) for i in range(groups_y)]
    trios = [
        trio,
        lax.ppermute(trio, "gy", [(i, i ^ 1) for i in range(groups_y)]),
        lax.ppermute(trio, "gy", other),
    ]

    far, marks = gather_rows(trios, me, plane_x, plane_y)

    returned = []
    for c in range(chunks):
        spec, ends = forward[c]
        others, joined, level = [], ends, 0
        while 2**level < groups_x:
            others.append(lax.ppermute(joined, "gx", [(i, i ^ 2**level) for i in range(groups_x)]))
            if 2 ** (level + 1) < groups_x:
                joined = join_ends(joined, others[-1], lines, mes[c], level, plane_x)
            level += 1
        after = [returned[-1][0], far] if c else []
        returned.append(y_backward(spec, ends, others, table, lines, mes[c], groups_y, plane_y, after))
    landed = [swap(parts) for parts in returned]

    pull = pair_pull(near, far, marks, pairs, [returned[-1][0]])
    flat = [part for parts in landed for part in parts]
    stress, force = z_backward(
        flat, table, seg_cell.reshape(1, seg_total), me, groups_y, chunks, rows, pull, source
    )
    return stress.reshape(eigen.shape), force.reshape(3, 1, 1, seg_total)


def solution(mesh):
    return jax.shard_map(
        per_device,
        mesh=mesh,
        in_specs=(
            P("gx", "gy", None),
            P(None, "gx", "gy", None),
            P(None, "gx", "gy", None),
            P("gx", "gy", None),
            P("gx", "gy", None),
            P("gx", "gy", None, None),
        ),
        out_specs=(P("gx", "gy", None), P(None, "gx", "gy", None)),
        check_vma=False,
    )
```

time: 124 us -> 91.2 us (0.74)
  starting transfers between devices: 49.3 us -> 24.1 us
  waiting for transfers between devices: 19.1 us -> 26 us
  other arithmetic: 6.33 us -> 0.15 us
  local copies, waits for them, and re-layouts: 9.66 us -> 5.51 us
  Pallas kernels: 37.3 us -> 34.1 us
    ppermute x22 -> x10, starting transfers between devices: 37.2 us -> 13.4 us  [the longest x6 7.26 us: per_device(): lax.ppermute(joined, 'gx', [(i, i ^ 2 ** level) for i in range(groups_x)])]
    pallas_call x4 -> x12, Pallas kernels: 30.5 us -> 25.5 us  [the longest x1 9.63 us: pair_pull(): pl.pallas_call(kernel, in_specs=[whole(pltpu.SMEM)] * 2 + [whole()] * 2 +...]
    ppermute x22 -> x10, waiting for transfers between devices: 13.3 us -> 17.3 us  [the longest x6 9.87 us: per_device(): lax.ppermute(joined, 'gx', [(i, i ^ 2 ** level) for i in range(groups_x)])]
    reduce_or x10 -> x0, other arithmetic: 3.31 us -> none  [per_device(): jnp.any(part[3:6] != 0.0, axis=(0, 2))]
    ppermute x12, waiting for transfers between devices: 5.77 us -> 8.69 us  [swap(): lax.ppermute(parts[d], 'gy', [(i, i ^ d) for i in range(groups_y)])]
    unnamed x44 -> x36, local copies, waits for them, and re-layouts: 7.96 us -> 5.44 us
    ppermute x12, starting transfers between devices: 12.2 us -> 10.8 us  [swap(): lax.ppermute(parts[d], 'gy', [(i, i ^ d) for i in range(groups_y)])]
  transfers between devices with their start and end apart: 34 -> 22, of which waited for: 8 -> 7; matrix products, arithmetic and copies ran while one was open for 4% -> 0% of each run, Pallas kernels for 22% -> 26%
where the time goes in v2:
time: 91.2 us; the launch traced here: 90.9 us
  Pallas kernels  34.1 us (37%)
  waiting for transfers between devices  26 us (29%)
  starting transfers between devices  24.1 us (26%)
  local copies, waits for them, and re-layouts  5.51 us (6%)
  between operations  1.04 us (1%)
    ppermute x12, starting transfers between devices, swap(): lax.ppermute(parts[d], 'gy', [(i, i ^ d) for i in range(groups_y)])  10.8 us
    ppermute x6, waiting for transfers between devices, per_device(): lax.ppermute(joined, 'gx', [(i, i ^ 2 ** level) for i in range(groups_x)])  9.87 us
    pallas_call x1, Pallas kernels, pair_pull(): pl.pallas_call(kernel, in_specs=[whole(pltpu.SMEM)] * 2 + [whole()] * 2 +...  9.63 us
    ppermute x12, waiting for transfers between devices, swap(): lax.ppermute(parts[d], 'gy', [(i, i ^ d) for i in range(groups_y)])  8.69 us
    pallas_call x1, Pallas kernels, z_backward(): pl.pallas_call(kernel, in_specs=[whole(pltpu.SMEM)] + [whole()] * (groups...  7.27 us
    ppermute x6, starting transfers between devices, per_device(): lax.ppermute(joined, 'gx', [(i, i ^ 2 ** level) for i in range(groups_x)])  7.26 us
    unnamed x36, local copies, waits for them, and re-layouts  5.44 us
    pallas_call x2, Pallas kernels, z_forward(): pl.pallas_call(kernel, grid=(cells // tile,), in_specs=[pl.BlockSpec(memo...  5.42 us
  transfers between devices with their start and end apart: 22, of which 7 were waited for; matrix products, arithmetic and copies ran while one was open for 0% of the time, Pallas kernels for 26%

profile of v2, /device:TPU:1, one launch (start us, length us, event | category | flops | bytes accessed | tf_op | source)
XLA Modules:
  0.0 90.9 jit_solution(4165792511180484738)
XLA Ops:
  0.7 0.9 %copy-done.3 = f32[256,256]{1,0:T(8,128)S(1)} copy-done((f32[256,256]{1,0:T(8,128)S(1)}, f32[256,256]{1,0:T(8,128)}, u32[]{:S(2)}) %copy-start.3) | copy-done | bytes 262168
  1.7 1.6 %copy-done.5 = f32[32,64,256]{2,1,0:T(8,128)S(1)} copy-done((f32[32,64,256]{2,1,0:T(8,128)S(1)}, f32[32,64,256]{2,1,0:T(8,128)}, u32[]{:S(2)}) %copy-start.5) | copy-done | bytes 2097176
  3.3 3.2 %z_forward.2 = (f32[32,2048]{1,0:T(8,128)S(1)}, f32[32,2048]{1,0:T(8,128)}, f32[32,2048]{1,0:T(8,128)}, f32[32,2048]{1,0:T(8,128)}) custom-call(s32[3]{0:T(128)S(1)} %pad_add_fusion.me_ref, f32[2048,256]{1,0:T(8,128)S(1)} %bitcast.13, f32[256,256]{1,0:T(8,128)S(1)} %copy-done.3), custom_call_target="tpu_custom_call" | custom-call | flops 402653184 | bytes 4194304 | tf_op jit(solution)/shard_map/z_forward/pallas_call | solution.py:101
  6.5 2.7 %collective-permute-start.1 = (f32[32,2048]{1,0:T(8,128)}, f32[32,2048]{1,0:T(8,128)S(1)}, u32[]{:S(2)}, u32[]{:S(2)}) collective-permute-start(f32[32,2048]{1,0:T(8,128)} %get-tuple-element.30), channel_id=1, source_target_pairs={{0,2},{1,3},{2,0},{3,1},{4,6},{5,7},{6,4},{7,5},{8,10},{9,11},{10,... | collective-permute-start | bytes 786440 | tf_op jit(solution)/shard_map/ppermute | solution.py:597
  9.3 2.3 %z_forward.3 = (f32[32,2048]{1,0:T(8,128)S(1)}, f32[32,2048]{1,0:T(8,128)S(1)}, f32[32,2048]{1,0:T(8,128)S(1)}, f32[32,2048]{1,0:T(8,128)S(1)}) custom-call(s32[3]{0:T(128)S(1)} %pad_add_fusion.me_ref, f32[2048,256]{1,0:T(8,128)S(1)} %bitcast.14, f32[256,256]{1,0:T(8,128)S(1)} %copy-done.4, f32[32,2048]{1,0:T(8,128)S(1)} %get-tuple-element.28.refs_0_), custom_call_target="tpu_custom_call" | custom-call | flops 402653184 | bytes 4194304 | tf_op jit(solution)/shard_map/z_forward/pallas_call | solution.py:101
  12.2 1.7 %collective-permute-start.3 = (f32[9,16,128]{2,1,0:T(8,128)S(1)}, f32[9,16,128]{2,1,0:T(8,128)S(1)}, u32[]{:S(2)}, u32[]{:S(2)}) collective-permute-start(f32[9,16,128]{2,1,0:T(8,128)S(1)} %get-tuple-element.33.source_ref.own_ref.refs_11_), channel_id=1, source_target_pairs={{0,4},{4,8},{8,12},{12,16},{16,20},{20,24},{24,28},{28,0},{1,5},{5... | collective-permute-start | bytes 221192 | tf_op jit(solution)/shard_map/ppermute | solution.py:622
  13.9 3.1 %collective-permute-start.4 = (f32[9,16,128]{2,1,0:T(8,128)S(1)}, f32[9,16,128]{2,1,0:T(8,128)S(1)}, u32[]{:S(2)}, u32[]{:S(2)}) collective-permute-start(f32[9,16,128]{2,1,0:T(8,128)S(1)} %get-tuple-element.33.source_ref.own_ref.refs_11_), channel_id=1, source_target_pairs={{4,0},{8,4},{12,8},{16,12},{20,16},{24,20},{28,24},{0,28},{5,1},{9... | collective-permute-start | bytes 221192 | tf_op jit(solution)/shard_map/ppermute | solution.py:623
  17.0 2.4 %collective-permute-done.3.refs_6_.low_ref = f32[9,16,128]{2,1,0:T(8,128)S(1)} collective-permute-done((f32[9,16,128]{2,1,0:T(8,128)S(1)}, f32[9,16,128]{2,1,0:T(8,128)S(1)}, u32[]{:S(2)}, u32[]{:S(2)}) %collective-permute-start.3) | collective-permute-done | bytes 73760 | tf_op jit(solution)/shard_map/ppermute | solution.py:622
  20.2 1.2 %collective-permute-start.12 = (f32[32,2048]{1,0:T(8,128)S(1)}, f32[32,2048]{1,0:T(8,128)S(1)}, u32[]{:S(2)}, u32[]{:S(2)}) collective-permute-start(f32[32,2048]{1,0:T(8,128)S(1)} %get-tuple-element.41), channel_id=1, source_target_pairs={{0,2},{1,3},{2,0},{3,1},{4,6},{5,7},{6,4},{7,5},{8,10},{9,11},{10,... | collective-permute-start | bytes 786440 | tf_op jit(solution)/shard_map/ppermute | solution.py:597
  21.9 1.4 %spread_rows.1.refs_8_.near = f32[2048,1152]{1,0:T(8,128)S(1)} custom-call(f32[9,16,128]{2,1,0:T(8,128)S(1)} %get-tuple-element.33.source_ref.own_ref.refs_11_), custom_call_target="tpu_custom_call" | custom-call | tf_op jit(solution)/shard_map/spread_rows/pallas_call | solution.py:452
  24.1 1.2 %copy-done.12 = f32[32,2048]{1,0:T(8,128)S(1)} copy-done((f32[32,2048]{1,0:T(8,128)S(1)}, f32[32,2048]{1,0:T(8,128)}, u32[]{:S(2)}) %copy-start.12) | copy-done | bytes 262168
  25.3 1.9 %y_forward.2 = (f32[32,32,256]{2,1,0:T(8,128)S(1)}, f32[4,32,256]{2,1,0:T(8,128)S(1)}) custom-call(s32[3]{0:T(128)S(1)} %pad_add_fusion.me_ref, f32[32,2048]{1,0:T(8,128)S(1)} %get-tuple-element.28.refs_0_, f32[32,2048]{1,0:T(8,128)S(1)} %collective-permute-done.refs_1_, f32[32,2048]{1,0:T(8,128)S(1)} %copy-done.12, ...), custom_call_target="tpu_custom_call" | custom-call | flops 402653184 | bytes 2097152 | tf_op jit(solution)/shard_map/y_forward/pallas_call | solution.py:167
  27.9 4.4 %collective-permute-done.5.other_ref.refs_0_ = f32[4,32,256]{2,1,0:T(8,128)S(1)} collective-permute-done((f32[4,32,256]{2,1,0:T(8,128)S(1)}, f32[4,32,256]{2,1,0:T(8,128)S(1)}, u32[]{:S(2)}, u32[]{:S(2)}) %collective-permute-start.5) | collective-permute-done | bytes 131104 | tf_op jit(solution)/shard_map/ppermute | solution.py:646
  32.8 1.2 %collective-permute-start.6 = (f32[4,32,256]{2,1,0:T(8,128)S(1)}, f32[4,32,256]{2,1,0:T(8,128)S(1)}, u32[]{:S(2)}, u32[]{:S(2)}) collective-permute-start(f32[4,32,256]{2,1,0:T(8,128)S(1)} %join_ends.4.ends_ref), channel_id=1, source_target_pairs={{0,8},{4,12},{8,0},{12,4},{16,24},{20,28},{24,16},{28,20},{1,9},{5... | collective-permute-start | bytes 393224 | tf_op jit(solution)/shard_map/ppermute | solution.py:646
  34.0 1.3 %y_forward.3 = (f32[32,32,256]{2,1,0:T(8,128)S(1)}, f32[4,32,256]{2,1,0:T(8,128)S(1)}) custom-call(s32[3]{0:T(128)S(1)} %pad_add_fusion.me_ref, f32[32,2048]{1,0:T(8,128)S(1)} %get-tuple-element.32.after_ref.refs_0_, f32[32,2048]{1,0:T(8,128)S(1)} %collective-permute-done.11.refs_1_, f32[32,2048]{1,0:T(8,128)S(1)} %collective-permute-done.12.refs_2_, ...), custom_call_target="tpu_custom_call" | custom-call | flops 402653184 | bytes 2097152 | tf_op jit(solution)/shard_map/y_forward/pallas_call | solution.py:167
  35.3 1.0 %copy-done.7 = f32[32,32,256]{2,1,0:T(8,128)} copy-done((f32[32,32,256]{2,1,0:T(8,128)}, f32[32,32,256]{2,1,0:T(8,128)S(1)}, u32[]{:S(2)}) %copy-start.7) | copy-done | bytes 1048600
  36.3 1.1 %collective-permute-start.14 = (f32[4,32,256]{2,1,0:T(8,128)S(1)}, f32[4,32,256]{2,1,0:T(8,128)S(1)}, u32[]{:S(2)}, u32[]{:S(2)}) collective-permute-start(f32[4,32,256]{2,1,0:T(8,128)S(1)} %get-tuple-element.44.ends_ref.after_ref), channel_id=1, source_target_pairs={{0,4},{4,0},{8,12},{12,8},{16,20},{20,16},{24,28},{28,24},{1,5},{5... | collective-permute-start | bytes 393224 | tf_op jit(solution)/shard_map/ppermute | solution.py:646
  38.0 2.8 %collective-permute-start.7 = (f32[4,32,256]{2,1,0:T(8,128)S(1)}, f32[4,32,256]{2,1,0:T(8,128)S(1)}, u32[]{:S(2)}, u32[]{:S(2)}) collective-permute-start(f32[4,32,256]{2,1,0:T(8,128)S(1)} %join_ends.5), channel_id=1, source_target_pairs={{0,16},{4,20},{8,24},{12,28},{16,0},{20,4},{24,8},{28,12},{1,17},{... | collective-permute-start | bytes 393224 | tf_op jit(solution)/shard_map/ppermute | solution.py:646
  42.0 5.1 %collective-permute-done.7.refs_2_ = f32[4,32,256]{2,1,0:T(8,128)S(1)} collective-permute-done((f32[4,32,256]{2,1,0:T(8,128)S(1)}, f32[4,32,256]{2,1,0:T(8,128)S(1)}, u32[]{:S(2)}, u32[]{:S(2)}) %collective-permute-start.7) | collective-permute-done | bytes 131104 | tf_op jit(solution)/shard_map/ppermute | solution.py:646
  47.1 1.8 %y_backward.2 = (f32[32,2048]{1,0:T(8,128)S(1)}, f32[32,2048]{1,0:T(8,128)S(1)}, f32[32,2048]{1,0:T(8,128)S(1)}, f32[32,2048]{1,0:T(8,128)S(1)}) custom-call(s32[3]{0:T(128)S(1)} %pad_add_fusion.me_ref, f32[32,32,256]{2,1,0:T(8,128)S(1)} %copy-done.10, f32[4,32,256]{2,1,0:T(8,128)S(1)} %get-tuple-element.35.ends_ref.refs_6_, ...), custom_call_target="tpu_custom_call" | custom-call | flops 402653184 | bytes 2097152 | tf_op jit(solution)/shard_map/y_backward/pallas_call | solution.py:296
  48.9 1.1 %collective-permute-start.8 = (f32[32,2048]{1,0:T(8,128)S(1)}, f32[32,2048]{1,0:T(8,128)S(1)}, u32[]{:S(2)}, u32[]{:S(2)}) collective-permute-start(f32[32,2048]{1,0:T(8,128)S(1)} %get-tuple-element.37), channel_id=1, source_target_pairs={{0,1},{1,0},{2,3},{3,2},{4,5},{5,4},{6,7},{7,6},{8,9},{9,8},{10,11... | collective-permute-start | bytes 786440 | tf_op jit(solution)/shard_map/ppermute | solution.py:597
  50.1 1.3 %collective-permute-start.18 = (f32[27,16,128]{2,1,0:T(8,128)S(1)}, f32[27,16,128]{2,1,0:T(8,128)S(1)}, u32[]{:S(2)}, u32[]{:S(2)}) collective-permute-start(f32[27,16,128]{2,1,0:T(8,128)S(1)} %join_rows.1.refs_0_), channel_id=1, source_target_pairs={{0,3},{1,2},{2,1},{3,0},{4,7},{5,6},{6,5},{7,4},{8,11},{9,10},{10,... | collective-permute-start | bytes 663560 | tf_op jit(solution)/shard_map/ppermute | solution.py:636
  51.9 1.0 %collective-permute-start.16 = (f32[4,32,256]{2,1,0:T(8,128)S(1)}, f32[4,32,256]{2,1,0:T(8,128)S(1)}, u32[]{:S(2)}, u32[]{:S(2)}) collective-permute-start(f32[4,32,256]{2,1,0:T(8,128)S(1)} %join_ends.7), channel_id=1, source_target_pairs={{0,16},{4,20},{8,24},{12,28},{16,0},{20,4},{24,8},{28,12},{1,17},{... | collective-permute-start | bytes 393224 | tf_op jit(solution)/shard_map/ppermute | solution.py:646
  52.9 5.0 %collective-permute-done.18.refs_2_ = f32[27,16,128]{2,1,0:T(8,128)S(1)} collective-permute-done((f32[27,16,128]{2,1,0:T(8,128)S(1)}, f32[27,16,128]{2,1,0:T(8,128)S(1)}, u32[]{:S(2)}, u32[]{:S(2)}) %collective-permute-start.18) | collective-permute-done | bytes 221216 | tf_op jit(solution)/shard_map/ppermute | solution.py:636
  59.2 1.2 %collective-permute-start.10 = (f32[32,2048]{1,0:T(8,128)S(1)}, f32[32,2048]{1,0:T(8,128)S(1)}, u32[]{:S(2)}, u32[]{:S(2)}) collective-permute-start(f32[32,2048]{1,0:T(8,128)S(1)} %get-tuple-element.39), channel_id=1, source_target_pairs={{0,3},{1,2},{2,1},{3,0},{4,7},{5,6},{6,5},{7,4},{8,11},{9,10},{10,... | collective-permute-start | bytes 786440 | tf_op jit(solution)/shard_map/ppermute | solution.py:597
  60.8 1.8 %y_backward.3 = (f32[32,2048]{1,0:T(8,128)S(1)}, f32[32,2048]{1,0:T(8,128)S(1)}, f32[32,2048]{1,0:T(8,128)S(1)}, f32[32,2048]{1,0:T(8,128)S(1)}) custom-call(s32[3]{0:T(128)S(1)} %pad_add_fusion.2.me_ref, f32[32,32,256]{2,1,0:T(8,128)S(1)} %copy-done.8, f32[4,32,256]{2,1,0:T(8,128)S(1)} %get-tuple-element.44.ends_ref.after_ref, ...), custom_call_target="tpu_custom_call" | custom-call | flops 402653184 | bytes 2097152 | tf_op jit(solution)/shard_map/y_backward/pallas_call | solution.py:296
  62.5 0.9 %collective-permute-start.19 = (f32[32,2048]{1,0:T(8,128)S(1)}, f32[32,2048]{1,0:T(8,128)S(1)}, u32[]{:S(2)}, u32[]{:S(2)}) collective-permute-start(f32[32,2048]{1,0:T(8,128)S(1)} %get-tuple-element.47), channel_id=1, source_target_pairs={{0,1},{1,0},{2,3},{3,2},{4,5},{5,4},{6,7},{7,6},{8,9},{9,8},{10,11... | collective-permute-start | bytes 786440 | tf_op jit(solution)/shard_map/ppermute | solution.py:597
  64.1 1.1 %collective-permute-start.21 = (f32[32,2048]{1,0:T(8,128)S(1)}, f32[32,2048]{1,0:T(8,128)S(1)}, u32[]{:S(2)}, u32[]{:S(2)}) collective-permute-start(f32[32,2048]{1,0:T(8,128)S(1)} %get-tuple-element.49), channel_id=1, source_target_pairs={{0,3},{1,2},{2,1},{3,0},{4,7},{5,6},{6,5},{7,4},{8,11},{9,10},{10,... | collective-permute-start | bytes 786440 | tf_op jit(solution)/shard_map/ppermute | solution.py:597
  65.2 9.6 %pair_pull.1.refs_10_ = f32[3,16,128]{2,1,0:T(8,128)S(1)} custom-call(s32[16,8]{1,0:T(8,128)S(1)} %get-tuple-element.50.pairs_ref, s32[8,256]{1,0:T(8,128)S(1)} %get-tuple-element.51.marks_ref, f32[2048,1152]{1,0:T(8,128)S(1)} %copy-done.2, f32[1296,128]{1,0:T(8,128)S(1)} %get-tuple-element.45.refs_6_.far, f32[32,2048]{1,0:T(8,128)S(1)} %get-tuple-element.46.refs_0_.refs_4_), custom_call_target="tpu_custom_call" | custom-call | flops 104857600 | bytes 663552 | tf_op jit(solution)/shard_map/pair_pull/pallas_call | solution.py:565
  74.8 2.8 %collective-permute-done.20.refs_6_ = f32[32,2048]{1,0:T(8,128)S(1)} collective-permute-done((f32[32,2048]{1,0:T(8,128)S(1)}, f32[32,2048]{1,0:T(8,128)S(1)}, u32[]{:S(2)}, u32[]{:S(2)}) %collective-permute-start.20) | collective-permute-done | bytes 262176 | tf_op jit(solution)/shard_map/ppermute | solution.py:597
  77.6 5.9 %collective-permute-done.21.refs_7_ = f32[32,2048]{1,0:T(8,128)S(1)} collective-permute-done((f32[32,2048]{1,0:T(8,128)S(1)}, f32[32,2048]{1,0:T(8,128)S(1)}, u32[]{:S(2)}, u32[]{:S(2)}) %collective-permute-start.21) | collective-permute-done | bytes 262176 | tf_op jit(solution)/shard_map/ppermute | solution.py:597
  83.5 7.3 %z_backward.1 = (f32[2048,256]{1,0:T(8,128)}, f32[3,16,128]{2,1,0:T(8,128)}) custom-call(s32[3]{0:T(128)S(1)} %pad_add_fusion.me_ref, f32[32,2048]{1,0:T(8,128)S(1)} %get-tuple-element.36.refs_5_.refs_0_, f32[32,2048]{1,0:T(8,128)S(1)} %collective-permute-done.8.refs_1_, f32[32,2048]{1,0:T(8,128)S(1)} %collective-permute-done.9.refs_2_, ...), custom_call_target="tpu_custom_call" | custom-call | flops 805306368 | bytes 4194304 | tf_op jit(solution)/shard_map/z_backward/pallas_call | solution.py:399
  (67 shorter events, 8.9 us)
Async XLA Ops:
  0.6 8.6 %copy-start.17 = (s32[1,1,16,8]{2,3,1,0:T(8,128)S(1)}, s32[1,1,16,8]{2,3,1,0:T(8,128)}, u32[]{:S(2)}) copy-start(s32[1,1,16,8]{2,3,1,0:T(8,128)} %param.13) | copy-start | bytes 1540
  3.3 6.0 %copy-start.6 = (f32[32,64,256]{2,1,0:T(8,128)S(1)}, f32[32,64,256]{2,1,0:T(8,128)}, u32[]{:S(2)}) copy-start(f32[32,64,256]{2,1,0:T(8,128)} %param.8) | copy-start | bytes 6291460
  3.3 8.3 %copy-start.13 = (f32[6,1,1,2048]{3,2,1,0:T(1,128)S(1)}, f32[6,1,1,2048]{3,2,1,0:T(1,128)}, u32[]{:S(2)}) copy-start(f32[6,1,1,2048]{3,2,1,0:T(1,128)} %param.9) | copy-start | bytes 147460
  3.3 8.3 %copy-start.14 = (f32[3,1,1,2048]{3,2,1,0:T(1,128)S(1)}, f32[3,1,1,2048]{3,2,1,0:T(1,128)}, u32[]{:S(2)}) copy-start(f32[3,1,1,2048]{3,2,1,0:T(1,128)} %param.10) | copy-start | bytes 73732
  3.3 8.3 %copy-start.15 = (s32[1,1,2048]{2,1,0:T(1,128)S(1)}, s32[1,1,2048]{2,1,0:T(1,128)}, u32[]{:S(2)}) copy-start(s32[1,1,2048]{2,1,0:T(1,128)} %param.11) | copy-start | bytes 24580
  3.3 8.3 %copy-start.16 = (s32[1,1,16]{2,1,0:T(1,128)S(1)}, s32[1,1,16]{2,1,0:T(1,128)}, u32[]{:S(2)}) copy-start(s32[1,1,16]{2,1,0:T(1,128)} %param.12) | copy-start | bytes 196
  6.5 15.0 %collective-permute-start = (f32[32,2048]{1,0:T(8,128)}, f32[32,2048]{1,0:T(8,128)S(1)}, u32[]{:S(2)}, u32[]{:S(2)}) collective-permute-start(f32[32,2048]{1,0:T(8,128)} %get-tuple-element.29), channel_id=1, source_target_pairs={{0,1},{1,0},{2,3},{3,2},{4,5},{5,4},{6,7},{7,6},{8,9},{9,8},{10,11... | collective-permute-start | bytes 786440 | tf_op jit(solution)/shard_map/ppermute | solution.py:597
  6.5 16.9 %collective-permute-start.1 = (f32[32,2048]{1,0:T(8,128)}, f32[32,2048]{1,0:T(8,128)S(1)}, u32[]{:S(2)}, u32[]{:S(2)}) collective-permute-start(f32[32,2048]{1,0:T(8,128)} %get-tuple-element.30), channel_id=1, source_target_pairs={{0,2},{1,3},{2,0},{3,1},{4,6},{5,7},{6,4},{7,5},{8,10},{9,11},{10,... | collective-permute-start | bytes 786440 | tf_op jit(solution)/shard_map/ppermute | solution.py:597
  9.2 14.9 %collective-permute-start.2 = (f32[32,2048]{1,0:T(8,128)}, f32[32,2048]{1,0:T(8,128)}, u32[]{:S(2)}, u32[]{:S(2)}) collective-permute-start(f32[32,2048]{1,0:T(8,128)} %get-tuple-element.31), channel_id=1, source_target_pairs={{0,3},{1,2},{2,1},{3,0},{4,7},{5,6},{6,5},{7,4},{8,11},{9,10},{10,... | collective-permute-start | bytes 786440 | tf_op jit(solution)/shard_map/ppermute | solution.py:597
  12.2 7.2 %collective-permute-start.3 = (f32[9,16,128]{2,1,0:T(8,128)S(1)}, f32[9,16,128]{2,1,0:T(8,128)S(1)}, u32[]{:S(2)}, u32[]{:S(2)}) collective-permute-start(f32[9,16,128]{2,1,0:T(8,128)S(1)} %get-tuple-element.33.source_ref.own_ref.refs_11_), channel_id=1, source_target_pairs={{0,4},{4,8},{8,12},{12,16},{16,20},{20,24},{24,28},{28,0},{1,5},{5... | collective-permute-start | bytes 221192 | tf_op jit(solution)/shard_map/ppermute | solution.py:622
  13.9 6.4 %collective-permute-start.4 = (f32[9,16,128]{2,1,0:T(8,128)S(1)}, f32[9,16,128]{2,1,0:T(8,128)S(1)}, u32[]{:S(2)}, u32[]{:S(2)}) collective-permute-start(f32[9,16,128]{2,1,0:T(8,128)S(1)} %get-tuple-element.33.source_ref.own_ref.refs_11_), channel_id=1, source_target_pairs={{4,0},{8,4},{12,8},{16,12},{20,16},{24,20},{28,24},{0,28},{5,1},{9... | collective-permute-start | bytes 221192 | tf_op jit(solution)/shard_map/ppermute | solution.py:623
  19.4 14.6 %collective-permute-start.11 = (f32[32,2048]{1,0:T(8,128)S(1)}, f32[32,2048]{1,0:T(8,128)S(1)}, u32[]{:S(2)}, u32[]{:S(2)}) collective-permute-start(f32[32,2048]{1,0:T(8,128)S(1)} %get-tuple-element.40), channel_id=1, source_target_pairs={{0,1},{1,0},{2,3},{3,2},{4,5},{5,4},{6,7},{7,6},{8,9},{9,8},{10,11... | collective-permute-start | bytes 786440 | tf_op jit(solution)/shard_map/ppermute | solution.py:597
  20.2 13.8 %collective-permute-start.12 = (f32[32,2048]{1,0:T(8,128)S(1)}, f32[32,2048]{1,0:T(8,128)S(1)}, u32[]{:S(2)}, u32[]{:S(2)}) collective-permute-start(f32[32,2048]{1,0:T(8,128)S(1)} %get-tuple-element.41), channel_id=1, source_target_pairs={{0,2},{1,3},{2,0},{3,1},{4,6},{5,7},{6,4},{7,5},{8,10},{9,11},{10,... | collective-permute-start | bytes 786440 | tf_op jit(solution)/shard_map/ppermute | solution.py:597
  21.5 12.5 %collective-permute-start.13 = (f32[32,2048]{1,0:T(8,128)S(1)}, f32[32,2048]{1,0:T(8,128)S(1)}, u32[]{:S(2)}, u32[]{:S(2)}) collective-permute-start(f32[32,2048]{1,0:T(8,128)S(1)} %get-tuple-element.42), channel_id=1, source_target_pairs={{0,3},{1,2},{2,1},{3,0},{4,7},{5,6},{6,5},{7,4},{8,11},{9,10},{10,... | collective-permute-start | bytes 786440 | tf_op jit(solution)/shard_map/ppermute | solution.py:597
  27.2 8.1 %copy-start.9 = (f32[32,32,256]{2,1,0:T(8,128)}, f32[32,32,256]{2,1,0:T(8,128)S(1)}, u32[]{:S(2)}) copy-start(f32[32,32,256]{2,1,0:T(8,128)S(1)} %get-tuple-element.34.spec_ref) | copy-start | bytes 3145732
  27.3 5.0 %collective-permute-start.5 = (f32[4,32,256]{2,1,0:T(8,128)S(1)}, f32[4,32,256]{2,1,0:T(8,128)S(1)}, u32[]{:S(2)}, u32[]{:S(2)}) collective-permute-start(f32[4,32,256]{2,1,0:T(8,128)S(1)} %get-tuple-element.35.ends_ref.refs_6_), channel_id=1, source_target_pairs={{0,4},{4,0},{8,12},{12,8},{16,20},{20,16},{24,28},{28,24},{1,5},{5... | collective-permute-start | bytes 393224 | tf_op jit(solution)/shard_map/ppermute | solution.py:646
  32.8 4.6 %collective-permute-start.6 = (f32[4,32,256]{2,1,0:T(8,128)S(1)}, f32[4,32,256]{2,1,0:T(8,128)S(1)}, u32[]{:S(2)}, u32[]{:S(2)}) collective-permute-start(f32[4,32,256]{2,1,0:T(8,128)S(1)} %join_ends.4.ends_ref), channel_id=1, source_target_pairs={{0,8},{4,12},{8,0},{12,4},{16,24},{20,28},{24,16},{28,20},{1,9},{5... | collective-permute-start | bytes 393224 | tf_op jit(solution)/shard_map/ppermute | solution.py:646
  36.3 4.5 %collective-permute-start.14 = (f32[4,32,256]{2,1,0:T(8,128)S(1)}, f32[4,32,256]{2,1,0:T(8,128)S(1)}, u32[]{:S(2)}, u32[]{:S(2)}) collective-permute-start(f32[4,32,256]{2,1,0:T(8,128)S(1)} %get-tuple-element.44.ends_ref.after_ref), channel_id=1, source_target_pairs={{0,4},{4,0},{8,12},{12,8},{16,20},{20,16},{24,28},{28,24},{1,5},{5... | collective-permute-start | bytes 393224 | tf_op jit(solution)/shard_map/ppermute | solution.py:646
  38.0 9.1 %collective-permute-start.7 = (f32[4,32,256]{2,1,0:T(8,128)S(1)}, f32[4,32,256]{2,1,0:T(8,128)S(1)}, u32[]{:S(2)}, u32[]{:S(2)}) collective-permute-start(f32[4,32,256]{2,1,0:T(8,128)S(1)} %join_ends.5), channel_id=1, source_target_pairs={{0,16},{4,20},{8,24},{12,28},{16,0},{20,4},{24,8},{28,12},{1,17},{... | collective-permute-start | bytes 393224 | tf_op jit(solution)/shard_map/ppermute | solution.py:646
  40.7 6.4 %copy-start.10 = (f32[32,32,256]{2,1,0:T(8,128)S(1)}, f32[32,32,256]{2,1,0:T(8,128)}, u32[]{:S(2)}) copy-start(f32[32,32,256]{2,1,0:T(8,128)} %copy-done.9) | copy-start | bytes 3145732
  41.4 9.9 %collective-permute-start.15 = (f32[4,32,256]{2,1,0:T(8,128)S(1)}, f32[4,32,256]{2,1,0:T(8,128)S(1)}, u32[]{:S(2)}, u32[]{:S(2)}) collective-permute-start(f32[4,32,256]{2,1,0:T(8,128)S(1)} %join_ends.6.ends_ref), channel_id=1, source_target_pairs={{0,8},{4,12},{8,0},{12,4},{16,24},{20,28},{24,16},{28,20},{1,9},{5... | collective-permute-start | bytes 393224 | tf_op jit(solution)/shard_map/ppermute | solution.py:646
  47.1 13.7 %copy-start.8 = (f32[32,32,256]{2,1,0:T(8,128)S(1)}, f32[32,32,256]{2,1,0:T(8,128)}, u32[]{:S(2)}) copy-start(f32[32,32,256]{2,1,0:T(8,128)} %copy-done.7) | copy-start | bytes 3145732
  47.1 18.1 %copy-start.2 = (f32[2048,1152]{1,0:T(8,128)S(1)}, f32[2048,1152]{1,0:T(8,128)}, u32[]{:S(2)}) copy-start(f32[2048,1152]{1,0:T(8,128)} %copy-done.1) | copy-start | bytes 28311556
  48.9 15.2 %collective-permute-start.8 = (f32[32,2048]{1,0:T(8,128)S(1)}, f32[32,2048]{1,0:T(8,128)S(1)}, u32[]{:S(2)}, u32[]{:S(2)}) collective-permute-start(f32[32,2048]{1,0:T(8,128)S(1)} %get-tuple-element.37), channel_id=1, source_target_pairs={{0,1},{1,0},{2,3},{3,2},{4,5},{5,4},{6,7},{7,6},{8,9},{9,8},{10,11... | collective-permute-start | bytes 786440 | tf_op jit(solution)/shard_map/ppermute | solution.py:597
  50.0 3.0 %collective-permute-start.17 = (f32[27,16,128]{2,1,0:T(8,128)S(1)}, f32[27,16,128]{2,1,0:T(8,128)S(1)}, u32[]{:S(2)}, u32[]{:S(2)}) collective-permute-start(f32[27,16,128]{2,1,0:T(8,128)S(1)} %join_rows.1.refs_0_), channel_id=1, source_target_pairs={{0,1},{1,0},{2,3},{3,2},{4,5},{5,4},{6,7},{7,6},{8,9},{9,8},{10,11... | collective-permute-start | bytes 663560 | tf_op jit(solution)/shard_map/ppermute | solution.py:635
  50.1 7.8 %collective-permute-start.18 = (f32[27,16,128]{2,1,0:T(8,128)S(1)}, f32[27,16,128]{2,1,0:T(8,128)S(1)}, u32[]{:S(2)}, u32[]{:S(2)}) collective-permute-start(f32[27,16,128]{2,1,0:T(8,128)S(1)} %join_rows.1.refs_0_), channel_id=1, source_target_pairs={{0,3},{1,2},{2,1},{3,0},{4,7},{5,6},{6,5},{7,4},{8,11},{9,10},{10,... | collective-permute-start | bytes 663560 | tf_op jit(solution)/shard_map/ppermute | solution.py:636
  51.9 8.8 %collective-permute-start.16 = (f32[4,32,256]{2,1,0:T(8,128)S(1)}, f32[4,32,256]{2,1,0:T(8,128)S(1)}, u32[]{:S(2)}, u32[]{:S(2)}) collective-permute-start(f32[4,32,256]{2,1,0:T(8,128)S(1)} %join_ends.7), channel_id=1, source_target_pairs={{0,16},{4,20},{8,24},{12,28},{16,0},{20,4},{24,8},{28,12},{1,17},{... | collective-permute-start | bytes 393224 | tf_op jit(solution)/shard_map/ppermute | solution.py:646
  58.6 16.2 %collective-permute-start.9 = (f32[32,2048]{1,0:T(8,128)S(1)}, f32[32,2048]{1,0:T(8,128)S(1)}, u32[]{:S(2)}, u32[]{:S(2)}) collective-permute-start(f32[32,2048]{1,0:T(8,128)S(1)} %get-tuple-element.38), channel_id=1, source_target_pairs={{0,2},{1,3},{2,0},{3,1},{4,6},{5,7},{6,4},{7,5},{8,10},{9,11},{10,... | collective-permute-start | bytes 786440 | tf_op jit(solution)/shard_map/ppermute | solution.py:597
  59.2 15.6 %collective-permute-start.10 = (f32[32,2048]{1,0:T(8,128)S(1)}, f32[32,2048]{1,0:T(8,128)S(1)}, u32[]{:S(2)}, u32[]{:S(2)}) collective-permute-start(f32[32,2048]{1,0:T(8,128)S(1)} %get-tuple-element.39), channel_id=1, source_target_pairs={{0,3},{1,2},{2,1},{3,0},{4,7},{5,6},{6,5},{7,4},{8,11},{9,10},{10,... | collective-permute-start | bytes 786440 | tf_op jit(solution)/shard_map/ppermute | solution.py:597
  62.5 12.3 %collective-permute-start.19 = (f32[32,2048]{1,0:T(8,128)S(1)}, f32[32,2048]{1,0:T(8,128)S(1)}, u32[]{:S(2)}, u32[]{:S(2)}) collective-permute-start(f32[32,2048]{1,0:T(8,128)S(1)} %get-tuple-element.47), channel_id=1, source_target_pairs={{0,1},{1,0},{2,3},{3,2},{4,5},{5,4},{6,7},{7,6},{8,9},{9,8},{10,11... | collective-permute-start | bytes 786440 | tf_op jit(solution)/shard_map/ppermute | solution.py:597
  63.5 14.2 %collective-permute-start.20 = (f32[32,2048]{1,0:T(8,128)S(1)}, f32[32,2048]{1,0:T(8,128)S(1)}, u32[]{:S(2)}, u32[]{:S(2)}) collective-permute-start(f32[32,2048]{1,0:T(8,128)S(1)} %get-tuple-element.48), channel_id=1, source_target_pairs={{0,2},{1,3},{2,0},{3,1},{4,6},{5,7},{6,4},{7,5},{8,10},{9,11},{10,... | collective-permute-start | bytes 786440 | tf_op jit(solution)/shard_map/ppermute | solution.py:597
  64.1 19.4 %collective-permute-start.21 = (f32[32,2048]{1,0:T(8,128)S(1)}, f32[32,2048]{1,0:T(8,128)S(1)}, u32[]{:S(2)}, u32[]{:S(2)}) collective-permute-start(f32[32,2048]{1,0:T(8,128)S(1)} %get-tuple-element.49), channel_id=1, source_target_pairs={{0,3},{1,2},{2,1},{3,0},{4,7},{5,6},{6,5},{7,4},{8,11},{9,10},{10,... | collective-permute-start | bytes 786440 | tf_op jit(solution)/shard_map/ppermute | solution.py:597
  (8 other events, 17.9 us)

commit v3 on v2

--- a/solution.py
+++ b/solution.py
@@ -11,8 +11,15 @@
 nu_copper = 0.34
 core_sq = 4.0
 pair_scale = 4.0
-CHUNKS = 2
+CHUNKS = (32, 32)
+SHARES = (5, 11)
+ORDER = ()
 VMEM_LIMIT = 24 * 1024 * 1024
+COSTS = {'join_ends': (0.0, 3.0, 0.0, 0.0), 'pair_pull': (1.5, 0.0)}
+
+
+def counted(cost):
+    return pl.CostEstimate(flops=int(cost * 1e9), bytes_accessed=0, transcendentals=0)
 
 
 def hartley_table(length):
@@ -80,39 +87,35 @@
     return pltpu.CompilerParams(vmem_limit_bytes=VMEM_LIMIT)
 
 
-def z_forward(field, table, me, groups, chunk, rows, after):
+def z_forward(field, table, me, groups, offset, rows, after, cost):
     cells, length = field.shape
     per = length // groups
-    tile = min(512, cells)
+    depth = groups * rows
 
     def kernel(me_ref, field_ref, table_ref, *refs):
         outs = refs[-groups:]
         own = me_ref[0]
         picked = [
-            table_ref[pl.ds(pl.multiple_of((own ^ d) * per + chunk * rows, 8), rows), :]
-            for d in range(groups)
+            table_ref[pl.ds(pl.multiple_of((own ^ d) * per + offset, 8), rows), :] for d in range(groups)
         ]
         left = halves(jnp.concatenate(picked, axis=0))
         right = halves(field_ref[...])
-        result = three_dots(left, right, ((1,), (1,)))
+        dims = (((1,), (1,)), ((), ()))
+        both = lax.dot_general(
+            jnp.concatenate(left, axis=0), right[0], dims, preferred_element_type=jnp.float32
+        )
+        result = both[:depth] + both[depth:]
+        result = result + lax.dot_general(left[0], right[1], dims, preferred_element_type=jnp.float32)
         for d in range(groups):
             outs[d][...] = result[d * rows : (d + 1) * rows]
 
     return pl.pallas_call(
         kernel,
-        grid=(cells // tile,),
-        in_specs=[
-            pl.BlockSpec(memory_space=pltpu.SMEM),
-            pl.BlockSpec((tile, length), lambda i: (i, 0)),
-            pl.BlockSpec((length, length), lambda i: (0, 0)),
-        ]
-        + anywhere(len(after)),
-        out_specs=[pl.BlockSpec((rows, tile), lambda i: (0, i))] * groups,
+        in_specs=[whole(pltpu.SMEM)] + [whole()] * 2 + anywhere(len(after)),
+        out_specs=[whole()] * groups,
         out_shape=[jax.ShapeDtypeStruct((rows, cells), jnp.float32)] * groups,
         compiler_params=params(),
-        cost_estimate=pl.CostEstimate(
-            flops=6 * cells * length * rows * groups, bytes_accessed=8 * cells * length, transcendentals=0
-        ),
+        cost_estimate=counted(cost),
         name="z_forward",
     )(me, field, table, *after)
 
@@ -124,16 +127,19 @@
     return halves(jnp.concatenate(picked, axis=0))
 
 
-def y_forward(parts, table, lines, me, chunk, rows, plane_x, plane_y, after):
+def y_forward(parts, table, lines, me, offset, rows, plane_x, plane_y, after, cost):
     groups = len(parts)
     length = table.shape[0]
     per = length // groups
 
     def kernel(me_ref, *refs):
         part_refs = refs[:groups]
-        table_ref, lines_ref = refs[groups : groups + 2]
-        spec_ref, ends_ref, gathered = refs[-3:]
+        table_ref, all_lines = refs[groups : groups + 2]
+        spec_ref, ends_ref, lines_ref, gathered, lines_sem = refs[-5:]
         own = me_ref[0]
+        first = pl.multiple_of(own * per + offset, 8)
+        fetch = pltpu.make_async_copy(all_lines.at[:, pl.ds(first, rows)], lines_ref, lines_sem)
+        fetch.start()
         right = y_rows(table_ref, own, groups, plane_y)
         for x in range(plane_x):
             gathered[x * rows : (x + 1) * rows, :] = jnp.concatenate(
@@ -141,9 +147,9 @@
             )
         result = three_dots(halves(gathered[...]), right, ((1,), (0,)))
         gathered[...] = result
-        first = pl.multiple_of(own * per + chunk * rows, 8)
-        ratio = lines_ref[0, pl.ds(first, rows), :]
-        mask = lines_ref[2, pl.ds(first, rows), :]
+        fetch.wait()
+        ratio = lines_ref[0]
+        mask = lines_ref[2]
         for g in range(0, rows, 8):
             step = ratio[g : g + 8]
             keep = mask[g : g + 8]
@@ -166,19 +172,16 @@
 
     return pl.pallas_call(
         kernel,
-        in_specs=[whole(pltpu.SMEM)] + [whole()] * (groups + 2) + anywhere(len(after)),
-        out_specs=[whole(), whole()],
+        in_specs=[whole(pltpu.SMEM)] + [whole()] * (groups + 1) + anywhere(1 + len(after)),
+        out_specs=[whole()] * 3,
         out_shape=[
             jax.ShapeDtypeStruct((plane_x, rows, length), jnp.float32),
             jax.ShapeDtypeStruct((4, rows, length), jnp.float32),
+            jax.ShapeDtypeStruct((lines.shape[0], rows, length), jnp.float32),
         ],
-        scratch_shapes=[pltpu.VMEM((plane_x * rows, length), jnp.float32)],
-        compiler_params=params(),
-        cost_estimate=pl.CostEstimate(
-            flops=6 * plane_x * rows * length * length,
-            bytes_accessed=8 * plane_x * rows * length,
-            transcendentals=0,
-        ),
+        scratch_shapes=[pltpu.VMEM((plane_x * rows, length), jnp.float32), pltpu.SemaphoreType.DMA],
+        compiler_params=params(),
+        cost_estimate=counted(cost),
         name="y_forward",
     )(me, *parts, table, lines, *after)
 
@@ -193,13 +196,13 @@
     return result
 
 
-def join_ends(ends, other, lines, me, level, plane_x):
+def join_ends(ends, other, lines, me, level, plane_x, after, cost):
     rows, length = ends.shape[1:]
 
-    def kernel(me_ref, ends_ref, other_ref, lines_ref, out_ref):
-        first = pl.multiple_of(me_ref[2], 8)
+    def kernel(me_ref, ends_ref, other_ref, lines_ref, *refs):
+        out_ref = refs[-1]
         right_half = ((me_ref[1] >> level) & 1) == 1
-        leap = lines_ref[1, pl.ds(first, rows), :]
+        leap = lines_ref[1]
         for _ in range(level):
             leap = leap * leap
         span = float(plane_x * 2**level)
@@ -214,18 +217,16 @@
 
     return pl.pallas_call(
         kernel,
-        in_specs=[whole(pltpu.SMEM)] + [whole()] * 3,
+        in_specs=[whole(pltpu.SMEM)] + [whole()] * 3 + anywhere(len(after)),
         out_specs=whole(),
         out_shape=jax.ShapeDtypeStruct(ends.shape, jnp.float32),
         compiler_params=params(),
-        cost_estimate=pl.CostEstimate(
-            flops=8 * rows * length, bytes_accessed=48 * rows * length, transcendentals=0
-        ),
+        cost_estimate=counted(cost),
         name="join_ends",
-    )(me, ends, other, lines)
-
-
-def y_backward(spec, ends, others, table, lines, me, groups, plane_y, after):
+    )(me, ends, other, lines, *after)
+
+
+def y_backward(spec, ends, others, table, lines, me, groups, plane_y, after, cost):
     plane_x, rows, length = spec.shape
     levels = len(others)
     blocks = 2**levels
@@ -236,7 +237,6 @@
         outs, work = refs[-1 - groups : -1], refs[-1]
         right = y_rows(table_ref, me_ref[0], groups, plane_y)
         place = me_ref[1]
-        first = pl.multiple_of(me_ref[2], 8)
         gaps = ([], [])
         for level in range(levels):
             size = 2**level
@@ -246,7 +246,7 @@
             gaps[0].append(inside + jnp.where(on_right, 0, wrap))
             gaps[1].append(size - 1 - inside + jnp.where(on_right, wrap, 0))
         for g in range(0, rows, 8):
-            at = pl.ds(pl.multiple_of(first + g, 8), 8)
+            at = slice(g, g + 8)
             step, leap = lines_ref[0, at, :], lines_ref[1, at, :]
             wrap_one, wrap_two = lines_ref[6, at, :], lines_ref[7, at, :]
             power = jnp.ones_like(leap)
@@ -300,16 +300,12 @@
         out_shape=[jax.ShapeDtypeStruct((rows, plane_x * plane_y), jnp.float32)] * groups,
         scratch_shapes=[pltpu.VMEM((plane_x * rows, length), jnp.float32)],
         compiler_params=params(),
-        cost_estimate=pl.CostEstimate(
-            flops=6 * plane_x * rows * length * length,
-            bytes_accessed=8 * plane_x * rows * length,
-            transcendentals=0,
-        ),
+        cost_estimate=counted(cost),
         name="y_backward",
     )(me, spec, ends, *others, table, lines, *after)
 
 
-def segment_rows(vectors, offsets, cells, counts, pairs, me, plane_y, length, after):
+def segment_rows(vectors, offsets, cells, counts, pairs, me, plane_y, length, after, cost):
     blocks, width = cells.shape
 
     def kernel(counts_ref, me_ref, vectors_ref, offsets_ref, cells_ref, pairs_ref, after_ref, out_ref, places_ref):
@@ -339,39 +335,60 @@
             jax.ShapeDtypeStruct(pairs.shape, jnp.int32),
         ],
         compiler_params=params(),
+        cost_estimate=counted(cost),
         name="segment_rows",
     )(counts, me, vectors, offsets, cells, pairs, after)
 
 
-def z_backward(parts, table, cells, me, groups, chunks, rows, pull, source):
+def z_backward(parts, table, cells, me, groups, offset, rows, before, pull, source, after, cost):
     cell_total = parts[0].shape[1]
     length = table.shape[0]
     per = length // groups
+    depth = groups * rows
     seg_total = cells.shape[1]
-    blocks, width = pull.shape[1:]
+    blocks, width = source.shape[1:]
     tile = min(512, cell_total)
     steps = cell_total // tile
+    adds = before is not None
+    last = pull is not None
 
     def kernel(me_ref, *refs):
-        part_refs, refs = refs[: groups * chunks], refs[groups * chunks :]
-        table_ref, cells_ref, pull_ref, source_ref, stress_ref, force_ref, field, sems = refs
+        part_refs, refs = refs[:groups], refs[groups:]
+        table_ref, cells_ref, source_ref, refs = refs[0], refs[1], refs[2], refs[3:]
+        if adds:
+            old_ref, old_tau_ref, refs = refs[0], refs[1], refs[2:]
+        if last:
+            pull_ref, refs = refs[0], refs[1:]
+            stress_ref, out_ref, field, sems = refs[-4:]
+        else:
+            field, out_ref = refs[-2:]
         own = me_ref[0]
         picked = [
-            table_ref[pl.ds(pl.multiple_of((own ^ d) * per + c * rows, 8), rows), :]
-            for c in range(chunks)
+            table_ref[pl.ds(pl.multiple_of((own ^ d) * per + offset, 8), rows), :]
             for d in range(groups)
         ]
         right = halves(jnp.concatenate(picked, axis=0))
         left = halves(jnp.concatenate([ref[...] for ref in part_refs], axis=0))
+        both = jnp.concatenate(left, axis=0)
+        twice = jnp.concatenate([right[0], right[0]], axis=0)
         writes = []
         for i in range(steps):
             at = slice(i * tile, (i + 1) * tile)
-            field[at, :] = three_dots([half[:, at] for half in left], right, ((0,), (0,)))
-            writes.append(pltpu.make_async_copy(field.at[at], stress_ref.at[at], sems.at[i]))
-            writes[-1].start()
-        both = jnp.concatenate(left, axis=0)
+            share = lax.dot_general(
+                both[:, at], twice, (((0,), (0,)), ((), ())), preferred_element_type=jnp.float32
+            ) + lax.dot_general(
+                left[0][:, at], right[1], (((0,), (0,)), ((), ())), preferred_element_type=jnp.float32
+            )
+            field[at, :] = share + old_ref[at, :] if adds else share
+            if last:
+                writes.append(
+                    pltpu.make_async_copy(
+                        field.at[pl.ds(i * tile, tile)], stress_ref.at[pl.ds(i * tile, tile)], sems.at[i]
+                    )
+                )
+                writes[-1].start()
         place = cells_ref[...] // length
-        depth = cells_ref[...] % length
+        level = cells_ref[...] % length
         lane_tile = min(512, seg_total)
         taus = []
         for k in range(0, seg_total, lane_tile):
@@ -381,39 +398,48 @@
             ).astype(jnp.bfloat16)
             found = jnp.dot(both, hot, preferred_element_type=jnp.float32)
             hot_z = jnp.where(
-                lax.broadcasted_iota(jnp.int32, (length, lane_tile), 0) == depth[:, at], 1.0, 0.0
+                lax.broadcasted_iota(jnp.int32, (length, lane_tile), 0) == level[:, at], 1.0, 0.0
             ).astype(jnp.bfloat16)
             factor = jnp.dot(jnp.concatenate(right, axis=0), hot_z, preferred_element_type=jnp.float32)
             tau = jnp.sum(
-                (found[:length] + found[length:]) * (factor[:length] + factor[length:]), axis=0, keepdims=True
+                (found[:depth] + found[depth:]) * (factor[:depth] + factor[depth:]), axis=0, keepdims=True
             )
             taus += [tau[:, j : j + width] for j in range(0, lane_tile, width)]
         tau = jnp.concatenate(taus, axis=0)
-        b0, b1, b2, t0, t1, t2 = (source_ref[3 + k] for k in range(6))
-        force_ref[0] = pull_ref[0] + tau * (b1 * t2 - b2 * t1)
-        force_ref[1] = pull_ref[1] + tau * (b2 * t0 - b0 * t2)
-        force_ref[2] = pull_ref[2] + tau * (b0 * t1 - b1 * t0)
+        if adds:
+            tau = tau + old_tau_ref[...]
+        if last:
+            b0, b1, b2, t0, t1, t2 = (source_ref[3 + k] for k in range(6))
+            out_ref[0] = pull_ref[0] + tau * (b1 * t2 - b2 * t1)
+            out_ref[1] = pull_ref[1] + tau * (b2 * t0 - b0 * t2)
+            out_ref[2] = pull_ref[2] + tau * (b0 * t1 - b1 * t0)
+        else:
+            out_ref[...] = tau
         for write in writes:
             write.wait()
 
-    return pl.pallas_call(
-        kernel,
-        in_specs=[whole(pltpu.SMEM)] + [whole()] * (groups * chunks + 4),
-        out_specs=anywhere(1) + [whole()],
+    operands = [me, *parts, table, cells, source]
+    if adds:
+        operands += list(before)
+    if last:
+        operands.append(pull)
+    scratch = [pltpu.VMEM((cell_total, length), jnp.float32), pltpu.SemaphoreType.DMA((steps,))]
+    return pl.pallas_call(
+        kernel,
+        in_specs=[whole(pltpu.SMEM)] + [whole()] * (len(operands) - 1) + anywhere(len(after)),
+        out_specs=(anywhere(1) if last else [whole()]) + [whole()],
         out_shape=[
             jax.ShapeDtypeStruct((cell_total, length), jnp.float32),
-            jax.ShapeDtypeStruct((3, blocks, width), jnp.float32),
+            jax.ShapeDtypeStruct((3, blocks, width) if last else (blocks, width), jnp.float32),
         ],
-        scratch_shapes=[pltpu.VMEM((cell_total, length), jnp.float32), pltpu.SemaphoreType.DMA((steps,))],
-        compiler_params=params(),
-        cost_estimate=pl.CostEstimate(
-            flops=6 * cell_total * length * length, bytes_accessed=8 * cell_total * length, transcendentals=0
-        ),
+        scratch_shapes=scratch if last else [],
+        compiler_params=params(),
+        cost_estimate=counted(cost),
         name="z_backward",
-    )(me, *parts, table, cells, pull, source)
-
-
-def join_rows(low, own, high, after):
+    )(*operands, *after)
+
+
+def join_rows(low, own, high, after, cost):
     rows = own.shape[0]
 
     def kernel(low_ref, own_ref, high_ref, after_ref, out_ref):
@@ -427,11 +453,12 @@
         out_specs=whole(),
         out_shape=jax.ShapeDtypeStruct((3 * rows,) + own.shape[1:], jnp.float32),
         compiler_params=params(),
+        cost_estimate=counted(cost),
         name="join_rows",
     )(low, own, high, after)
 
 
-def spread_rows(source, after):
+def spread_rows(source, after, cost):
     rows, blocks, width = source.shape
 
     def kernel(source_ref, *refs):
@@ -455,11 +482,12 @@
         out_specs=whole(),
         out_shape=jax.ShapeDtypeStruct((blocks * width, rows * width), jnp.float32),
         compiler_params=params(),
+        cost_estimate=counted(cost),
         name="spread_rows",
     )(source, *after)
 
 
-def gather_rows(trios, me, plane_x, plane_y):
+def gather_rows(trios, me, plane_x, plane_y, cost):
     blocks, width = trios[0].shape[1:]
     rows = trios[0].shape[0] // 3
     stride = rows * blocks
@@ -504,11 +532,12 @@
         ],
         scratch_shapes=[pltpu.VMEM((padded, width), jnp.float32)],
         compiler_params=params(),
+        cost_estimate=counted(cost),
         name="gather_rows",
     )(me, *trios)
 
 
-def pair_pull(near, far, marks, pairs, after):
+def pair_pull(near, far, marks, pairs, first_block, count, after, cost):
     blocks, partners = pairs.shape
     width = near.shape[0] // blocks
     rows = near.shape[1] // width
@@ -518,8 +547,10 @@
         out_ref, total = refs[-2:]
         total[...] = jnp.zeros_like(total)
 
-        def one_block(b, carry):
+        def one_block(index, carry):
+            b = first_block + index
             own_at = pl.multiple_of(b * width, width)
+            sum_at = pl.multiple_of(index * width, width)
 
             def one_partner(p, carry):
                 number = pairs_ref[b, p]
@@ -543,15 +574,16 @@
                         weight = (line_dot * (squared * inverse)) * (
                             burg_dot - (3.0 * squared) * (burg_own * burg_far)
                         )
-                        total[0, at, :] += weight * dx
-                        total[1, at, :] += weight * dy
-                        total[2, at, :] += weight * dz
+                        to = pl.ds(pl.multiple_of(sum_at + t, 8), 8)
+                        total[0, to, :] += weight * dx
+                        total[1, to, :] += weight * dy
+                        total[2, to, :] += weight * dz
 
                 return carry
 
             return lax.fori_loop(0, partners, one_partner, carry)
 
-        lax.fori_loop(0, blocks, one_block, 0)
+        lax.fori_loop(0, count, one_block, 0)
         ones = jnp.ones((8, width), jnp.bfloat16)
         dims = (((1,), (1,)), ((), ()))
         for k in range(3):
@@ -559,23 +591,24 @@
             summed = lax.dot_general(ones, high, dims, preferred_element_type=jnp.float32) + lax.dot_general(
                 ones, low, dims, preferred_element_type=jnp.float32
             )
-            for b in range(blocks):
+            for b in range(count):
                 out_ref[k, b : b + 1, :] = pair_scale * summed[0:1, b * width : (b + 1) * width]
 
     return pl.pallas_call(
         kernel,
         in_specs=[whole(pltpu.SMEM)] * 2 + [whole()] * 2 + anywhere(len(after)),
         out_specs=whole(),
-        out_shape=jax.ShapeDtypeStruct((3, blocks, width), jnp.float32),
-        scratch_shapes=[pltpu.VMEM((3, blocks * width, width), jnp.float32)],
-        compiler_params=params(),
-        cost_estimate=pl.CostEstimate(
-            flops=50 * blocks * partners * width * width,
-            bytes_accessed=36 * stride * width,
-            transcendentals=blocks * partners * width * width,
-        ),
+        out_shape=jax.ShapeDtypeStruct((3, count, width), jnp.float32),
+        scratch_shapes=[pltpu.VMEM((3, count * width, width), jnp.float32)],
+        compiler_params=params(),
+        cost_estimate=counted(cost),
         name="pair_pull",
     )(pairs, marks, near, far, *after)
+
+
+def hint(name, index):
+    costs = COSTS.get(name, ())
+    return costs[index] if index < len(costs) else 0.0
 
 
 def per_device(eigen, seg_vec, seg_off, seg_cell, blk_count, pair_list):
@@ -583,12 +616,12 @@
     groups_x = lax.axis_size("gx")
     groups_y = lax.axis_size("gy")
     per = length // groups_y
-    chunks = CHUNKS if per // CHUNKS >= 8 else 1
-    rows = per // chunks
+    sizes = CHUNKS if sum(CHUNKS) == per else (per,)
+    offsets = [sum(sizes[:c]) for c in range(len(sizes))]
+    chunks = len(sizes)
     place_x = lax.axis_index("gx").astype(jnp.int32)
     place_y = lax.axis_index("gy").astype(jnp.int32)
-    mes = [jnp.stack([place_y, place_x, place_y * per + c * rows]) for c in range(chunks)]
-    me = mes[0]
+    me = jnp.stack([place_y, place_x])
     table = jnp.asarray(hartley_table(length))
     lines = jnp.asarray(line_tables(length, plane_x))
 
@@ -599,10 +632,7 @@
         ]
 
     field = eigen.reshape(plane_x * plane_y, length)
-    sent = []
-    for c in range(chunks):
-        sent.append(z_forward(field, table, me, groups_y, c, rows, sent[-1][:1] if sent else []))
-    arrived = [swap(parts) for parts in sent]
+    sent = [z_forward(field, table, me, groups_y, 0, sizes[0], [], hint("z_forward", 0))]
 
     seg_total = seg_cell.shape[2]
     block_total = blk_count.shape[2]
@@ -617,45 +647,59 @@
         me,
         plane_y,
         length,
-        sent[-1][0],
+        sent[0][0],
+        hint("segment_rows", 0),
     )
+    for c in range(1, chunks):
+        sent.append(z_forward(field, table, me, groups_y, offsets[c], sizes[c], [source], hint("z_forward", c)))
+    arrived = [swap(parts) for parts in sent]
     low = lax.ppermute(source, "gx", [(i, (i + 1) % groups_x) for i in range(groups_x)])
     high = lax.ppermute(source, "gx", [((i + 1) % groups_x, i) for i in range(groups_x)])
 
-    near = spread_rows(source, [])
-
-    forward = []
+    near = spread_rows(source, [sent[-1][0]] if "near" in ORDER else [], hint("spread_rows", 0))
+
+    levels = groups_x.bit_length() - 1
+    forward, others, joined = [], [], []
     for c in range(chunks):
-        after = [low, high, near] if c == 0 else [forward[-1][1]]
-        forward.append(y_forward(arrived[c], table, lines, me, c, rows, plane_x, plane_y, after))
-    trio = join_rows(low, source, high, forward[-1][1])
+        after = [low, high, near] if c == 0 else [joined[0][-1] if "yf1" in ORDER else forward[-1][1]]
+        forward.append(y_forward(arrived[c], table, lines, me, offsets[c], sizes[c], plane_x, plane_y, after, hint("y_forward", c)))
+        others.append([])
+        joined.append([forward[c][1]])
+        for level in range(levels):
+            others[c].append(lax.ppermute(joined[c][-1], "gx", [(i, i ^ 2**level) for i in range(groups_x)]))
+            if level < levels - 1:
+                joined[c].append(
+                    join_ends(joined[c][-1], others[c][-1], forward[c][2], me, level, plane_x, [], hint("join_ends", 2 * c + level))
+                )
+    trio = join_rows(low, source, high, joined[0][-1] if "trio" in ORDER else forward[-1][1], hint("join_rows", 0))
     other = [(i, (i + 1 if i % 2 else i - 1) % groups_y) for i in range(groups_y)]
     trios = [
         trio,
         lax.ppermute(trio, "gy", [(i, i ^ 1) for i in range(groups_y)]),
         lax.ppermute(trio, "gy", other),
     ]
-
-    far, marks = gather_rows(trios, me, plane_x, plane_y)
-
-    returned = []
+    far, marks = gather_rows(trios, me, plane_x, plane_y, hint("gather_rows", 0))
+
+    shares = SHARES if len(SHARES) == chunks and sum(SHARES) == block_total else (0,) * (chunks - 1) + (block_total,)
+    returned, pulls = [], []
     for c in range(chunks):
-        spec, ends = forward[c]
-        others, joined, level = [], ends, 0
-        while 2**level < groups_x:
-            others.append(lax.ppermute(joined, "gx", [(i, i ^ 2**level) for i in range(groups_x)]))
-            if 2 ** (level + 1) < groups_x:
-                joined = join_ends(joined, others[-1], lines, mes[c], level, plane_x)
-            level += 1
-        after = [returned[-1][0], far] if c else []
-        returned.append(y_backward(spec, ends, others, table, lines, mes[c], groups_y, plane_y, after))
+        spec, ends, own_lines = forward[c]
+        after = pulls[-1:] if pulls else [far] + (joined[-1][-1:] if "yb0" in ORDER else [])
+        returned.append(y_backward(spec, ends, others[c], table, own_lines, me, groups_y, plane_y, after, hint("y_backward", c)))
+        first = sum(shares[:c])
+        if shares[c]:
+            pulls.append(pair_pull(near, far, marks, pairs, first, shares[c], returned[-1][:1], hint("pair_pull", c)))
     landed = [swap(parts) for parts in returned]
 
-    pull = pair_pull(near, far, marks, pairs, [returned[-1][0]])
-    flat = [part for parts in landed for part in parts]
-    stress, force = z_backward(
-        flat, table, seg_cell.reshape(1, seg_total), me, groups_y, chunks, rows, pull, source
-    )
+    pull = pulls[0] if len(pulls) == 1 else jnp.concatenate(pulls, axis=1)
+    before = None
+    flat_cells = seg_cell.reshape(1, seg_total)
+    for c in range(chunks):
+        before = z_backward(
+            landed[c], table, flat_cells, me, groups_y, offsets[c], sizes[c], before,
+            pull if c == chunks - 1 else None, source, pulls[-1:], hint("z_backward", c),
+        )
+    stress, force = before
     return stress.reshape(eigen.shape), force.reshape(3, 1, 1, seg_total)
 
 

time: 91.2 us -> 79.9 us (0.88)
  waiting for transfers between devices: 26 us -> 11.9 us
  starting transfers between devices: 24.1 us -> 28.3 us
  local copies, waits for them, and re-layouts: 5.51 us -> 2.65 us
  Pallas kernels: 34.1 us -> 35.7 us
    ppermute x1, waiting for transfers between devices: 4.95 us -> 0.01 us  [per_device(): lax.ppermute(trio, 'gy', other)]
    ppermute x12, waiting for transfers between devices: 8.69 us -> 4.02 us  [swap(): lax.ppermute(parts[d], 'gy', [(i, i ^ d) for i in range(groups_y)])]
    pallas_call x1 -> x2, Pallas kernels: 9.63 us -> 12.8 us  [pair_pull(): pl.pallas_call(kernel, in_specs=[whole(pltpu.SMEM)] * 2 + [whole()] * 2 +...]
    unnamed x36 -> x20, local copies, waits for them, and re-layouts: 5.44 us -> 2.58 us
    ppermute x6, starting transfers between devices: 7.26 us -> 9.9 us  [per_device(): lax.ppermute(joined[c][-1], 'gx', [(i, i ^ 2 ** level) for i in range(gro...]
    ppermute x1, waiting for transfers between devices: 2.44 us -> 0.01 us  [per_device(): lax.ppermute(source, 'gx', [(i, (i + 1) % groups_x) for i in range(groups...]
    ppermute x6, waiting for transfers between devices: 9.87 us -> 7.87 us  [per_device(): lax.ppermute(joined[c][-1], 'gx', [(i, i ^ 2 ** level) for i in range(gro...]
    pallas_call x7 -> x8, Pallas kernels: 15 us -> 13.5 us  [the longest x2 8.58 us: z_backward(): pl.pallas_call(kernel, in_specs=[whole(pltpu.SMEM)] + [whole()] * (len(op...]
  transfers between devices with their start and end apart: 22 -> 22, of which waited for: 7 -> 7; matrix products, arithmetic and copies ran while one was open for 0% -> 0% of each run, Pallas kernels for 26% -> 37%
where the time goes in v3:
time: 79.9 us; the launch traced here: 79.7 us
  Pallas kernels  35.7 us (45%)
  starting transfers between devices  28.3 us (35%)
  waiting for transfers between devices  11.9 us (15%)
  local copies, waits for them, and re-layouts  2.65 us (3%)
  between operations  1.04 us (1%)
    pallas_call x2, Pallas kernels, pair_pull(): pl.pallas_call(kernel, in_specs=[whole(pltpu.SMEM)] * 2 + [whole()] * 2 +...  12.8 us
    ppermute x12, starting transfers between devices, swap(): lax.ppermute(parts[d], 'gy', [(i, i ^ d) for i in range(groups_y)])  11.7 us
    ppermute x6, starting transfers between devices, per_device(): lax.ppermute(joined[c][-1], 'gx', [(i, i ^ 2 ** level) for i in range(gro...  9.9 us
    pallas_call x2, Pallas kernels, z_backward(): pl.pallas_call(kernel, in_specs=[whole(pltpu.SMEM)] + [whole()] * (len(op...  8.58 us
    ppermute x6, waiting for transfers between devices, per_device(): lax.ppermute(joined[c][-1], 'gx', [(i, i ^ 2 ** level) for i in range(gro...  7.87 us
    ppermute x12, waiting for transfers between devices, swap(): lax.ppermute(parts[d], 'gy', [(i, i ^ d) for i in range(groups_y)])  4.02 us
    pallas_call x2, Pallas kernels, y_backward(): pl.pallas_call(kernel, in_specs=[whole(pltpu.SMEM)] + [whole()] * (levels...  3.53 us
    pallas_call x2, Pallas kernels, y_forward(): pl.pallas_call(kernel, in_specs=[whole(pltpu.SMEM)] + [whole()] * (groups...  3.11 us
  transfers between devices with their start and end apart: 22, of which 7 were waited for; matrix products, arithmetic and copies ran while one was open for 0% of the time, Pallas kernels for 37%

profile of v3, /device:TPU:1, one launch (start us, length us, event | category | flops | bytes accessed | tf_op | source)
XLA Modules:
  0.0 79.7 jit_solution(4679565783644816836)
XLA Ops:
  0.7 0.9 %copy-done = f32[256,256]{1,0:T(8,128)S(1)} copy-done((f32[256,256]{1,0:T(8,128)S(1)}, f32[256,256]{1,0:T(8,128)}, u32[]{:S(2)}) %copy-start) | copy-done | bytes 262168
  1.7 1.6 %copy-done.3 = f32[32,64,256]{2,1,0:T(8,128)S(1)} copy-done((f32[32,64,256]{2,1,0:T(8,128)S(1)}, f32[32,64,256]{2,1,0:T(8,128)}, u32[]{:S(2)}) %copy-start.3) | copy-done | bytes 2097176
  3.3 1.3 %z_forward.2 = (f32[32,2048]{1,0:T(8,128)S(1)}, f32[32,2048]{1,0:T(8,128)S(1)}, f32[32,2048]{1,0:T(8,128)S(1)}, f32[32,2048]{1,0:T(8,128)S(1)}) custom-call(s32[2]{0:T(128)S(1)} %pad_add_fusion.me_ref, f32[2048,256]{1,0:T(8,128)S(1)} %bitcast.11, f32[256,256]{1,0:T(8,128)S(1)} %copy-done), custom_call_target="tpu_custom_call" | custom-call | tf_op jit(solution)/shard_map/z_forward/pallas_call | solution.py:112
  4.7 2.7 %collective-permute-start.4 = (f32[32,2048]{1,0:T(8,128)S(1)}, f32[32,2048]{1,0:T(8,128)S(1)}, u32[]{:S(2)}, u32[]{:S(2)}) collective-permute-start(f32[32,2048]{1,0:T(8,128)S(1)} %get-tuple-element.39), channel_id=1, source_target_pairs={{0,2},{1,3},{2,0},{3,1},{4,6},{5,7},{6,4},{7,5},{8,10},{9,11},{10,... | collective-permute-start | bytes 786440 | tf_op jit(solution)/shard_map/ppermute | solution.py:630
  8.2 1.7 %collective-permute-start.6 = (f32[9,16,128]{2,1,0:T(8,128)S(1)}, f32[9,16,128]{2,1,0:T(8,128)S(1)}, u32[]{:S(2)}, u32[]{:S(2)}) collective-permute-start(f32[9,16,128]{2,1,0:T(8,128)S(1)} %get-tuple-element.33.refs_0_.source_ref.own_ref.refs_6_), channel_id=1, source_target_pairs={{0,4},{4,8},{8,12},{12,16},{16,20},{20,24},{24,28},{28,0},{1,5},{5... | collective-permute-start | bytes 221192 | tf_op jit(solution)/shard_map/ppermute | solution.py:656
  9.9 3.1 %collective-permute-start.7 = (f32[9,16,128]{2,1,0:T(8,128)S(1)}, f32[9,16,128]{2,1,0:T(8,128)S(1)}, u32[]{:S(2)}, u32[]{:S(2)}) collective-permute-start(f32[9,16,128]{2,1,0:T(8,128)S(1)} %get-tuple-element.33.refs_0_.source_ref.own_ref.refs_6_), channel_id=1, source_target_pairs={{4,0},{8,4},{12,8},{16,12},{20,16},{24,20},{28,24},{0,28},{5,1},{9... | collective-permute-start | bytes 221192 | tf_op jit(solution)/shard_map/ppermute | solution.py:657
  13.0 1.4 %spread_rows.1.refs_8_.near = f32[2048,1152]{1,0:T(8,128)S(1)} custom-call(f32[9,16,128]{2,1,0:T(8,128)S(1)} %get-tuple-element.33.refs_0_.source_ref.own_ref.refs_6_), custom_call_target="tpu_custom_call" | custom-call | tf_op jit(solution)/shard_map/spread_rows/pallas_call | solution.py:479
  14.4 1.3 %z_forward.3 = (f32[32,2048]{1,0:T(8,128)S(1)}, f32[32,2048]{1,0:T(8,128)S(1)}, f32[32,2048]{1,0:T(8,128)S(1)}, f32[32,2048]{1,0:T(8,128)S(1)}) custom-call(s32[2]{0:T(128)S(1)} %pad_add_fusion.me_ref, f32[2048,256]{1,0:T(8,128)S(1)} %bitcast.12, f32[256,256]{1,0:T(8,128)S(1)} %copy-done.1, f32[9,16,128]{2,1,0:T(8,128)S(1)} %get-tuple-element.33.refs_0_.source_ref.own_ref.refs_6_), custom_call_target="tpu_custom_call" | custom-call | tf_op jit(solution)/shard_map/z_forward/pallas_call | solution.py:112
  16.3 1.4 %collective-permute-start.1 = (f32[32,2048]{1,0:T(8,128)S(1)}, f32[32,2048]{1,0:T(8,128)S(1)}, u32[]{:S(2)}, u32[]{:S(2)}) collective-permute-start(f32[32,2048]{1,0:T(8,128)S(1)} %get-tuple-element.36), channel_id=1, source_target_pairs={{0,2},{1,3},{2,0},{3,1},{4,6},{5,7},{6,4},{7,5},{8,10},{9,11},{10,... | collective-permute-start | bytes 786440 | tf_op jit(solution)/shard_map/ppermute | solution.py:630
  18.0 1.8 %collective-permute-done.5.refs_3_ = f32[32,2048]{1,0:T(8,128)S(1)} collective-permute-done((f32[32,2048]{1,0:T(8,128)S(1)}, f32[32,2048]{1,0:T(8,128)S(1)}, u32[]{:S(2)}, u32[]{:S(2)}) %collective-permute-start.5) | collective-permute-done | bytes 262176 | tf_op jit(solution)/shard_map/ppermute | solution.py:630
  19.9 1.6 %y_forward.2 = (f32[32,32,256]{2,1,0:T(8,128)S(1)}, f32[4,32,256]{2,1,0:T(8,128)S(1)}, f32[8,32,256]{2,1,0:T(8,128)S(1)}) custom-call(s32[2]{0:T(128)S(1)} %pad_add_fusion.me_ref, f32[32,2048]{1,0:T(8,128)S(1)} %get-tuple-element.32.after_ref.refs_0_, f32[32,2048]{1,0:T(8,128)S(1)} %collective-permute-done.3.refs_1_, ...), custom_call_target="tpu_custom_call" | custom-call | tf_op jit(solution)/shard_map/y_forward/pallas_call | solution.py:173
  21.4 1.7 %collective-permute-start.13 = (f32[4,32,256]{2,1,0:T(8,128)S(1)}, f32[4,32,256]{2,1,0:T(8,128)S(1)}, u32[]{:S(2)}, u32[]{:S(2)}) collective-permute-start(f32[4,32,256]{2,1,0:T(8,128)S(1)} %get-tuple-element.41.refs_6_.ends_ref), channel_id=1, source_target_pairs={{0,4},{4,0},{8,12},{12,8},{16,20},{20,16},{24,28},{28,24},{1,5},{5... | collective-permute-start | bytes 393224 | tf_op jit(solution)/shard_map/ppermute | solution.py:669
  23.1 3.7 %collective-permute-done.13.other_ref.refs_0_ = f32[4,32,256]{2,1,0:T(8,128)S(1)} collective-permute-done((f32[4,32,256]{2,1,0:T(8,128)S(1)}, f32[4,32,256]{2,1,0:T(8,128)S(1)}, u32[]{:S(2)}, u32[]{:S(2)}) %collective-permute-start.13) | collective-permute-done | bytes 131104 | tf_op jit(solution)/shard_map/ppermute | solution.py:669
  27.4 1.7 %collective-permute-start.14 = (f32[4,32,256]{2,1,0:T(8,128)S(1)}, f32[4,32,256]{2,1,0:T(8,128)S(1)}, u32[]{:S(2)}, u32[]{:S(2)}) collective-permute-start(f32[4,32,256]{2,1,0:T(8,128)S(1)} %join_ends.6.ends_ref), channel_id=1, source_target_pairs={{0,8},{4,12},{8,0},{12,4},{16,24},{20,28},{24,16},{28,20},{1,9},{5... | collective-permute-start | bytes 393224 | tf_op jit(solution)/shard_map/ppermute | solution.py:669
  29.1 1.7 %collective-permute-done.2.refs_3_ = f32[32,2048]{1,0:T(8,128)S(1)} collective-permute-done((f32[32,2048]{1,0:T(8,128)S(1)}, f32[32,2048]{1,0:T(8,128)S(1)}, u32[]{:S(2)}, u32[]{:S(2)}) %collective-permute-start.2) | collective-permute-done | bytes 262176 | tf_op jit(solution)/shard_map/ppermute | solution.py:630
  30.9 1.6 %y_forward.3 = (f32[32,32,256]{2,1,0:T(8,128)S(1)}, f32[4,32,256]{2,1,0:T(8,128)S(1)}, f32[8,32,256]{2,1,0:T(8,128)S(1)}) custom-call(s32[2]{0:T(128)S(1)} %pad_add_fusion.me_ref, f32[32,2048]{1,0:T(8,128)S(1)} %get-tuple-element.34.refs_0_, f32[32,2048]{1,0:T(8,128)S(1)} %collective-permute-done.refs_1_, f32[32,2048]{1,0:T(8,128)S(1)} %collective-permute-done.1.refs_2_, ...), custom_call_target="tpu_custom_call" | custom-call | tf_op jit(solution)/shard_map/y_forward/pallas_call | solution.py:173
  32.9 1.4 %collective-permute-start.12 = (f32[27,16,128]{2,1,0:T(8,128)S(1)}, f32[27,16,128]{2,1,0:T(8,128)S(1)}, u32[]{:S(2)}, u32[]{:S(2)}) collective-permute-start(f32[27,16,128]{2,1,0:T(8,128)S(1)} %join_rows.1.refs_0_), channel_id=1, source_target_pairs={{0,3},{1,2},{2,1},{3,0},{4,7},{5,6},{6,5},{7,4},{8,11},{9,10},{10,... | collective-permute-start | bytes 663560 | tf_op jit(solution)/shard_map/ppermute | solution.py:679
  34.4 1.2 %collective-permute-start.8 = (f32[4,32,256]{2,1,0:T(8,128)S(1)}, f32[4,32,256]{2,1,0:T(8,128)S(1)}, u32[]{:S(2)}, u32[]{:S(2)}) collective-permute-start(f32[4,32,256]{2,1,0:T(8,128)S(1)} %get-tuple-element.43.ends_ref.after_ref), channel_id=1, source_target_pairs={{0,4},{4,0},{8,12},{12,8},{16,20},{20,16},{24,28},{28,24},{1,5},{5... | collective-permute-start | bytes 393224 | tf_op jit(solution)/shard_map/ppermute | solution.py:669
  36.2 2.4 %collective-permute-start.15 = (f32[4,32,256]{2,1,0:T(8,128)S(1)}, f32[4,32,256]{2,1,0:T(8,128)S(1)}, u32[]{:S(2)}, u32[]{:S(2)}) collective-permute-start(f32[4,32,256]{2,1,0:T(8,128)S(1)} %join_ends.7), channel_id=1, source_target_pairs={{0,16},{4,20},{8,24},{12,28},{16,0},{20,4},{24,8},{28,12},{1,17},{... | collective-permute-start | bytes 393224 | tf_op jit(solution)/shard_map/ppermute | solution.py:669
  39.8 1.3 %collective-permute-start.9 = (f32[4,32,256]{2,1,0:T(8,128)S(1)}, f32[4,32,256]{2,1,0:T(8,128)S(1)}, u32[]{:S(2)}, u32[]{:S(2)}) collective-permute-start(f32[4,32,256]{2,1,0:T(8,128)S(1)} %join_ends.4.ends_ref), channel_id=1, source_target_pairs={{0,8},{4,12},{8,0},{12,4},{16,24},{20,28},{24,16},{28,20},{1,9},{5... | collective-permute-start | bytes 393224 | tf_op jit(solution)/shard_map/ppermute | solution.py:669
  41.9 2.6 %collective-permute-done.15.refs_2_ = f32[4,32,256]{2,1,0:T(8,128)S(1)} collective-permute-done((f32[4,32,256]{2,1,0:T(8,128)S(1)}, f32[4,32,256]{2,1,0:T(8,128)S(1)}, u32[]{:S(2)}, u32[]{:S(2)}) %collective-permute-start.15) | collective-permute-done | bytes 131104 | tf_op jit(solution)/shard_map/ppermute | solution.py:669
  44.5 1.8 %y_backward.2 = (f32[32,2048]{1,0:T(8,128)S(1)}, f32[32,2048]{1,0:T(8,128)S(1)}, f32[32,2048]{1,0:T(8,128)S(1)}, f32[32,2048]{1,0:T(8,128)S(1)}) custom-call(s32[2]{0:T(128)S(1)} %pad_add_fusion.me_ref, f32[32,32,256]{2,1,0:T(8,128)S(1)} %get-tuple-element.48.spec_ref, f32[4,32,256]{2,1,0:T(8,128)S(1)} %get-tuple-element.41.refs_6_.ends_ref, ...), custom_call_target="tpu_custom_call" | custom-call | tf_op jit(solution)/shard_map/y_backward/pallas_call | solution.py:296
  46.3 1.5 %collective-permute-start.19 = (f32[32,2048]{1,0:T(8,128)S(1)}, f32[32,2048]{1,0:T(8,128)S(1)}, u32[]{:S(2)}, u32[]{:S(2)}) collective-permute-start(f32[32,2048]{1,0:T(8,128)S(1)} %get-tuple-element.55), channel_id=1, source_target_pairs={{0,1},{1,0},{2,3},{3,2},{4,5},{5,4},{6,7},{7,6},{8,9},{9,8},{10,11... | collective-permute-start | bytes 786440 | tf_op jit(solution)/shard_map/ppermute | solution.py:630
  48.4 1.6 %collective-permute-start.10 = (f32[4,32,256]{2,1,0:T(8,128)S(1)}, f32[4,32,256]{2,1,0:T(8,128)S(1)}, u32[]{:S(2)}, u32[]{:S(2)}) collective-permute-start(f32[4,32,256]{2,1,0:T(8,128)S(1)} %join_ends.5), channel_id=1, source_target_pairs={{0,16},{4,20},{8,24},{12,28},{16,0},{20,4},{24,8},{28,12},{1,17},{... | collective-permute-start | bytes 393224 | tf_op jit(solution)/shard_map/ppermute | solution.py:669
  50.2 2.2 %collective-permute-start.21 = (f32[32,2048]{1,0:T(8,128)S(1)}, f32[32,2048]{1,0:T(8,128)S(1)}, u32[]{:S(2)}, u32[]{:S(2)}) collective-permute-start(f32[32,2048]{1,0:T(8,128)S(1)} %get-tuple-element.57), channel_id=1, source_target_pairs={{0,3},{1,2},{2,1},{3,0},{4,7},{5,6},{6,5},{7,4},{8,11},{9,10},{10,... | collective-permute-start | bytes 786440 | tf_op jit(solution)/shard_map/ppermute | solution.py:630
  52.4 4.0 %pair_pull.2.refs_5_ = f32[3,5,128]{2,1,0:T(8,128)S(1)} custom-call(s32[16,8]{1,0:T(8,128)S(1)} %get-tuple-element.45.pairs_ref, s32[8,256]{1,0:T(8,128)S(1)} %get-tuple-element.46.marks_ref, f32[2048,1152]{1,0:T(8,128)S(1)} %spread_rows.1.refs_8_.near, f32[1296,128]{1,0:T(8,128)S(1)} %get-tuple-element.47.refs_5_.far, f32[32,2048]{1,0:T(8,128)S(1)} %get-tuple-element.50.refs_0_), custom_call_target="tpu_custom_call" | custom-call | flops 1500000000 | tf_op jit(solution)/shard_map/pair_pull/pallas_call | solution.py:597
  57.3 1.8 %y_backward.3 = (f32[32,2048]{1,0:T(8,128)S(1)}, f32[32,2048]{1,0:T(8,128)S(1)}, f32[32,2048]{1,0:T(8,128)S(1)}, f32[32,2048]{1,0:T(8,128)S(1)}) custom-call(s32[2]{0:T(128)S(1)} %pad_add_fusion.me_ref, f32[32,32,256]{2,1,0:T(8,128)S(1)} %get-tuple-element.42.spec_ref, f32[4,32,256]{2,1,0:T(8,128)S(1)} %get-tuple-element.43.ends_ref.after_ref, ...), custom_call_target="tpu_custom_call" | custom-call | tf_op jit(solution)/shard_map/y_backward/pallas_call | solution.py:296
  59.0 0.9 %collective-permute-start.16 = (f32[32,2048]{1,0:T(8,128)S(1)}, f32[32,2048]{1,0:T(8,128)S(1)}, u32[]{:S(2)}, u32[]{:S(2)}) collective-permute-start(f32[32,2048]{1,0:T(8,128)S(1)} %get-tuple-element.52), channel_id=1, source_target_pairs={{0,1},{1,0},{2,3},{3,2},{4,5},{5,4},{6,7},{7,6},{8,9},{9,8},{10,11... | collective-permute-start | bytes 786440 | tf_op jit(solution)/shard_map/ppermute | solution.py:630
  60.2 1.5 %collective-permute-start.18 = (f32[32,2048]{1,0:T(8,128)S(1)}, f32[32,2048]{1,0:T(8,128)S(1)}, u32[]{:S(2)}, u32[]{:S(2)}) collective-permute-start(f32[32,2048]{1,0:T(8,128)S(1)} %get-tuple-element.54), channel_id=1, source_target_pairs={{0,3},{1,2},{2,1},{3,0},{4,7},{5,6},{6,5},{7,4},{8,11},{9,10},{10,... | collective-permute-start | bytes 786440 | tf_op jit(solution)/shard_map/ppermute | solution.py:630
  61.6 8.8 %pair_pull.3.refs_7_.refs_10_ = f32[3,11,128]{2,1,0:T(8,128)S(1)} custom-call(s32[16,8]{1,0:T(8,128)S(1)} %get-tuple-element.45.pairs_ref, s32[8,256]{1,0:T(8,128)S(1)} %get-tuple-element.46.marks_ref, f32[2048,1152]{1,0:T(8,128)S(1)} %spread_rows.1.refs_8_.near, f32[1296,128]{1,0:T(8,128)S(1)} %get-tuple-element.47.refs_5_.far, ...), custom_call_target="tpu_custom_call" | custom-call | tf_op jit(solution)/shard_map/pair_pull/pallas_call | solution.py:597
  70.5 3.9 %z_backward.2 = (f32[2048,256]{1,0:T(8,128)S(1)}, f32[16,128]{1,0:T(8,128)S(1)}) custom-call(s32[2]{0:T(128)S(1)} %pad_add_fusion.me_ref, f32[32,2048]{1,0:T(8,128)S(1)} %get-tuple-element.50.refs_0_, f32[32,2048]{1,0:T(8,128)S(1)} %collective-permute-done.19.refs_1_, f32[32,2048]{1,0:T(8,128)S(1)} %collective-permute-done.20.refs_2_, ...), custom_call_target="tpu_custom_call" | custom-call | tf_op jit(solution)/shard_map/z_backward/pallas_call | solution.py:427
  74.8 4.7 %z_backward.3 = (f32[2048,256]{1,0:T(8,128)}, f32[3,16,128]{2,1,0:T(8,128)}) custom-call(s32[2]{0:T(128)S(1)} %pad_add_fusion.me_ref, f32[32,2048]{1,0:T(8,128)S(1)} %get-tuple-element.51.refs_0_, f32[32,2048]{1,0:T(8,128)S(1)} %collective-permute-done.16.refs_1_, f32[32,2048]{1,0:T(8,128)S(1)} %collective-permute-done.17.refs_2_, ...), custom_call_target="tpu_custom_call" | custom-call | tf_op jit(solution)/shard_map/z_backward/pallas_call | solution.py:427
  (53 shorter events, 7.9 us)
Async XLA Ops:
  0.6 6.9 %copy-start.9 = (s32[1,1,16,8]{2,3,1,0:T(8,128)S(1)}, s32[1,1,16,8]{2,3,1,0:T(8,128)}, u32[]{:S(2)}) copy-start(s32[1,1,16,8]{2,3,1,0:T(8,128)} %param.13) | copy-start | bytes 1540
  0.6 6.9 %copy-start.8 = (s32[1,1,16]{2,1,0:T(1,128)S(1)}, s32[1,1,16]{2,1,0:T(1,128)}, u32[]{:S(2)}) copy-start(s32[1,1,16]{2,1,0:T(1,128)} %param.12) | copy-start | bytes 196
  0.7 6.9 %copy-start.5 = (s32[1,1,2048]{2,1,0:T(1,128)S(1)}, s32[1,1,2048]{2,1,0:T(1,128)}, u32[]{:S(2)}) copy-start(s32[1,1,2048]{2,1,0:T(1,128)} %param.11) | copy-start | bytes 24580
  0.7 1.0 %copy-start = (f32[256,256]{1,0:T(8,128)S(1)}, f32[256,256]{1,0:T(8,128)}, u32[]{:S(2)}) copy-start(f32[256,256]{1,0:T(8,128)} %constant.13.clone.table_ref.refs_4_.refs_3_) | copy-start | bytes 786436
  1.7 1.6 %copy-start.3 = (f32[32,64,256]{2,1,0:T(8,128)S(1)}, f32[32,64,256]{2,1,0:T(8,128)}, u32[]{:S(2)}) copy-start(f32[32,64,256]{2,1,0:T(8,128)} %param.8) | copy-start | bytes 6291460
  3.3 4.3 %copy-start.6 = (f32[6,1,1,2048]{3,2,1,0:T(1,128)S(1)}, f32[6,1,1,2048]{3,2,1,0:T(1,128)}, u32[]{:S(2)}) copy-start(f32[6,1,1,2048]{3,2,1,0:T(1,128)} %param.9) | copy-start | bytes 147460
  3.3 4.3 %copy-start.7 = (f32[3,1,1,2048]{3,2,1,0:T(1,128)S(1)}, f32[3,1,1,2048]{3,2,1,0:T(1,128)}, u32[]{:S(2)}) copy-start(f32[3,1,1,2048]{3,2,1,0:T(1,128)} %param.10) | copy-start | bytes 73732
  4.6 13.1 %collective-permute-start.3 = (f32[32,2048]{1,0:T(8,128)S(1)}, f32[32,2048]{1,0:T(8,128)S(1)}, u32[]{:S(2)}, u32[]{:S(2)}) collective-permute-start(f32[32,2048]{1,0:T(8,128)S(1)} %get-tuple-element.38), channel_id=1, source_target_pairs={{0,1},{1,0},{2,3},{3,2},{4,5},{5,4},{6,7},{7,6},{8,9},{9,8},{10,11... | collective-permute-start | bytes 786440 | tf_op jit(solution)/shard_map/ppermute | solution.py:630
  4.7 13.3 %collective-permute-start.4 = (f32[32,2048]{1,0:T(8,128)S(1)}, f32[32,2048]{1,0:T(8,128)S(1)}, u32[]{:S(2)}, u32[]{:S(2)}) collective-permute-start(f32[32,2048]{1,0:T(8,128)S(1)} %get-tuple-element.39), channel_id=1, source_target_pairs={{0,2},{1,3},{2,0},{3,1},{4,6},{5,7},{6,4},{7,5},{8,10},{9,11},{10,... | collective-permute-start | bytes 786440 | tf_op jit(solution)/shard_map/ppermute | solution.py:630
  7.4 12.4 %collective-permute-start.5 = (f32[32,2048]{1,0:T(8,128)S(1)}, f32[32,2048]{1,0:T(8,128)S(1)}, u32[]{:S(2)}, u32[]{:S(2)}) collective-permute-start(f32[32,2048]{1,0:T(8,128)S(1)} %get-tuple-element.40), channel_id=1, source_target_pairs={{0,3},{1,2},{2,1},{3,0},{4,7},{5,6},{6,5},{7,4},{8,11},{9,10},{10,... | collective-permute-start | bytes 786440 | tf_op jit(solution)/shard_map/ppermute | solution.py:630
  8.2 6.2 %copy-start.1 = (f32[256,256]{1,0:T(8,128)S(1)}, f32[256,256]{1,0:T(8,128)}, u32[]{:S(2)}) copy-start(f32[256,256]{1,0:T(8,128)} %constant.13.clone.table_ref.refs_4_.refs_3_) | copy-start | bytes 786436
  8.2 6.2 %copy-start.4 = (f32[32,64,256]{2,1,0:T(8,128)S(1)}, f32[32,64,256]{2,1,0:T(8,128)}, u32[]{:S(2)}) copy-start(f32[32,64,256]{2,1,0:T(8,128)} %param.8) | copy-start | bytes 6291460
  8.2 7.6 %collective-permute-start.6 = (f32[9,16,128]{2,1,0:T(8,128)S(1)}, f32[9,16,128]{2,1,0:T(8,128)S(1)}, u32[]{:S(2)}, u32[]{:S(2)}) collective-permute-start(f32[9,16,128]{2,1,0:T(8,128)S(1)} %get-tuple-element.33.refs_0_.source_ref.own_ref.refs_6_), channel_id=1, source_target_pairs={{0,4},{4,8},{8,12},{12,16},{16,20},{20,24},{24,28},{28,0},{1,5},{5... | collective-permute-start | bytes 221192 | tf_op jit(solution)/shard_map/ppermute | solution.py:656
  9.9 6.4 %collective-permute-start.7 = (f32[9,16,128]{2,1,0:T(8,128)S(1)}, f32[9,16,128]{2,1,0:T(8,128)S(1)}, u32[]{:S(2)}, u32[]{:S(2)}) collective-permute-start(f32[9,16,128]{2,1,0:T(8,128)S(1)} %get-tuple-element.33.refs_0_.source_ref.own_ref.refs_6_), channel_id=1, source_target_pairs={{4,0},{8,4},{12,8},{16,12},{20,16},{24,20},{28,24},{0,28},{5,1},{9... | collective-permute-start | bytes 221192 | tf_op jit(solution)/shard_map/ppermute | solution.py:657
  14.4 5.4 %copy-start.2 = (f32[8,256,256]{2,1,0:T(8,128)S(1)}, f32[8,256,256]{2,1,0:T(8,128)}, u32[]{:S(2)}) copy-start(f32[8,256,256]{2,1,0:T(8,128)} %constant.14.clone.refs_5_) | copy-start | bytes 6291460
  15.8 13.4 %collective-permute-start = (f32[32,2048]{1,0:T(8,128)S(1)}, f32[32,2048]{1,0:T(8,128)S(1)}, u32[]{:S(2)}, u32[]{:S(2)}) collective-permute-start(f32[32,2048]{1,0:T(8,128)S(1)} %get-tuple-element.35), channel_id=1, source_target_pairs={{0,1},{1,0},{2,3},{3,2},{4,5},{5,4},{6,7},{7,6},{8,9},{9,8},{10,11... | collective-permute-start | bytes 786440 | tf_op jit(solution)/shard_map/ppermute | solution.py:630
  16.3 12.8 %collective-permute-start.1 = (f32[32,2048]{1,0:T(8,128)S(1)}, f32[32,2048]{1,0:T(8,128)S(1)}, u32[]{:S(2)}, u32[]{:S(2)}) collective-permute-start(f32[32,2048]{1,0:T(8,128)S(1)} %get-tuple-element.36), channel_id=1, source_target_pairs={{0,2},{1,3},{2,0},{3,1},{4,6},{5,7},{6,4},{7,5},{8,10},{9,11},{10,... | collective-permute-start | bytes 786440 | tf_op jit(solution)/shard_map/ppermute | solution.py:630
  17.7 13.2 %collective-permute-start.2 = (f32[32,2048]{1,0:T(8,128)S(1)}, f32[32,2048]{1,0:T(8,128)S(1)}, u32[]{:S(2)}, u32[]{:S(2)}) collective-permute-start(f32[32,2048]{1,0:T(8,128)S(1)} %get-tuple-element.37), channel_id=1, source_target_pairs={{0,3},{1,2},{2,1},{3,0},{4,7},{5,6},{6,5},{7,4},{8,11},{9,10},{10,... | collective-permute-start | bytes 786440 | tf_op jit(solution)/shard_map/ppermute | solution.py:630
  21.4 5.4 %collective-permute-start.13 = (f32[4,32,256]{2,1,0:T(8,128)S(1)}, f32[4,32,256]{2,1,0:T(8,128)S(1)}, u32[]{:S(2)}, u32[]{:S(2)}) collective-permute-start(f32[4,32,256]{2,1,0:T(8,128)S(1)} %get-tuple-element.41.refs_6_.ends_ref), channel_id=1, source_target_pairs={{0,4},{4,0},{8,12},{12,8},{16,20},{20,16},{24,28},{28,24},{1,5},{5... | collective-permute-start | bytes 393224 | tf_op jit(solution)/shard_map/ppermute | solution.py:669
  27.4 8.2 %collective-permute-start.14 = (f32[4,32,256]{2,1,0:T(8,128)S(1)}, f32[4,32,256]{2,1,0:T(8,128)S(1)}, u32[]{:S(2)}, u32[]{:S(2)}) collective-permute-start(f32[4,32,256]{2,1,0:T(8,128)S(1)} %join_ends.6.ends_ref), channel_id=1, source_target_pairs={{0,8},{4,12},{8,0},{12,4},{16,24},{20,28},{24,16},{28,20},{1,9},{5... | collective-permute-start | bytes 393224 | tf_op jit(solution)/shard_map/ppermute | solution.py:669
  32.5 8.7 %collective-permute-start.11 = (f32[27,16,128]{2,1,0:T(8,128)S(1)}, f32[27,16,128]{2,1,0:T(8,128)S(1)}, u32[]{:S(2)}, u32[]{:S(2)}) collective-permute-start(f32[27,16,128]{2,1,0:T(8,128)S(1)} %join_rows.1.refs_0_), channel_id=1, source_target_pairs={{0,1},{1,0},{2,3},{3,2},{4,5},{5,4},{6,7},{7,6},{8,9},{9,8},{10,11... | collective-permute-start | bytes 663560 | tf_op jit(solution)/shard_map/ppermute | solution.py:678
  32.9 8.2 %collective-permute-start.12 = (f32[27,16,128]{2,1,0:T(8,128)S(1)}, f32[27,16,128]{2,1,0:T(8,128)S(1)}, u32[]{:S(2)}, u32[]{:S(2)}) collective-permute-start(f32[27,16,128]{2,1,0:T(8,128)S(1)} %join_rows.1.refs_0_), channel_id=1, source_target_pairs={{0,3},{1,2},{2,1},{3,0},{4,7},{5,6},{6,5},{7,4},{8,11},{9,10},{10,... | collective-permute-start | bytes 663560 | tf_op jit(solution)/shard_map/ppermute | solution.py:679
  34.4 4.9 %collective-permute-start.8 = (f32[4,32,256]{2,1,0:T(8,128)S(1)}, f32[4,32,256]{2,1,0:T(8,128)S(1)}, u32[]{:S(2)}, u32[]{:S(2)}) collective-permute-start(f32[4,32,256]{2,1,0:T(8,128)S(1)} %get-tuple-element.43.ends_ref.after_ref), channel_id=1, source_target_pairs={{0,4},{4,0},{8,12},{12,8},{16,20},{20,16},{24,28},{28,24},{1,5},{5... | collective-permute-start | bytes 393224 | tf_op jit(solution)/shard_map/ppermute | solution.py:669
  36.2 8.3 %collective-permute-start.15 = (f32[4,32,256]{2,1,0:T(8,128)S(1)}, f32[4,32,256]{2,1,0:T(8,128)S(1)}, u32[]{:S(2)}, u32[]{:S(2)}) collective-permute-start(f32[4,32,256]{2,1,0:T(8,128)S(1)} %join_ends.7), channel_id=1, source_target_pairs={{0,16},{4,20},{8,24},{12,28},{16,0},{20,4},{24,8},{28,12},{1,17},{... | collective-permute-start | bytes 393224 | tf_op jit(solution)/shard_map/ppermute | solution.py:669
  39.8 8.0 %collective-permute-start.9 = (f32[4,32,256]{2,1,0:T(8,128)S(1)}, f32[4,32,256]{2,1,0:T(8,128)S(1)}, u32[]{:S(2)}, u32[]{:S(2)}) collective-permute-start(f32[4,32,256]{2,1,0:T(8,128)S(1)} %join_ends.4.ends_ref), channel_id=1, source_target_pairs={{0,8},{4,12},{8,0},{12,4},{16,24},{20,28},{24,16},{28,20},{1,9},{5... | collective-permute-start | bytes 393224 | tf_op jit(solution)/shard_map/ppermute | solution.py:669
  46.3 13.9 %collective-permute-start.19 = (f32[32,2048]{1,0:T(8,128)S(1)}, f32[32,2048]{1,0:T(8,128)S(1)}, u32[]{:S(2)}, u32[]{:S(2)}) collective-permute-start(f32[32,2048]{1,0:T(8,128)S(1)} %get-tuple-element.55), channel_id=1, source_target_pairs={{0,1},{1,0},{2,3},{3,2},{4,5},{5,4},{6,7},{7,6},{8,9},{9,8},{10,11... | collective-permute-start | bytes 786440 | tf_op jit(solution)/shard_map/ppermute | solution.py:630
  48.4 8.9 %collective-permute-start.10 = (f32[4,32,256]{2,1,0:T(8,128)S(1)}, f32[4,32,256]{2,1,0:T(8,128)S(1)}, u32[]{:S(2)}, u32[]{:S(2)}) collective-permute-start(f32[4,32,256]{2,1,0:T(8,128)S(1)} %join_ends.5), channel_id=1, source_target_pairs={{0,16},{4,20},{8,24},{12,28},{16,0},{20,4},{24,8},{28,12},{1,17},{... | collective-permute-start | bytes 393224 | tf_op jit(solution)/shard_map/ppermute | solution.py:669
  49.9 20.5 %collective-permute-start.20 = (f32[32,2048]{1,0:T(8,128)S(1)}, f32[32,2048]{1,0:T(8,128)S(1)}, u32[]{:S(2)}, u32[]{:S(2)}) collective-permute-start(f32[32,2048]{1,0:T(8,128)S(1)} %get-tuple-element.56), channel_id=1, source_target_pairs={{0,2},{1,3},{2,0},{3,1},{4,6},{5,7},{6,4},{7,5},{8,10},{9,11},{10,... | collective-permute-start | bytes 786440 | tf_op jit(solution)/shard_map/ppermute | solution.py:630
  50.2 20.3 %collective-permute-start.21 = (f32[32,2048]{1,0:T(8,128)S(1)}, f32[32,2048]{1,0:T(8,128)S(1)}, u32[]{:S(2)}, u32[]{:S(2)}) collective-permute-start(f32[32,2048]{1,0:T(8,128)S(1)} %get-tuple-element.57), channel_id=1, source_target_pairs={{0,3},{1,2},{2,1},{3,0},{4,7},{5,6},{6,5},{7,4},{8,11},{9,10},{10,... | collective-permute-start | bytes 786440 | tf_op jit(solution)/shard_map/ppermute | solution.py:630
  59.0 15.3 %collective-permute-start.16 = (f32[32,2048]{1,0:T(8,128)S(1)}, f32[32,2048]{1,0:T(8,128)S(1)}, u32[]{:S(2)}, u32[]{:S(2)}) collective-permute-start(f32[32,2048]{1,0:T(8,128)S(1)} %get-tuple-element.52), channel_id=1, source_target_pairs={{0,1},{1,0},{2,3},{3,2},{4,5},{5,4},{6,7},{7,6},{8,9},{9,8},{10,11... | collective-permute-start | bytes 786440 | tf_op jit(solution)/shard_map/ppermute | solution.py:630
  59.9 14.5 %collective-permute-start.17 = (f32[32,2048]{1,0:T(8,128)S(1)}, f32[32,2048]{1,0:T(8,128)S(1)}, u32[]{:S(2)}, u32[]{:S(2)}) collective-permute-start(f32[32,2048]{1,0:T(8,128)S(1)} %get-tuple-element.53), channel_id=1, source_target_pairs={{0,2},{1,3},{2,0},{3,1},{4,6},{5,7},{6,4},{7,5},{8,10},{9,11},{10,... | collective-permute-start | bytes 786440 | tf_op jit(solution)/shard_map/ppermute | solution.py:630
  60.2 14.7 %collective-permute-start.18 = (f32[32,2048]{1,0:T(8,128)S(1)}, f32[32,2048]{1,0:T(8,128)S(1)}, u32[]{:S(2)}, u32[]{:S(2)}) collective-permute-start(f32[32,2048]{1,0:T(8,128)S(1)} %get-tuple-element.54), channel_id=1, source_target_pairs={{0,3},{1,2},{2,1},{3,0},{4,7},{5,6},{6,5},{7,4},{8,11},{9,10},{10,... | collective-permute-start | bytes 786440 | tf_op jit(solution)/shard_map/ppermute | solution.py:630

commit v4 on v3

--- a/solution.py
+++ b/solution.py
@@ -15,7 +15,7 @@
 SHARES = (5, 11)
 ORDER = ()
 VMEM_LIMIT = 24 * 1024 * 1024
-COSTS = {'join_ends': (0.0, 3.0, 0.0, 0.0), 'pair_pull': (1.5, 0.0)}
+COSTS = {'join_ends': (0, 3.0, 0, 2.0), 'pair_pull': (1.5, 0.0)}
 
 
 def counted(cost):
@@ -340,7 +340,37 @@
     )(counts, me, vectors, offsets, cells, pairs, after)
 
 
-def z_backward(parts, table, cells, me, groups, offset, rows, before, pull, source, after, cost):
+def sample_factors(cells, table, me, groups, offsets, sizes, cost):
+    length = table.shape[0]
+    per = length // groups
+    seg_total = cells.shape[1]
+
+    def kernel(me_ref, table_ref, cells_ref, *outs):
+        own = me_ref[0]
+        level = cells_ref[...] % length
+        hot_z = jnp.where(
+            lax.broadcasted_iota(jnp.int32, (length, seg_total), 0) == level, 1.0, 0.0
+        ).astype(jnp.bfloat16)
+        for out, offset, rows in zip(outs, offsets, sizes):
+            picked = [
+                table_ref[pl.ds(pl.multiple_of((own ^ d) * per + offset, 8), rows), :] for d in range(groups)
+            ]
+            right = jnp.concatenate(halves(jnp.concatenate(picked, axis=0)), axis=0)
+            factor = jnp.dot(right, hot_z, preferred_element_type=jnp.float32)
+            out[...] = factor[: groups * rows] + factor[groups * rows :]
+
+    return pl.pallas_call(
+        kernel,
+        in_specs=[whole(pltpu.SMEM)] + [whole()] * 2,
+        out_specs=[whole()] * len(sizes),
+        out_shape=[jax.ShapeDtypeStruct((groups * rows, seg_total), jnp.float32) for rows in sizes],
+        compiler_params=params(),
+        cost_estimate=counted(cost),
+        name="sample_factors",
+    )(me, table, cells)
+
+
+def z_backward(parts, table, cells, factor, me, groups, offset, rows, before, pull, source, after, cost):
     cell_total = parts[0].shape[1]
     length = table.shape[0]
     per = length // groups
@@ -354,7 +384,7 @@
 
     def kernel(me_ref, *refs):
         part_refs, refs = refs[:groups], refs[groups:]
-        table_ref, cells_ref, source_ref, refs = refs[0], refs[1], refs[2], refs[3:]
+        table_ref, cells_ref, factor_ref, source_ref, refs = refs[0], refs[1], refs[2], refs[3], refs[4:]
         if adds:
             old_ref, old_tau_ref, refs = refs[0], refs[1], refs[2:]
         if last:
@@ -388,7 +418,6 @@
                 )
                 writes[-1].start()
         place = cells_ref[...] // length
-        level = cells_ref[...] % length
         lane_tile = min(512, seg_total)
         taus = []
         for k in range(0, seg_total, lane_tile):
@@ -397,13 +426,7 @@
                 lax.broadcasted_iota(jnp.int32, (cell_total, lane_tile), 0) == place[:, at], 1.0, 0.0
             ).astype(jnp.bfloat16)
             found = jnp.dot(both, hot, preferred_element_type=jnp.float32)
-            hot_z = jnp.where(
-                lax.broadcasted_iota(jnp.int32, (length, lane_tile), 0) == level[:, at], 1.0, 0.0
-            ).astype(jnp.bfloat16)
-            factor = jnp.dot(jnp.concatenate(right, axis=0), hot_z, preferred_element_type=jnp.float32)
-            tau = jnp.sum(
-                (found[:depth] + found[depth:]) * (factor[:depth] + factor[depth:]), axis=0, keepdims=True
-            )
+            tau = jnp.sum((found[:depth] + found[depth:]) * factor_ref[:, at], axis=0, keepdims=True)
             taus += [tau[:, j : j + width] for j in range(0, lane_tile, width)]
         tau = jnp.concatenate(taus, axis=0)
         if adds:
@@ -418,7 +441,7 @@
         for write in writes:
             write.wait()
 
-    operands = [me, *parts, table, cells, source]
+    operands = [me, *parts, table, cells, factor, source]
     if adds:
         operands += list(before)
     if last:
@@ -657,11 +680,13 @@
     high = lax.ppermute(source, "gx", [((i + 1) % groups_x, i) for i in range(groups_x)])
 
     near = spread_rows(source, [sent[-1][0]] if "near" in ORDER else [], hint("spread_rows", 0))
+    flat_cells = seg_cell.reshape(1, seg_total)
+    factors = sample_factors(flat_cells, table, me, groups_y, offsets, sizes, 0.0)
 
     levels = groups_x.bit_length() - 1
     forward, others, joined = [], [], []
     for c in range(chunks):
-        after = [low, high, near] if c == 0 else [joined[0][-1] if "yf1" in ORDER else forward[-1][1]]
+        after = [low, high, near, factors[0]] if c == 0 else [joined[0][-1] if "yf1" in ORDER else forward[-1][1]]
         forward.append(y_forward(arrived[c], table, lines, me, offsets[c], sizes[c], plane_x, plane_y, after, hint("y_forward", c)))
         others.append([])
         joined.append([forward[c][1]])
@@ -693,10 +718,9 @@
 
     pull = pulls[0] if len(pulls) == 1 else jnp.concatenate(pulls, axis=1)
     before = None
-    flat_cells = seg_cell.reshape(1, seg_total)
     for c in range(chunks):
         before = z_backward(
-            landed[c], table, flat_cells, me, groups_y, offsets[c], sizes[c], before,
+            landed[c], table, flat_cells, factors[c], me, groups_y, offsets[c], sizes[c], before,
             pull if c == chunks - 1 else None, source, pulls[-1:], hint("z_backward", c),
         )
     stress, force = before

time: 79.9 us -> 79.7 us (level)
    pallas_call x0 -> x1, Pallas kernels: none -> 1.32 us  [sample_factors(): pl.pallas_call(kernel, in_specs=[whole(pltpu.SMEM)] + [whole()] * 2, out_...]
    pallas_call x2, Pallas kernels: 12.8 us -> 11.6 us  [pair_pull(): pl.pallas_call(kernel, in_specs=[whole(pltpu.SMEM)] * 2 + [whole()] * 2 +...]
    ppermute x6, starting transfers between devices: 9.9 us -> 8.77 us  [per_device(): lax.ppermute(joined[c][-1], 'gx', [(i, i ^ 2 ** level) for i in range(gro...]
where the time goes in v4:
time: 79.7 us; the launch traced here: 79.5 us
  Pallas kernels  35.5 us (45%)
  starting transfers between devices  27.6 us (35%)
  waiting for transfers between devices  12.6 us (16%)
  local copies, waits for them, and re-layouts  2.65 us (3%)
  between operations  1.05 us (1%)
    ppermute x12, starting transfers between devices, swap(): lax.ppermute(parts[d], 'gy', [(i, i ^ d) for i in range(groups_y)])  12.3 us
    pallas_call x2, Pallas kernels, pair_pull(): pl.pallas_call(kernel, in_specs=[whole(pltpu.SMEM)] * 2 + [whole()] * 2 +...  11.6 us
    ppermute x6, starting transfers between devices, per_device(): lax.ppermute(joined[c][-1], 'gx', [(i, i ^ 2 ** level) for i in range(gro...  8.77 us
    ppermute x6, waiting for transfers between devices, per_device(): lax.ppermute(joined[c][-1], 'gx', [(i, i ^ 2 ** level) for i in range(gro...  8.08 us
    pallas_call x2, Pallas kernels, z_backward(): pl.pallas_call(kernel, in_specs=[whole(pltpu.SMEM)] + [whole()] * (len(op...  8.04 us
    ppermute x12, waiting for transfers between devices, swap(): lax.ppermute(parts[d], 'gy', [(i, i ^ d) for i in range(groups_y)])  4.53 us
    pallas_call x2, Pallas kernels, y_backward(): pl.pallas_call(kernel, in_specs=[whole(pltpu.SMEM)] + [whole()] * (levels...  3.53 us
    pallas_call x2, Pallas kernels, y_forward(): pl.pallas_call(kernel, in_specs=[whole(pltpu.SMEM)] + [whole()] * (groups...  3.31 us
  transfers between devices with their start and end apart: 22, of which 7 were waited for; matrix products, arithmetic and copies ran while one was open for 0% of the time, Pallas kernels for 37%

profile of v4, /device:TPU:1, one launch (start us, length us, event | category | flops | bytes accessed | tf_op | source)
XLA Modules:
  0.0 79.5 jit_solution(582191571757846484)
XLA Ops:
  0.7 0.9 %copy-done = f32[256,256]{1,0:T(8,128)S(1)} copy-done((f32[256,256]{1,0:T(8,128)S(1)}, f32[256,256]{1,0:T(8,128)}, u32[]{:S(2)}) %copy-start) | copy-done | bytes 262168
  1.7 1.6 %copy-done.2 = f32[32,64,256]{2,1,0:T(8,128)S(1)} copy-done((f32[32,64,256]{2,1,0:T(8,128)S(1)}, f32[32,64,256]{2,1,0:T(8,128)}, u32[]{:S(2)}) %copy-start.2) | copy-done | bytes 2097176
  3.3 1.3 %z_forward.2 = (f32[32,2048]{1,0:T(8,128)S(1)}, f32[32,2048]{1,0:T(8,128)S(1)}, f32[32,2048]{1,0:T(8,128)S(1)}, f32[32,2048]{1,0:T(8,128)S(1)}) custom-call(s32[2]{0:T(128)S(1)} %pad_add_fusion.me_ref, f32[2048,256]{1,0:T(8,128)S(1)} %bitcast.11, f32[256,256]{1,0:T(8,128)S(1)} %copy-done), custom_call_target="tpu_custom_call" | custom-call | tf_op jit(solution)/shard_map/z_forward/pallas_call | solution.py:112
  4.7 2.7 %collective-permute-start.4 = (f32[32,2048]{1,0:T(8,128)S(1)}, f32[32,2048]{1,0:T(8,128)S(1)}, u32[]{:S(2)}, u32[]{:S(2)}) collective-permute-start(f32[32,2048]{1,0:T(8,128)S(1)} %get-tuple-element.41), channel_id=1, source_target_pairs={{0,2},{1,3},{2,0},{3,1},{4,6},{5,7},{6,4},{7,5},{8,10},{9,11},{10,... | collective-permute-start | bytes 786440 | tf_op jit(solution)/shard_map/ppermute | solution.py:653
  8.2 1.7 %collective-permute-start.6 = (f32[9,16,128]{2,1,0:T(8,128)S(1)}, f32[9,16,128]{2,1,0:T(8,128)S(1)}, u32[]{:S(2)}, u32[]{:S(2)}) collective-permute-start(f32[9,16,128]{2,1,0:T(8,128)S(1)} %get-tuple-element.35.refs_0_.source_ref.own_ref.refs_7_), channel_id=1, source_target_pairs={{0,4},{4,8},{8,12},{12,16},{16,20},{20,24},{24,28},{28,0},{1,5},{5... | collective-permute-start | bytes 221192 | tf_op jit(solution)/shard_map/ppermute | solution.py:679
  9.9 3.1 %collective-permute-start.7 = (f32[9,16,128]{2,1,0:T(8,128)S(1)}, f32[9,16,128]{2,1,0:T(8,128)S(1)}, u32[]{:S(2)}, u32[]{:S(2)}) collective-permute-start(f32[9,16,128]{2,1,0:T(8,128)S(1)} %get-tuple-element.35.refs_0_.source_ref.own_ref.refs_7_), channel_id=1, source_target_pairs={{4,0},{8,4},{12,8},{16,12},{20,16},{24,20},{28,24},{0,28},{5,1},{9... | collective-permute-start | bytes 221192 | tf_op jit(solution)/shard_map/ppermute | solution.py:680
  13.0 1.4 %spread_rows.1.refs_8_.near = f32[2048,1152]{1,0:T(8,128)S(1)} custom-call(f32[9,16,128]{2,1,0:T(8,128)S(1)} %get-tuple-element.35.refs_0_.source_ref.own_ref.refs_7_), custom_call_target="tpu_custom_call" | custom-call | tf_op jit(solution)/shard_map/spread_rows/pallas_call | solution.py:502
  14.4 1.3 %z_forward.3 = (f32[32,2048]{1,0:T(8,128)S(1)}, f32[32,2048]{1,0:T(8,128)S(1)}, f32[32,2048]{1,0:T(8,128)S(1)}, f32[32,2048]{1,0:T(8,128)S(1)}) custom-call(s32[2]{0:T(128)S(1)} %pad_add_fusion.me_ref, f32[2048,256]{1,0:T(8,128)S(1)} %bitcast.12, f32[256,256]{1,0:T(8,128)S(1)} %copy-done.1, f32[9,16,128]{2,1,0:T(8,128)S(1)} %get-tuple-element.35.refs_0_.source_ref.own_ref.refs_7_), custom_call_target="tpu_custom_call" | custom-call | tf_op jit(solution)/shard_map/z_forward/pallas_call | solution.py:112
  15.8 1.3 %sample_factors.1 = (f32[128,2048]{1,0:T(8,128)S(1)}, f32[128,2048]{1,0:T(8,128)S(1)}) custom-call(s32[2]{0:T(128)S(1)} %pad_add_fusion.me_ref, f32[256,256]{1,0:T(8,128)S(1)} %copy-done.1, s32[1,2048]{1,0:T(1,128)S(1)} %bitcast.14), custom_call_target="tpu_custom_call" | custom-call | tf_op jit(solution)/shard_map/sample_factors/pallas_call | solution.py:362
  17.6 1.4 %collective-permute-start.1 = (f32[32,2048]{1,0:T(8,128)S(1)}, f32[32,2048]{1,0:T(8,128)S(1)}, u32[]{:S(2)}, u32[]{:S(2)}) collective-permute-start(f32[32,2048]{1,0:T(8,128)S(1)} %get-tuple-element.38), channel_id=1, source_target_pairs={{0,2},{1,3},{2,0},{3,1},{4,6},{5,7},{6,4},{7,5},{8,10},{9,11},{10,... | collective-permute-start | bytes 786440 | tf_op jit(solution)/shard_map/ppermute | solution.py:653
  19.6 1.7 %y_forward.2 = (f32[32,32,256]{2,1,0:T(8,128)S(1)}, f32[4,32,256]{2,1,0:T(8,128)S(1)}, f32[8,32,256]{2,1,0:T(8,128)S(1)}) custom-call(s32[2]{0:T(128)S(1)} %pad_add_fusion.me_ref, f32[32,2048]{1,0:T(8,128)S(1)} %get-tuple-element.34.after_ref.refs_0_, f32[32,2048]{1,0:T(8,128)S(1)} %collective-permute-done.3.refs_1_, ...), custom_call_target="tpu_custom_call" | custom-call | tf_op jit(solution)/shard_map/y_forward/pallas_call | solution.py:173
  21.4 1.9 %collective-permute-start.13 = (f32[4,32,256]{2,1,0:T(8,128)S(1)}, f32[4,32,256]{2,1,0:T(8,128)S(1)}, u32[]{:S(2)}, u32[]{:S(2)}) collective-permute-start(f32[4,32,256]{2,1,0:T(8,128)S(1)} %get-tuple-element.44.refs_6_.ends_ref), channel_id=1, source_target_pairs={{0,4},{4,0},{8,12},{12,8},{16,20},{20,16},{24,28},{28,24},{1,5},{5... | collective-permute-start | bytes 393224 | tf_op jit(solution)/shard_map/ppermute | solution.py:694
  23.3 3.7 %collective-permute-done.13.other_ref.refs_0_ = f32[4,32,256]{2,1,0:T(8,128)S(1)} collective-permute-done((f32[4,32,256]{2,1,0:T(8,128)S(1)}, f32[4,32,256]{2,1,0:T(8,128)S(1)}, u32[]{:S(2)}, u32[]{:S(2)}) %collective-permute-start.13) | collective-permute-done | bytes 131104 | tf_op jit(solution)/shard_map/ppermute | solution.py:694
  27.6 1.7 %collective-permute-start.14 = (f32[4,32,256]{2,1,0:T(8,128)S(1)}, f32[4,32,256]{2,1,0:T(8,128)S(1)}, u32[]{:S(2)}, u32[]{:S(2)}) collective-permute-start(f32[4,32,256]{2,1,0:T(8,128)S(1)} %join_ends.6.ends_ref), channel_id=1, source_target_pairs={{0,8},{4,12},{8,0},{12,4},{16,24},{20,28},{24,16},{28,20},{1,9},{5... | collective-permute-start | bytes 393224 | tf_op jit(solution)/shard_map/ppermute | solution.py:694
  29.3 2.3 %collective-permute-done.2.refs_3_ = f32[32,2048]{1,0:T(8,128)S(1)} collective-permute-done((f32[32,2048]{1,0:T(8,128)S(1)}, f32[32,2048]{1,0:T(8,128)S(1)}, u32[]{:S(2)}, u32[]{:S(2)}) %collective-permute-start.2) | collective-permute-done | bytes 262176 | tf_op jit(solution)/shard_map/ppermute | solution.py:653
  31.6 1.6 %y_forward.3 = (f32[32,32,256]{2,1,0:T(8,128)S(1)}, f32[4,32,256]{2,1,0:T(8,128)S(1)}, f32[8,32,256]{2,1,0:T(8,128)S(1)}) custom-call(s32[2]{0:T(128)S(1)} %pad_add_fusion.me_ref, f32[32,2048]{1,0:T(8,128)S(1)} %get-tuple-element.36.refs_0_, f32[32,2048]{1,0:T(8,128)S(1)} %collective-permute-done.refs_1_, f32[32,2048]{1,0:T(8,128)S(1)} %collective-permute-done.1.refs_2_, ...), custom_call_target="tpu_custom_call" | custom-call | tf_op jit(solution)/shard_map/y_forward/pallas_call | solution.py:173
  33.3 1.7 %collective-permute-start.12 = (f32[27,16,128]{2,1,0:T(8,128)S(1)}, f32[27,16,128]{2,1,0:T(8,128)S(1)}, u32[]{:S(2)}, u32[]{:S(2)}) collective-permute-start(f32[27,16,128]{2,1,0:T(8,128)S(1)} %join_rows.1.refs_0_), channel_id=1, source_target_pairs={{0,3},{1,2},{2,1},{3,0},{4,7},{5,6},{6,5},{7,4},{8,11},{9,10},{10,... | collective-permute-start | bytes 663560 | tf_op jit(solution)/shard_map/ppermute | solution.py:704
  36.2 2.4 %collective-permute-start.15 = (f32[4,32,256]{2,1,0:T(8,128)S(1)}, f32[4,32,256]{2,1,0:T(8,128)S(1)}, u32[]{:S(2)}, u32[]{:S(2)}) collective-permute-start(f32[4,32,256]{2,1,0:T(8,128)S(1)} %join_ends.7), channel_id=1, source_target_pairs={{0,16},{4,20},{8,24},{12,28},{16,0},{20,4},{24,8},{28,12},{1,17},{... | collective-permute-start | bytes 393224 | tf_op jit(solution)/shard_map/ppermute | solution.py:694
  38.6 1.5 %collective-permute-done.8.other_ref.refs_0_ = f32[4,32,256]{2,1,0:T(8,128)S(1)} collective-permute-done((f32[4,32,256]{2,1,0:T(8,128)S(1)}, f32[4,32,256]{2,1,0:T(8,128)S(1)}, u32[]{:S(2)}, u32[]{:S(2)}) %collective-permute-start.8) | collective-permute-done | bytes 131104 | tf_op jit(solution)/shard_map/ppermute | solution.py:694
  41.9 2.6 %collective-permute-done.15.refs_2_ = f32[4,32,256]{2,1,0:T(8,128)S(1)} collective-permute-done((f32[4,32,256]{2,1,0:T(8,128)S(1)}, f32[4,32,256]{2,1,0:T(8,128)S(1)}, u32[]{:S(2)}, u32[]{:S(2)}) %collective-permute-start.15) | collective-permute-done | bytes 131104 | tf_op jit(solution)/shard_map/ppermute | solution.py:694
  44.5 1.8 %y_backward.2 = (f32[32,2048]{1,0:T(8,128)S(1)}, f32[32,2048]{1,0:T(8,128)S(1)}, f32[32,2048]{1,0:T(8,128)S(1)}, f32[32,2048]{1,0:T(8,128)S(1)}) custom-call(s32[2]{0:T(128)S(1)} %pad_add_fusion.me_ref, f32[32,32,256]{2,1,0:T(8,128)S(1)} %get-tuple-element.51.spec_ref, f32[4,32,256]{2,1,0:T(8,128)S(1)} %get-tuple-element.44.refs_6_.ends_ref, ...), custom_call_target="tpu_custom_call" | custom-call | tf_op jit(solution)/shard_map/y_backward/pallas_call | solution.py:296
  46.3 1.5 %collective-permute-start.19 = (f32[32,2048]{1,0:T(8,128)S(1)}, f32[32,2048]{1,0:T(8,128)S(1)}, u32[]{:S(2)}, u32[]{:S(2)}) collective-permute-start(f32[32,2048]{1,0:T(8,128)S(1)} %get-tuple-element.59), channel_id=1, source_target_pairs={{0,1},{1,0},{2,3},{3,2},{4,5},{5,4},{6,7},{7,6},{8,9},{9,8},{10,11... | collective-permute-start | bytes 786440 | tf_op jit(solution)/shard_map/ppermute | solution.py:653
  48.4 1.6 %collective-permute-start.10 = (f32[4,32,256]{2,1,0:T(8,128)S(1)}, f32[4,32,256]{2,1,0:T(8,128)S(1)}, u32[]{:S(2)}, u32[]{:S(2)}) collective-permute-start(f32[4,32,256]{2,1,0:T(8,128)S(1)} %join_ends.5), channel_id=1, source_target_pairs={{0,16},{4,20},{8,24},{12,28},{16,0},{20,4},{24,8},{28,12},{1,17},{... | collective-permute-start | bytes 393224 | tf_op jit(solution)/shard_map/ppermute | solution.py:694
  50.2 2.2 %collective-permute-start.21 = (f32[32,2048]{1,0:T(8,128)S(1)}, f32[32,2048]{1,0:T(8,128)S(1)}, u32[]{:S(2)}, u32[]{:S(2)}) collective-permute-start(f32[32,2048]{1,0:T(8,128)S(1)} %get-tuple-element.61), channel_id=1, source_target_pairs={{0,3},{1,2},{2,1},{3,0},{4,7},{5,6},{6,5},{7,4},{8,11},{9,10},{10,... | collective-permute-start | bytes 786440 | tf_op jit(solution)/shard_map/ppermute | solution.py:653
  52.5 4.0 %pair_pull.2.refs_5_ = f32[3,5,128]{2,1,0:T(8,128)S(1)} custom-call(s32[16,8]{1,0:T(8,128)S(1)} %get-tuple-element.48.pairs_ref, s32[8,256]{1,0:T(8,128)S(1)} %get-tuple-element.49.marks_ref, f32[2048,1152]{1,0:T(8,128)S(1)} %spread_rows.1.refs_8_.near, f32[1296,128]{1,0:T(8,128)S(1)} %get-tuple-element.50.refs_5_.far, f32[32,2048]{1,0:T(8,128)S(1)} %get-tuple-element.53.refs_0_), custom_call_target="tpu_custom_call" | custom-call | flops 1500000000 | tf_op jit(solution)/shard_map/pair_pull/pallas_call | solution.py:620
  56.7 1.8 %y_backward.3 = (f32[32,2048]{1,0:T(8,128)S(1)}, f32[32,2048]{1,0:T(8,128)S(1)}, f32[32,2048]{1,0:T(8,128)S(1)}, f32[32,2048]{1,0:T(8,128)S(1)}) custom-call(s32[2]{0:T(128)S(1)} %pad_add_fusion.me_ref, f32[32,32,256]{2,1,0:T(8,128)S(1)} %get-tuple-element.45.spec_ref, f32[4,32,256]{2,1,0:T(8,128)S(1)} %get-tuple-element.46.ends_ref.after_ref, ...), custom_call_target="tpu_custom_call" | custom-call | tf_op jit(solution)/shard_map/y_backward/pallas_call | solution.py:296
  58.5 1.4 %collective-permute-start.16 = (f32[32,2048]{1,0:T(8,128)S(1)}, f32[32,2048]{1,0:T(8,128)S(1)}, u32[]{:S(2)}, u32[]{:S(2)}) collective-permute-start(f32[32,2048]{1,0:T(8,128)S(1)} %get-tuple-element.55), channel_id=1, source_target_pairs={{0,1},{1,0},{2,3},{3,2},{4,5},{5,4},{6,7},{7,6},{8,9},{9,8},{10,11... | collective-permute-start | bytes 786440 | tf_op jit(solution)/shard_map/ppermute | solution.py:653
  60.2 1.5 %collective-permute-start.18 = (f32[32,2048]{1,0:T(8,128)S(1)}, f32[32,2048]{1,0:T(8,128)S(1)}, u32[]{:S(2)}, u32[]{:S(2)}) collective-permute-start(f32[32,2048]{1,0:T(8,128)S(1)} %get-tuple-element.57), channel_id=1, source_target_pairs={{0,3},{1,2},{2,1},{3,0},{4,7},{5,6},{6,5},{7,4},{8,11},{9,10},{10,... | collective-permute-start | bytes 786440 | tf_op jit(solution)/shard_map/ppermute | solution.py:653
  61.6 7.6 %pair_pull.3.refs_8_.refs_11_ = f32[3,11,128]{2,1,0:T(8,128)S(1)} custom-call(s32[16,8]{1,0:T(8,128)S(1)} %get-tuple-element.48.pairs_ref, s32[8,256]{1,0:T(8,128)S(1)} %get-tuple-element.49.marks_ref, f32[2048,1152]{1,0:T(8,128)S(1)} %spread_rows.1.refs_8_.near, f32[1296,128]{1,0:T(8,128)S(1)} %get-tuple-element.50.refs_5_.far, ...), custom_call_target="tpu_custom_call" | custom-call | tf_op jit(solution)/shard_map/pair_pull/pallas_call | solution.py:620
  69.3 3.6 %z_backward.2 = (f32[2048,256]{1,0:T(8,128)S(1)}, f32[16,128]{1,0:T(8,128)S(1)}) custom-call(s32[2]{0:T(128)S(1)} %pad_add_fusion.me_ref, f32[32,2048]{1,0:T(8,128)S(1)} %get-tuple-element.53.refs_0_, f32[32,2048]{1,0:T(8,128)S(1)} %collective-permute-done.19.refs_1_, f32[32,2048]{1,0:T(8,128)S(1)} %collective-permute-done.20.refs_2_, ...), custom_call_target="tpu_custom_call" | custom-call | tf_op jit(solution)/shard_map/z_backward/pallas_call | solution.py:450
  72.9 2.0 %collective-permute-done.18.refs_3_ = f32[32,2048]{1,0:T(8,128)S(1)} collective-permute-done((f32[32,2048]{1,0:T(8,128)S(1)}, f32[32,2048]{1,0:T(8,128)S(1)}, u32[]{:S(2)}, u32[]{:S(2)}) %collective-permute-start.18) | collective-permute-done | bytes 262176 | tf_op jit(solution)/shard_map/ppermute | solution.py:653
  74.9 4.4 %z_backward.3 = (f32[2048,256]{1,0:T(8,128)}, f32[3,16,128]{2,1,0:T(8,128)}) custom-call(s32[2]{0:T(128)S(1)} %pad_add_fusion.me_ref, f32[32,2048]{1,0:T(8,128)S(1)} %get-tuple-element.54.refs_0_, f32[32,2048]{1,0:T(8,128)S(1)} %collective-permute-done.16.refs_1_, f32[32,2048]{1,0:T(8,128)S(1)} %collective-permute-done.17.refs_2_, ...), custom_call_target="tpu_custom_call" | custom-call | tf_op jit(solution)/shard_map/z_backward/pallas_call | solution.py:450
  (54 shorter events, 7.2 us)
Async XLA Ops:
  0.6 6.9 %copy-start.9 = (s32[1,1,16,8]{2,3,1,0:T(8,128)S(1)}, s32[1,1,16,8]{2,3,1,0:T(8,128)}, u32[]{:S(2)}) copy-start(s32[1,1,16,8]{2,3,1,0:T(8,128)} %param.13) | copy-start | bytes 1540
  0.6 6.9 %copy-start.8 = (s32[1,1,16]{2,1,0:T(1,128)S(1)}, s32[1,1,16]{2,1,0:T(1,128)}, u32[]{:S(2)}) copy-start(s32[1,1,16]{2,1,0:T(1,128)} %param.12) | copy-start | bytes 196
  0.7 6.9 %copy-start.5 = (s32[1,1,2048]{2,1,0:T(1,128)S(1)}, s32[1,1,2048]{2,1,0:T(1,128)}, u32[]{:S(2)}) copy-start(s32[1,1,2048]{2,1,0:T(1,128)} %param.11) | copy-start | bytes 24580
  0.7 1.0 %copy-start = (f32[256,256]{1,0:T(8,128)S(1)}, f32[256,256]{1,0:T(8,128)}, u32[]{:S(2)}) copy-start(f32[256,256]{1,0:T(8,128)} %constant.13.clone.table_ref.refs_4_.refs_3_) | copy-start | bytes 786436
  1.7 1.6 %copy-start.2 = (f32[32,64,256]{2,1,0:T(8,128)S(1)}, f32[32,64,256]{2,1,0:T(8,128)}, u32[]{:S(2)}) copy-start(f32[32,64,256]{2,1,0:T(8,128)} %param.8) | copy-start | bytes 6291460
  3.3 4.3 %copy-start.6 = (f32[6,1,1,2048]{3,2,1,0:T(1,128)S(1)}, f32[6,1,1,2048]{3,2,1,0:T(1,128)}, u32[]{:S(2)}) copy-start(f32[6,1,1,2048]{3,2,1,0:T(1,128)} %param.9) | copy-start | bytes 147460
  3.3 4.3 %copy-start.7 = (f32[3,1,1,2048]{3,2,1,0:T(1,128)S(1)}, f32[3,1,1,2048]{3,2,1,0:T(1,128)}, u32[]{:S(2)}) copy-start(f32[3,1,1,2048]{3,2,1,0:T(1,128)} %param.10) | copy-start | bytes 73732
  4.6 14.4 %collective-permute-start.3 = (f32[32,2048]{1,0:T(8,128)S(1)}, f32[32,2048]{1,0:T(8,128)S(1)}, u32[]{:S(2)}, u32[]{:S(2)}) collective-permute-start(f32[32,2048]{1,0:T(8,128)S(1)} %get-tuple-element.40), channel_id=1, source_target_pairs={{0,1},{1,0},{2,3},{3,2},{4,5},{5,4},{6,7},{7,6},{8,9},{9,8},{10,11... | collective-permute-start | bytes 786440 | tf_op jit(solution)/shard_map/ppermute | solution.py:653
  4.7 14.6 %collective-permute-start.4 = (f32[32,2048]{1,0:T(8,128)S(1)}, f32[32,2048]{1,0:T(8,128)S(1)}, u32[]{:S(2)}, u32[]{:S(2)}) collective-permute-start(f32[32,2048]{1,0:T(8,128)S(1)} %get-tuple-element.41), channel_id=1, source_target_pairs={{0,2},{1,3},{2,0},{3,1},{4,6},{5,7},{6,4},{7,5},{8,10},{9,11},{10,... | collective-permute-start | bytes 786440 | tf_op jit(solution)/shard_map/ppermute | solution.py:653
  7.4 12.2 %collective-permute-start.5 = (f32[32,2048]{1,0:T(8,128)S(1)}, f32[32,2048]{1,0:T(8,128)S(1)}, u32[]{:S(2)}, u32[]{:S(2)}) collective-permute-start(f32[32,2048]{1,0:T(8,128)S(1)} %get-tuple-element.42), channel_id=1, source_target_pairs={{0,3},{1,2},{2,1},{3,0},{4,7},{5,6},{6,5},{7,4},{8,11},{9,10},{10,... | collective-permute-start | bytes 786440 | tf_op jit(solution)/shard_map/ppermute | solution.py:653
  8.2 6.2 %copy-start.1 = (f32[256,256]{1,0:T(8,128)S(1)}, f32[256,256]{1,0:T(8,128)}, u32[]{:S(2)}) copy-start(f32[256,256]{1,0:T(8,128)} %constant.13.clone.table_ref.refs_4_.refs_3_) | copy-start | bytes 786436
  8.2 6.2 %copy-start.3 = (f32[32,64,256]{2,1,0:T(8,128)S(1)}, f32[32,64,256]{2,1,0:T(8,128)}, u32[]{:S(2)}) copy-start(f32[32,64,256]{2,1,0:T(8,128)} %param.8) | copy-start | bytes 6291460
  8.2 8.9 %collective-permute-start.6 = (f32[9,16,128]{2,1,0:T(8,128)S(1)}, f32[9,16,128]{2,1,0:T(8,128)S(1)}, u32[]{:S(2)}, u32[]{:S(2)}) collective-permute-start(f32[9,16,128]{2,1,0:T(8,128)S(1)} %get-tuple-element.35.refs_0_.source_ref.own_ref.refs_7_), channel_id=1, source_target_pairs={{0,4},{4,8},{8,12},{12,16},{16,20},{20,24},{24,28},{28,0},{1,5},{5... | collective-permute-start | bytes 221192 | tf_op jit(solution)/shard_map/ppermute | solution.py:679
  9.9 7.7 %collective-permute-start.7 = (f32[9,16,128]{2,1,0:T(8,128)S(1)}, f32[9,16,128]{2,1,0:T(8,128)S(1)}, u32[]{:S(2)}, u32[]{:S(2)}) collective-permute-start(f32[9,16,128]{2,1,0:T(8,128)S(1)} %get-tuple-element.35.refs_0_.source_ref.own_ref.refs_7_), channel_id=1, source_target_pairs={{4,0},{8,4},{12,8},{16,12},{20,16},{24,20},{28,24},{0,28},{5,1},{9... | collective-permute-start | bytes 221192 | tf_op jit(solution)/shard_map/ppermute | solution.py:680
  14.4 5.2 %copy-start.4 = (f32[8,256,256]{2,1,0:T(8,128)S(1)}, f32[8,256,256]{2,1,0:T(8,128)}, u32[]{:S(2)}) copy-start(f32[8,256,256]{2,1,0:T(8,128)} %constant.14.clone.refs_5_) | copy-start | bytes 6291460
  17.1 12.2 %collective-permute-start = (f32[32,2048]{1,0:T(8,128)S(1)}, f32[32,2048]{1,0:T(8,128)S(1)}, u32[]{:S(2)}, u32[]{:S(2)}) collective-permute-start(f32[32,2048]{1,0:T(8,128)S(1)} %get-tuple-element.37), channel_id=1, source_target_pairs={{0,1},{1,0},{2,3},{3,2},{4,5},{5,4},{6,7},{7,6},{8,9},{9,8},{10,11... | collective-permute-start | bytes 786440 | tf_op jit(solution)/shard_map/ppermute | solution.py:653
  17.6 11.7 %collective-permute-start.1 = (f32[32,2048]{1,0:T(8,128)S(1)}, f32[32,2048]{1,0:T(8,128)S(1)}, u32[]{:S(2)}, u32[]{:S(2)}) collective-permute-start(f32[32,2048]{1,0:T(8,128)S(1)} %get-tuple-element.38), channel_id=1, source_target_pairs={{0,2},{1,3},{2,0},{3,1},{4,6},{5,7},{6,4},{7,5},{8,10},{9,11},{10,... | collective-permute-start | bytes 786440 | tf_op jit(solution)/shard_map/ppermute | solution.py:653
  19.0 12.6 %collective-permute-start.2 = (f32[32,2048]{1,0:T(8,128)S(1)}, f32[32,2048]{1,0:T(8,128)S(1)}, u32[]{:S(2)}, u32[]{:S(2)}) collective-permute-start(f32[32,2048]{1,0:T(8,128)S(1)} %get-tuple-element.39), channel_id=1, source_target_pairs={{0,3},{1,2},{2,1},{3,0},{4,7},{5,6},{6,5},{7,4},{8,11},{9,10},{10,... | collective-permute-start | bytes 786440 | tf_op jit(solution)/shard_map/ppermute | solution.py:653
  21.4 5.6 %collective-permute-start.13 = (f32[4,32,256]{2,1,0:T(8,128)S(1)}, f32[4,32,256]{2,1,0:T(8,128)S(1)}, u32[]{:S(2)}, u32[]{:S(2)}) collective-permute-start(f32[4,32,256]{2,1,0:T(8,128)S(1)} %get-tuple-element.44.refs_6_.ends_ref), channel_id=1, source_target_pairs={{0,4},{4,0},{8,12},{12,8},{16,20},{20,16},{24,28},{28,24},{1,5},{5... | collective-permute-start | bytes 393224 | tf_op jit(solution)/shard_map/ppermute | solution.py:694
  27.6 8.0 %collective-permute-start.14 = (f32[4,32,256]{2,1,0:T(8,128)S(1)}, f32[4,32,256]{2,1,0:T(8,128)S(1)}, u32[]{:S(2)}, u32[]{:S(2)}) collective-permute-start(f32[4,32,256]{2,1,0:T(8,128)S(1)} %join_ends.6.ends_ref), channel_id=1, source_target_pairs={{0,8},{4,12},{8,0},{12,4},{16,24},{20,28},{24,16},{28,20},{1,9},{5... | collective-permute-start | bytes 393224 | tf_op jit(solution)/shard_map/ppermute | solution.py:694
  33.2 8.0 %collective-permute-start.11 = (f32[27,16,128]{2,1,0:T(8,128)S(1)}, f32[27,16,128]{2,1,0:T(8,128)S(1)}, u32[]{:S(2)}, u32[]{:S(2)}) collective-permute-start(f32[27,16,128]{2,1,0:T(8,128)S(1)} %join_rows.1.refs_0_), channel_id=1, source_target_pairs={{0,1},{1,0},{2,3},{3,2},{4,5},{5,4},{6,7},{7,6},{8,9},{9,8},{10,11... | collective-permute-start | bytes 663560 | tf_op jit(solution)/shard_map/ppermute | solution.py:703
  33.3 7.9 %collective-permute-start.12 = (f32[27,16,128]{2,1,0:T(8,128)S(1)}, f32[27,16,128]{2,1,0:T(8,128)S(1)}, u32[]{:S(2)}, u32[]{:S(2)}) collective-permute-start(f32[27,16,128]{2,1,0:T(8,128)S(1)} %join_rows.1.refs_0_), channel_id=1, source_target_pairs={{0,3},{1,2},{2,1},{3,0},{4,7},{5,6},{6,5},{7,4},{8,11},{9,10},{10,... | collective-permute-start | bytes 663560 | tf_op jit(solution)/shard_map/ppermute | solution.py:704
  35.0 5.1 %collective-permute-start.8 = (f32[4,32,256]{2,1,0:T(8,128)S(1)}, f32[4,32,256]{2,1,0:T(8,128)S(1)}, u32[]{:S(2)}, u32[]{:S(2)}) collective-permute-start(f32[4,32,256]{2,1,0:T(8,128)S(1)} %get-tuple-element.46.ends_ref.after_ref), channel_id=1, source_target_pairs={{0,4},{4,0},{8,12},{12,8},{16,20},{20,16},{24,28},{28,24},{1,5},{5... | collective-permute-start | bytes 393224 | tf_op jit(solution)/shard_map/ppermute | solution.py:694
  36.2 8.3 %collective-permute-start.15 = (f32[4,32,256]{2,1,0:T(8,128)S(1)}, f32[4,32,256]{2,1,0:T(8,128)S(1)}, u32[]{:S(2)}, u32[]{:S(2)}) collective-permute-start(f32[4,32,256]{2,1,0:T(8,128)S(1)} %join_ends.7), channel_id=1, source_target_pairs={{0,16},{4,20},{8,24},{12,28},{16,0},{20,4},{24,8},{28,12},{1,17},{... | collective-permute-start | bytes 393224 | tf_op jit(solution)/shard_map/ppermute | solution.py:694
  40.7 7.2 %collective-permute-start.9 = (f32[4,32,256]{2,1,0:T(8,128)S(1)}, f32[4,32,256]{2,1,0:T(8,128)S(1)}, u32[]{:S(2)}, u32[]{:S(2)}) collective-permute-start(f32[4,32,256]{2,1,0:T(8,128)S(1)} %join_ends.4.ends_ref), channel_id=1, source_target_pairs={{0,8},{4,12},{8,0},{12,4},{16,24},{20,28},{24,16},{28,20},{1,9},{5... | collective-permute-start | bytes 393224 | tf_op jit(solution)/shard_map/ppermute | solution.py:694
  46.3 13.9 %collective-permute-start.19 = (f32[32,2048]{1,0:T(8,128)S(1)}, f32[32,2048]{1,0:T(8,128)S(1)}, u32[]{:S(2)}, u32[]{:S(2)}) collective-permute-start(f32[32,2048]{1,0:T(8,128)S(1)} %get-tuple-element.59), channel_id=1, source_target_pairs={{0,1},{1,0},{2,3},{3,2},{4,5},{5,4},{6,7},{7,6},{8,9},{9,8},{10,11... | collective-permute-start | bytes 786440 | tf_op jit(solution)/shard_map/ppermute | solution.py:653
  48.4 8.3 %collective-permute-start.10 = (f32[4,32,256]{2,1,0:T(8,128)S(1)}, f32[4,32,256]{2,1,0:T(8,128)S(1)}, u32[]{:S(2)}, u32[]{:S(2)}) collective-permute-start(f32[4,32,256]{2,1,0:T(8,128)S(1)} %join_ends.5), channel_id=1, source_target_pairs={{0,16},{4,20},{8,24},{12,28},{16,0},{20,4},{24,8},{28,12},{1,17},{... | collective-permute-start | bytes 393224 | tf_op jit(solution)/shard_map/ppermute | solution.py:694
  50.0 19.3 %collective-permute-start.20 = (f32[32,2048]{1,0:T(8,128)S(1)}, f32[32,2048]{1,0:T(8,128)S(1)}, u32[]{:S(2)}, u32[]{:S(2)}) collective-permute-start(f32[32,2048]{1,0:T(8,128)S(1)} %get-tuple-element.60), channel_id=1, source_target_pairs={{0,2},{1,3},{2,0},{3,1},{4,6},{5,7},{6,4},{7,5},{8,10},{9,11},{10,... | collective-permute-start | bytes 786440 | tf_op jit(solution)/shard_map/ppermute | solution.py:653
  50.2 19.1 %collective-permute-start.21 = (f32[32,2048]{1,0:T(8,128)S(1)}, f32[32,2048]{1,0:T(8,128)S(1)}, u32[]{:S(2)}, u32[]{:S(2)}) collective-permute-start(f32[32,2048]{1,0:T(8,128)S(1)} %get-tuple-element.61), channel_id=1, source_target_pairs={{0,3},{1,2},{2,1},{3,0},{4,7},{5,6},{6,5},{7,4},{8,11},{9,10},{10,... | collective-permute-start | bytes 786440 | tf_op jit(solution)/shard_map/ppermute | solution.py:653
  58.5 14.4 %collective-permute-start.16 = (f32[32,2048]{1,0:T(8,128)S(1)}, f32[32,2048]{1,0:T(8,128)S(1)}, u32[]{:S(2)}, u32[]{:S(2)}) collective-permute-start(f32[32,2048]{1,0:T(8,128)S(1)} %get-tuple-element.55), channel_id=1, source_target_pairs={{0,1},{1,0},{2,3},{3,2},{4,5},{5,4},{6,7},{7,6},{8,9},{9,8},{10,11... | collective-permute-start | bytes 786440 | tf_op jit(solution)/shard_map/ppermute | solution.py:653
  59.9 13.0 %collective-permute-start.17 = (f32[32,2048]{1,0:T(8,128)S(1)}, f32[32,2048]{1,0:T(8,128)S(1)}, u32[]{:S(2)}, u32[]{:S(2)}) collective-permute-start(f32[32,2048]{1,0:T(8,128)S(1)} %get-tuple-element.56), channel_id=1, source_target_pairs={{0,2},{1,3},{2,0},{3,1},{4,6},{5,7},{6,4},{7,5},{8,10},{9,11},{10,... | collective-permute-start | bytes 786440 | tf_op jit(solution)/shard_map/ppermute | solution.py:653
  60.2 14.7 %collective-permute-start.18 = (f32[32,2048]{1,0:T(8,128)S(1)}, f32[32,2048]{1,0:T(8,128)S(1)}, u32[]{:S(2)}, u32[]{:S(2)}) collective-permute-start(f32[32,2048]{1,0:T(8,128)S(1)} %get-tuple-element.57), channel_id=1, source_target_pairs={{0,3},{1,2},{2,1},{3,0},{4,7},{5,6},{6,5},{7,4},{8,11},{9,10},{10,... | collective-permute-start | bytes 786440 | tf_op jit(solution)/shard_map/ppermute | solution.py:653

commit v5 on v4

--- a/solution.py
+++ b/solution.py
@@ -72,7 +72,9 @@
     def one(a, b):
         return lax.dot_general(a, b, (dims, ((), ())), preferred_element_type=jnp.float32)
 
-    return one(left[0], right[0]) + one(left[0], right[1]) + one(left[1], right[0])
+    rows = left[0].shape[0]
+    both = one(jnp.concatenate(left, axis=0), right[0])
+    return both[:rows] + both[rows:] + one(left[0], right[1])
 
 
 def whole(memory=pltpu.VMEM):
@@ -418,7 +420,7 @@
                 )
                 writes[-1].start()
         place = cells_ref[...] // length
-        lane_tile = min(512, seg_total)
+        lane_tile = min(1024, seg_total)
         taus = []
         for k in range(0, seg_total, lane_tile):
             at = slice(k, k + lane_tile)

time: 79.7 us -> 79.8 us (level)
  no operation moved by 1% of the time
where the time goes in v5:
time: 79.8 us; the launch traced here: 79.6 us
  Pallas kernels  35.4 us (44%)
  starting transfers between devices  27.4 us (34%)
  waiting for transfers between devices  13 us (16%)
  local copies, waits for them, and re-layouts  2.65 us (3%)
  between operations  1.05 us (1%)
    ppermute x12, starting transfers between devices, swap(): lax.ppermute(parts[d], 'gy', [(i, i ^ d) for i in range(groups_y)])  12.2 us
    pallas_call x2, Pallas kernels, pair_pull(): pl.pallas_call(kernel, in_specs=[whole(pltpu.SMEM)] * 2 + [whole()] * 2 +...  11.4 us
    ppermute x6, starting transfers between devices, per_device(): lax.ppermute(joined[c][-1], 'gx', [(i, i ^ 2 ** level) for i in range(gro...  8.66 us
    pallas_call x2, Pallas kernels, z_backward(): pl.pallas_call(kernel, in_specs=[whole(pltpu.SMEM)] + [whole()] * (len(op...  8.04 us
    ppermute x6, waiting for transfers between devices, per_device(): lax.ppermute(joined[c][-1], 'gx', [(i, i ^ 2 ** level) for i in range(gro...  7.88 us
    ppermute x12, waiting for transfers between devices, swap(): lax.ppermute(parts[d], 'gy', [(i, i ^ d) for i in range(groups_y)])  5.07 us
    pallas_call x2, Pallas kernels, y_backward(): pl.pallas_call(kernel, in_specs=[whole(pltpu.SMEM)] + [whole()] * (levels...  3.72 us
    pallas_call x2, Pallas kernels, y_forward(): pl.pallas_call(kernel, in_specs=[whole(pltpu.SMEM)] + [whole()] * (groups...  3.32 us
  transfers between devices with their start and end apart: 22, of which 7 were waited for; matrix products, arithmetic and copies ran while one was open for 0% of the time, Pallas kernels for 37%

profile of v5, /device:TPU:1, one launch (start us, length us, event | category | flops | bytes accessed | tf_op | source)
XLA Modules:
  0.0 79.6 jit_solution(8565188517690752772)
XLA Ops:
  0.7 0.9 %copy-done = f32[256,256]{1,0:T(8,128)S(1)} copy-done((f32[256,256]{1,0:T(8,128)S(1)}, f32[256,256]{1,0:T(8,128)}, u32[]{:S(2)}) %copy-start) | copy-done | bytes 262168
  1.7 1.6 %copy-done.2 = f32[32,64,256]{2,1,0:T(8,128)S(1)} copy-done((f32[32,64,256]{2,1,0:T(8,128)S(1)}, f32[32,64,256]{2,1,0:T(8,128)}, u32[]{:S(2)}) %copy-start.2) | copy-done | bytes 2097176
  3.3 1.3 %z_forward.2 = (f32[32,2048]{1,0:T(8,128)S(1)}, f32[32,2048]{1,0:T(8,128)S(1)}, f32[32,2048]{1,0:T(8,128)S(1)}, f32[32,2048]{1,0:T(8,128)S(1)}) custom-call(s32[2]{0:T(128)S(1)} %pad_add_fusion.me_ref, f32[2048,256]{1,0:T(8,128)S(1)} %bitcast.11, f32[256,256]{1,0:T(8,128)S(1)} %copy-done), custom_call_target="tpu_custom_call" | custom-call | tf_op jit(solution)/shard_map/z_forward/pallas_call | solution.py:114
  4.7 2.7 %collective-permute-start.4 = (f32[32,2048]{1,0:T(8,128)S(1)}, f32[32,2048]{1,0:T(8,128)S(1)}, u32[]{:S(2)}, u32[]{:S(2)}) collective-permute-start(f32[32,2048]{1,0:T(8,128)S(1)} %get-tuple-element.41), channel_id=1, source_target_pairs={{0,2},{1,3},{2,0},{3,1},{4,6},{5,7},{6,4},{7,5},{8,10},{9,11},{10,... | collective-permute-start | bytes 786440 | tf_op jit(solution)/shard_map/ppermute | solution.py:655
  8.2 1.7 %collective-permute-start.6 = (f32[9,16,128]{2,1,0:T(8,128)S(1)}, f32[9,16,128]{2,1,0:T(8,128)S(1)}, u32[]{:S(2)}, u32[]{:S(2)}) collective-permute-start(f32[9,16,128]{2,1,0:T(8,128)S(1)} %get-tuple-element.35.refs_0_.source_ref.own_ref.refs_7_), channel_id=1, source_target_pairs={{0,4},{4,8},{8,12},{12,16},{16,20},{20,24},{24,28},{28,0},{1,5},{5... | collective-permute-start | bytes 221192 | tf_op jit(solution)/shard_map/ppermute | solution.py:681
  9.9 3.1 %collective-permute-start.7 = (f32[9,16,128]{2,1,0:T(8,128)S(1)}, f32[9,16,128]{2,1,0:T(8,128)S(1)}, u32[]{:S(2)}, u32[]{:S(2)}) collective-permute-start(f32[9,16,128]{2,1,0:T(8,128)S(1)} %get-tuple-element.35.refs_0_.source_ref.own_ref.refs_7_), channel_id=1, source_target_pairs={{4,0},{8,4},{12,8},{16,12},{20,16},{24,20},{28,24},{0,28},{5,1},{9... | collective-permute-start | bytes 221192 | tf_op jit(solution)/shard_map/ppermute | solution.py:682
  13.0 1.4 %spread_rows.1.refs_8_.near = f32[2048,1152]{1,0:T(8,128)S(1)} custom-call(f32[9,16,128]{2,1,0:T(8,128)S(1)} %get-tuple-element.35.refs_0_.source_ref.own_ref.refs_7_), custom_call_target="tpu_custom_call" | custom-call | tf_op jit(solution)/shard_map/spread_rows/pallas_call | solution.py:504
  14.4 1.3 %z_forward.3 = (f32[32,2048]{1,0:T(8,128)S(1)}, f32[32,2048]{1,0:T(8,128)S(1)}, f32[32,2048]{1,0:T(8,128)S(1)}, f32[32,2048]{1,0:T(8,128)S(1)}) custom-call(s32[2]{0:T(128)S(1)} %pad_add_fusion.me_ref, f32[2048,256]{1,0:T(8,128)S(1)} %bitcast.12, f32[256,256]{1,0:T(8,128)S(1)} %copy-done.1, f32[9,16,128]{2,1,0:T(8,128)S(1)} %get-tuple-element.35.refs_0_.source_ref.own_ref.refs_7_), custom_call_target="tpu_custom_call" | custom-call | tf_op jit(solution)/shard_map/z_forward/pallas_call | solution.py:114
  15.8 1.3 %sample_factors.1 = (f32[128,2048]{1,0:T(8,128)S(1)}, f32[128,2048]{1,0:T(8,128)S(1)}) custom-call(s32[2]{0:T(128)S(1)} %pad_add_fusion.me_ref, f32[256,256]{1,0:T(8,128)S(1)} %copy-done.1, s32[1,2048]{1,0:T(1,128)S(1)} %bitcast.14), custom_call_target="tpu_custom_call" | custom-call | tf_op jit(solution)/shard_map/sample_factors/pallas_call | solution.py:364
  17.6 1.4 %collective-permute-start.1 = (f32[32,2048]{1,0:T(8,128)S(1)}, f32[32,2048]{1,0:T(8,128)S(1)}, u32[]{:S(2)}, u32[]{:S(2)}) collective-permute-start(f32[32,2048]{1,0:T(8,128)S(1)} %get-tuple-element.38), channel_id=1, source_target_pairs={{0,2},{1,3},{2,0},{3,1},{4,6},{5,7},{6,4},{7,5},{8,10},{9,11},{10,... | collective-permute-start | bytes 786440 | tf_op jit(solution)/shard_map/ppermute | solution.py:655
  19.6 1.7 %y_forward.2 = (f32[32,32,256]{2,1,0:T(8,128)S(1)}, f32[4,32,256]{2,1,0:T(8,128)S(1)}, f32[8,32,256]{2,1,0:T(8,128)S(1)}) custom-call(s32[2]{0:T(128)S(1)} %pad_add_fusion.me_ref, f32[32,2048]{1,0:T(8,128)S(1)} %get-tuple-element.34.after_ref.refs_0_, f32[32,2048]{1,0:T(8,128)S(1)} %collective-permute-done.3.refs_1_, ...), custom_call_target="tpu_custom_call" | custom-call | tf_op jit(solution)/shard_map/y_forward/pallas_call | solution.py:175
  21.3 1.9 %collective-permute-start.13 = (f32[4,32,256]{2,1,0:T(8,128)S(1)}, f32[4,32,256]{2,1,0:T(8,128)S(1)}, u32[]{:S(2)}, u32[]{:S(2)}) collective-permute-start(f32[4,32,256]{2,1,0:T(8,128)S(1)} %get-tuple-element.44.refs_6_.ends_ref), channel_id=1, source_target_pairs={{0,4},{4,0},{8,12},{12,8},{16,20},{20,16},{24,28},{28,24},{1,5},{5... | collective-permute-start | bytes 393224 | tf_op jit(solution)/shard_map/ppermute | solution.py:696
  23.3 3.7 %collective-permute-done.13.other_ref.refs_0_ = f32[4,32,256]{2,1,0:T(8,128)S(1)} collective-permute-done((f32[4,32,256]{2,1,0:T(8,128)S(1)}, f32[4,32,256]{2,1,0:T(8,128)S(1)}, u32[]{:S(2)}, u32[]{:S(2)}) %collective-permute-start.13) | collective-permute-done | bytes 131104 | tf_op jit(solution)/shard_map/ppermute | solution.py:696
  27.5 1.7 %collective-permute-start.14 = (f32[4,32,256]{2,1,0:T(8,128)S(1)}, f32[4,32,256]{2,1,0:T(8,128)S(1)}, u32[]{:S(2)}, u32[]{:S(2)}) collective-permute-start(f32[4,32,256]{2,1,0:T(8,128)S(1)} %join_ends.6.ends_ref), channel_id=1, source_target_pairs={{0,8},{4,12},{8,0},{12,4},{16,24},{20,28},{24,16},{28,20},{1,9},{5... | collective-permute-start | bytes 393224 | tf_op jit(solution)/shard_map/ppermute | solution.py:696
  29.3 2.3 %collective-permute-done.2.refs_3_ = f32[32,2048]{1,0:T(8,128)S(1)} collective-permute-done((f32[32,2048]{1,0:T(8,128)S(1)}, f32[32,2048]{1,0:T(8,128)S(1)}, u32[]{:S(2)}, u32[]{:S(2)}) %collective-permute-start.2) | collective-permute-done | bytes 262176 | tf_op jit(solution)/shard_map/ppermute | solution.py:655
  31.6 1.7 %y_forward.3 = (f32[32,32,256]{2,1,0:T(8,128)S(1)}, f32[4,32,256]{2,1,0:T(8,128)S(1)}, f32[8,32,256]{2,1,0:T(8,128)S(1)}) custom-call(s32[2]{0:T(128)S(1)} %pad_add_fusion.me_ref, f32[32,2048]{1,0:T(8,128)S(1)} %get-tuple-element.36.refs_0_, f32[32,2048]{1,0:T(8,128)S(1)} %collective-permute-done.refs_1_, f32[32,2048]{1,0:T(8,128)S(1)} %collective-permute-done.1.refs_2_, ...), custom_call_target="tpu_custom_call" | custom-call | tf_op jit(solution)/shard_map/y_forward/pallas_call | solution.py:175
  33.4 1.7 %collective-permute-start.12 = (f32[27,16,128]{2,1,0:T(8,128)S(1)}, f32[27,16,128]{2,1,0:T(8,128)S(1)}, u32[]{:S(2)}, u32[]{:S(2)}) collective-permute-start(f32[27,16,128]{2,1,0:T(8,128)S(1)} %join_rows.1.refs_0_), channel_id=1, source_target_pairs={{0,3},{1,2},{2,1},{3,0},{4,7},{5,6},{6,5},{7,4},{8,11},{9,10},{10,... | collective-permute-start | bytes 663560 | tf_op jit(solution)/shard_map/ppermute | solution.py:706
  36.3 2.4 %collective-permute-start.15 = (f32[4,32,256]{2,1,0:T(8,128)S(1)}, f32[4,32,256]{2,1,0:T(8,128)S(1)}, u32[]{:S(2)}, u32[]{:S(2)}) collective-permute-start(f32[4,32,256]{2,1,0:T(8,128)S(1)} %join_ends.7), channel_id=1, source_target_pairs={{0,16},{4,20},{8,24},{12,28},{16,0},{20,4},{24,8},{28,12},{1,17},{... | collective-permute-start | bytes 393224 | tf_op jit(solution)/shard_map/ppermute | solution.py:696
  38.6 1.5 %collective-permute-done.8.other_ref.refs_0_ = f32[4,32,256]{2,1,0:T(8,128)S(1)} collective-permute-done((f32[4,32,256]{2,1,0:T(8,128)S(1)}, f32[4,32,256]{2,1,0:T(8,128)S(1)}, u32[]{:S(2)}, u32[]{:S(2)}) %collective-permute-start.8) | collective-permute-done | bytes 131104 | tf_op jit(solution)/shard_map/ppermute | solution.py:696
  42.0 2.6 %collective-permute-done.15.refs_2_ = f32[4,32,256]{2,1,0:T(8,128)S(1)} collective-permute-done((f32[4,32,256]{2,1,0:T(8,128)S(1)}, f32[4,32,256]{2,1,0:T(8,128)S(1)}, u32[]{:S(2)}, u32[]{:S(2)}) %collective-permute-start.15) | collective-permute-done | bytes 131104 | tf_op jit(solution)/shard_map/ppermute | solution.py:696
  44.6 1.9 %y_backward.2 = (f32[32,2048]{1,0:T(8,128)S(1)}, f32[32,2048]{1,0:T(8,128)S(1)}, f32[32,2048]{1,0:T(8,128)S(1)}, f32[32,2048]{1,0:T(8,128)S(1)}) custom-call(s32[2]{0:T(128)S(1)} %pad_add_fusion.me_ref, f32[32,32,256]{2,1,0:T(8,128)S(1)} %get-tuple-element.51.spec_ref, f32[4,32,256]{2,1,0:T(8,128)S(1)} %get-tuple-element.44.refs_6_.ends_ref, ...), custom_call_target="tpu_custom_call" | custom-call | tf_op jit(solution)/shard_map/y_backward/pallas_call | solution.py:298
  46.5 1.5 %collective-permute-start.19 = (f32[32,2048]{1,0:T(8,128)S(1)}, f32[32,2048]{1,0:T(8,128)S(1)}, u32[]{:S(2)}, u32[]{:S(2)}) collective-permute-start(f32[32,2048]{1,0:T(8,128)S(1)} %get-tuple-element.59), channel_id=1, source_target_pairs={{0,1},{1,0},{2,3},{3,2},{4,5},{5,4},{6,7},{7,6},{8,9},{9,8},{10,11... | collective-permute-start | bytes 786440 | tf_op jit(solution)/shard_map/ppermute | solution.py:655
  48.6 1.5 %collective-permute-start.10 = (f32[4,32,256]{2,1,0:T(8,128)S(1)}, f32[4,32,256]{2,1,0:T(8,128)S(1)}, u32[]{:S(2)}, u32[]{:S(2)}) collective-permute-start(f32[4,32,256]{2,1,0:T(8,128)S(1)} %join_ends.5), channel_id=1, source_target_pairs={{0,16},{4,20},{8,24},{12,28},{16,0},{20,4},{24,8},{28,12},{1,17},{... | collective-permute-start | bytes 393224 | tf_op jit(solution)/shard_map/ppermute | solution.py:696
  50.3 2.2 %collective-permute-start.21 = (f32[32,2048]{1,0:T(8,128)S(1)}, f32[32,2048]{1,0:T(8,128)S(1)}, u32[]{:S(2)}, u32[]{:S(2)}) collective-permute-start(f32[32,2048]{1,0:T(8,128)S(1)} %get-tuple-element.61), channel_id=1, source_target_pairs={{0,3},{1,2},{2,1},{3,0},{4,7},{5,6},{6,5},{7,4},{8,11},{9,10},{10,... | collective-permute-start | bytes 786440 | tf_op jit(solution)/shard_map/ppermute | solution.py:655
  52.5 4.4 %pair_pull.2.refs_5_ = f32[3,5,128]{2,1,0:T(8,128)S(1)} custom-call(s32[16,8]{1,0:T(8,128)S(1)} %get-tuple-element.48.pairs_ref, s32[8,256]{1,0:T(8,128)S(1)} %get-tuple-element.49.marks_ref, f32[2048,1152]{1,0:T(8,128)S(1)} %spread_rows.1.refs_8_.near, f32[1296,128]{1,0:T(8,128)S(1)} %get-tuple-element.50.refs_5_.far, f32[32,2048]{1,0:T(8,128)S(1)} %get-tuple-element.53.refs_0_), custom_call_target="tpu_custom_call" | custom-call | flops 1500000000 | tf_op jit(solution)/shard_map/pair_pull/pallas_call | solution.py:622
  57.0 1.9 %y_backward.3 = (f32[32,2048]{1,0:T(8,128)S(1)}, f32[32,2048]{1,0:T(8,128)S(1)}, f32[32,2048]{1,0:T(8,128)S(1)}, f32[32,2048]{1,0:T(8,128)S(1)}) custom-call(s32[2]{0:T(128)S(1)} %pad_add_fusion.me_ref, f32[32,32,256]{2,1,0:T(8,128)S(1)} %get-tuple-element.45.spec_ref, f32[4,32,256]{2,1,0:T(8,128)S(1)} %get-tuple-element.46.ends_ref.after_ref, ...), custom_call_target="tpu_custom_call" | custom-call | tf_op jit(solution)/shard_map/y_backward/pallas_call | solution.py:298
  58.9 1.3 %collective-permute-start.16 = (f32[32,2048]{1,0:T(8,128)S(1)}, f32[32,2048]{1,0:T(8,128)S(1)}, u32[]{:S(2)}, u32[]{:S(2)}) collective-permute-start(f32[32,2048]{1,0:T(8,128)S(1)} %get-tuple-element.55), channel_id=1, source_target_pairs={{0,1},{1,0},{2,3},{3,2},{4,5},{5,4},{6,7},{7,6},{8,9},{9,8},{10,11... | collective-permute-start | bytes 786440 | tf_op jit(solution)/shard_map/ppermute | solution.py:655
  60.5 1.5 %collective-permute-start.18 = (f32[32,2048]{1,0:T(8,128)S(1)}, f32[32,2048]{1,0:T(8,128)S(1)}, u32[]{:S(2)}, u32[]{:S(2)}) collective-permute-start(f32[32,2048]{1,0:T(8,128)S(1)} %get-tuple-element.57), channel_id=1, source_target_pairs={{0,3},{1,2},{2,1},{3,0},{4,7},{5,6},{6,5},{7,4},{8,11},{9,10},{10,... | collective-permute-start | bytes 786440 | tf_op jit(solution)/shard_map/ppermute | solution.py:655
  61.9 6.9 %pair_pull.3.refs_8_.refs_11_ = f32[3,11,128]{2,1,0:T(8,128)S(1)} custom-call(s32[16,8]{1,0:T(8,128)S(1)} %get-tuple-element.48.pairs_ref, s32[8,256]{1,0:T(8,128)S(1)} %get-tuple-element.49.marks_ref, f32[2048,1152]{1,0:T(8,128)S(1)} %spread_rows.1.refs_8_.near, f32[1296,128]{1,0:T(8,128)S(1)} %get-tuple-element.50.refs_5_.far, ...), custom_call_target="tpu_custom_call" | custom-call | tf_op jit(solution)/shard_map/pair_pull/pallas_call | solution.py:622
  68.9 3.6 %z_backward.2 = (f32[2048,256]{1,0:T(8,128)S(1)}, f32[16,128]{1,0:T(8,128)S(1)}) custom-call(s32[2]{0:T(128)S(1)} %pad_add_fusion.me_ref, f32[32,2048]{1,0:T(8,128)S(1)} %get-tuple-element.53.refs_0_, f32[32,2048]{1,0:T(8,128)S(1)} %collective-permute-done.19.refs_1_, f32[32,2048]{1,0:T(8,128)S(1)} %collective-permute-done.20.refs_2_, ...), custom_call_target="tpu_custom_call" | custom-call | tf_op jit(solution)/shard_map/z_backward/pallas_call | solution.py:452
  72.5 2.4 %collective-permute-done.18.refs_3_ = f32[32,2048]{1,0:T(8,128)S(1)} collective-permute-done((f32[32,2048]{1,0:T(8,128)S(1)}, f32[32,2048]{1,0:T(8,128)S(1)}, u32[]{:S(2)}, u32[]{:S(2)}) %collective-permute-start.18) | collective-permute-done | bytes 262176 | tf_op jit(solution)/shard_map/ppermute | solution.py:655
  75.0 4.4 %z_backward.3 = (f32[2048,256]{1,0:T(8,128)}, f32[3,16,128]{2,1,0:T(8,128)}) custom-call(s32[2]{0:T(128)S(1)} %pad_add_fusion.me_ref, f32[32,2048]{1,0:T(8,128)S(1)} %get-tuple-element.54.refs_0_, f32[32,2048]{1,0:T(8,128)S(1)} %collective-permute-done.16.refs_1_, f32[32,2048]{1,0:T(8,128)S(1)} %collective-permute-done.17.refs_2_, ...), custom_call_target="tpu_custom_call" | custom-call | tf_op jit(solution)/shard_map/z_backward/pallas_call | solution.py:452
  (54 shorter events, 7.0 us)
Async XLA Ops:
  0.6 6.9 %copy-start.9 = (s32[1,1,16,8]{2,3,1,0:T(8,128)S(1)}, s32[1,1,16,8]{2,3,1,0:T(8,128)}, u32[]{:S(2)}) copy-start(s32[1,1,16,8]{2,3,1,0:T(8,128)} %param.13) | copy-start | bytes 1540
  0.6 6.9 %copy-start.8 = (s32[1,1,16]{2,1,0:T(1,128)S(1)}, s32[1,1,16]{2,1,0:T(1,128)}, u32[]{:S(2)}) copy-start(s32[1,1,16]{2,1,0:T(1,128)} %param.12) | copy-start | bytes 196
  0.7 6.9 %copy-start.5 = (s32[1,1,2048]{2,1,0:T(1,128)S(1)}, s32[1,1,2048]{2,1,0:T(1,128)}, u32[]{:S(2)}) copy-start(s32[1,1,2048]{2,1,0:T(1,128)} %param.11) | copy-start | bytes 24580
  0.7 1.0 %copy-start = (f32[256,256]{1,0:T(8,128)S(1)}, f32[256,256]{1,0:T(8,128)}, u32[]{:S(2)}) copy-start(f32[256,256]{1,0:T(8,128)} %constant.13.clone.table_ref.refs_4_.refs_3_) | copy-start | bytes 786436
  1.7 1.6 %copy-start.2 = (f32[32,64,256]{2,1,0:T(8,128)S(1)}, f32[32,64,256]{2,1,0:T(8,128)}, u32[]{:S(2)}) copy-start(f32[32,64,256]{2,1,0:T(8,128)} %param.8) | copy-start | bytes 6291460
  3.3 4.3 %copy-start.6 = (f32[6,1,1,2048]{3,2,1,0:T(1,128)S(1)}, f32[6,1,1,2048]{3,2,1,0:T(1,128)}, u32[]{:S(2)}) copy-start(f32[6,1,1,2048]{3,2,1,0:T(1,128)} %param.9) | copy-start | bytes 147460
  3.3 4.3 %copy-start.7 = (f32[3,1,1,2048]{3,2,1,0:T(1,128)S(1)}, f32[3,1,1,2048]{3,2,1,0:T(1,128)}, u32[]{:S(2)}) copy-start(f32[3,1,1,2048]{3,2,1,0:T(1,128)} %param.10) | copy-start | bytes 73732
  4.6 14.4 %collective-permute-start.3 = (f32[32,2048]{1,0:T(8,128)S(1)}, f32[32,2048]{1,0:T(8,128)S(1)}, u32[]{:S(2)}, u32[]{:S(2)}) collective-permute-start(f32[32,2048]{1,0:T(8,128)S(1)} %get-tuple-element.40), channel_id=1, source_target_pairs={{0,1},{1,0},{2,3},{3,2},{4,5},{5,4},{6,7},{7,6},{8,9},{9,8},{10,11... | collective-permute-start | bytes 786440 | tf_op jit(solution)/shard_map/ppermute | solution.py:655
  4.7 14.6 %collective-permute-start.4 = (f32[32,2048]{1,0:T(8,128)S(1)}, f32[32,2048]{1,0:T(8,128)S(1)}, u32[]{:S(2)}, u32[]{:S(2)}) collective-permute-start(f32[32,2048]{1,0:T(8,128)S(1)} %get-tuple-element.41), channel_id=1, source_target_pairs={{0,2},{1,3},{2,0},{3,1},{4,6},{5,7},{6,4},{7,5},{8,10},{9,11},{10,... | collective-permute-start | bytes 786440 | tf_op jit(solution)/shard_map/ppermute | solution.py:655
  7.4 12.2 %collective-permute-start.5 = (f32[32,2048]{1,0:T(8,128)S(1)}, f32[32,2048]{1,0:T(8,128)S(1)}, u32[]{:S(2)}, u32[]{:S(2)}) collective-permute-start(f32[32,2048]{1,0:T(8,128)S(1)} %get-tuple-element.42), channel_id=1, source_target_pairs={{0,3},{1,2},{2,1},{3,0},{4,7},{5,6},{6,5},{7,4},{8,11},{9,10},{10,... | collective-permute-start | bytes 786440 | tf_op jit(solution)/shard_map/ppermute | solution.py:655
  8.2 6.2 %copy-start.1 = (f32[256,256]{1,0:T(8,128)S(1)}, f32[256,256]{1,0:T(8,128)}, u32[]{:S(2)}) copy-start(f32[256,256]{1,0:T(8,128)} %constant.13.clone.table_ref.refs_4_.refs_3_) | copy-start | bytes 786436
  8.2 6.2 %copy-start.3 = (f32[32,64,256]{2,1,0:T(8,128)S(1)}, f32[32,64,256]{2,1,0:T(8,128)}, u32[]{:S(2)}) copy-start(f32[32,64,256]{2,1,0:T(8,128)} %param.8) | copy-start | bytes 6291460
  8.2 8.9 %collective-permute-start.6 = (f32[9,16,128]{2,1,0:T(8,128)S(1)}, f32[9,16,128]{2,1,0:T(8,128)S(1)}, u32[]{:S(2)}, u32[]{:S(2)}) collective-permute-start(f32[9,16,128]{2,1,0:T(8,128)S(1)} %get-tuple-element.35.refs_0_.source_ref.own_ref.refs_7_), channel_id=1, source_target_pairs={{0,4},{4,8},{8,12},{12,16},{16,20},{20,24},{24,28},{28,0},{1,5},{5... | collective-permute-start | bytes 221192 | tf_op jit(solution)/shard_map/ppermute | solution.py:681
  9.9 7.7 %collective-permute-start.7 = (f32[9,16,128]{2,1,0:T(8,128)S(1)}, f32[9,16,128]{2,1,0:T(8,128)S(1)}, u32[]{:S(2)}, u32[]{:S(2)}) collective-permute-start(f32[9,16,128]{2,1,0:T(8,128)S(1)} %get-tuple-element.35.refs_0_.source_ref.own_ref.refs_7_), channel_id=1, source_target_pairs={{4,0},{8,4},{12,8},{16,12},{20,16},{24,20},{28,24},{0,28},{5,1},{9... | collective-permute-start | bytes 221192 | tf_op jit(solution)/shard_map/ppermute | solution.py:682
  14.4 5.2 %copy-start.4 = (f32[8,256,256]{2,1,0:T(8,128)S(1)}, f32[8,256,256]{2,1,0:T(8,128)}, u32[]{:S(2)}) copy-start(f32[8,256,256]{2,1,0:T(8,128)} %constant.14.clone.refs_5_) | copy-start | bytes 6291460
  17.1 12.2 %collective-permute-start = (f32[32,2048]{1,0:T(8,128)S(1)}, f32[32,2048]{1,0:T(8,128)S(1)}, u32[]{:S(2)}, u32[]{:S(2)}) collective-permute-start(f32[32,2048]{1,0:T(8,128)S(1)} %get-tuple-element.37), channel_id=1, source_target_pairs={{0,1},{1,0},{2,3},{3,2},{4,5},{5,4},{6,7},{7,6},{8,9},{9,8},{10,11... | collective-permute-start | bytes 786440 | tf_op jit(solution)/shard_map/ppermute | solution.py:655
  17.6 11.6 %collective-permute-start.1 = (f32[32,2048]{1,0:T(8,128)S(1)}, f32[32,2048]{1,0:T(8,128)S(1)}, u32[]{:S(2)}, u32[]{:S(2)}) collective-permute-start(f32[32,2048]{1,0:T(8,128)S(1)} %get-tuple-element.38), channel_id=1, source_target_pairs={{0,2},{1,3},{2,0},{3,1},{4,6},{5,7},{6,4},{7,5},{8,10},{9,11},{10,... | collective-permute-start | bytes 786440 | tf_op jit(solution)/shard_map/ppermute | solution.py:655
  19.0 12.6 %collective-permute-start.2 = (f32[32,2048]{1,0:T(8,128)S(1)}, f32[32,2048]{1,0:T(8,128)S(1)}, u32[]{:S(2)}, u32[]{:S(2)}) collective-permute-start(f32[32,2048]{1,0:T(8,128)S(1)} %get-tuple-element.39), channel_id=1, source_target_pairs={{0,3},{1,2},{2,1},{3,0},{4,7},{5,6},{6,5},{7,4},{8,11},{9,10},{10,... | collective-permute-start | bytes 786440 | tf_op jit(solution)/shard_map/ppermute | solution.py:655
  21.3 5.6 %collective-permute-start.13 = (f32[4,32,256]{2,1,0:T(8,128)S(1)}, f32[4,32,256]{2,1,0:T(8,128)S(1)}, u32[]{:S(2)}, u32[]{:S(2)}) collective-permute-start(f32[4,32,256]{2,1,0:T(8,128)S(1)} %get-tuple-element.44.refs_6_.ends_ref), channel_id=1, source_target_pairs={{0,4},{4,0},{8,12},{12,8},{16,20},{20,16},{24,28},{28,24},{1,5},{5... | collective-permute-start | bytes 393224 | tf_op jit(solution)/shard_map/ppermute | solution.py:696
  27.5 8.2 %collective-permute-start.14 = (f32[4,32,256]{2,1,0:T(8,128)S(1)}, f32[4,32,256]{2,1,0:T(8,128)S(1)}, u32[]{:S(2)}, u32[]{:S(2)}) collective-permute-start(f32[4,32,256]{2,1,0:T(8,128)S(1)} %join_ends.6.ends_ref), channel_id=1, source_target_pairs={{0,8},{4,12},{8,0},{12,4},{16,24},{20,28},{24,16},{28,20},{1,9},{5... | collective-permute-start | bytes 393224 | tf_op jit(solution)/shard_map/ppermute | solution.py:696
  33.3 8.0 %collective-permute-start.11 = (f32[27,16,128]{2,1,0:T(8,128)S(1)}, f32[27,16,128]{2,1,0:T(8,128)S(1)}, u32[]{:S(2)}, u32[]{:S(2)}) collective-permute-start(f32[27,16,128]{2,1,0:T(8,128)S(1)} %join_rows.1.refs_0_), channel_id=1, source_target_pairs={{0,1},{1,0},{2,3},{3,2},{4,5},{5,4},{6,7},{7,6},{8,9},{9,8},{10,11... | collective-permute-start | bytes 663560 | tf_op jit(solution)/shard_map/ppermute | solution.py:705
  33.4 7.9 %collective-permute-start.12 = (f32[27,16,128]{2,1,0:T(8,128)S(1)}, f32[27,16,128]{2,1,0:T(8,128)S(1)}, u32[]{:S(2)}, u32[]{:S(2)}) collective-permute-start(f32[27,16,128]{2,1,0:T(8,128)S(1)} %join_rows.1.refs_0_), channel_id=1, source_target_pairs={{0,3},{1,2},{2,1},{3,0},{4,7},{5,6},{6,5},{7,4},{8,11},{9,10},{10,... | collective-permute-start | bytes 663560 | tf_op jit(solution)/shard_map/ppermute | solution.py:706
  35.1 5.1 %collective-permute-start.8 = (f32[4,32,256]{2,1,0:T(8,128)S(1)}, f32[4,32,256]{2,1,0:T(8,128)S(1)}, u32[]{:S(2)}, u32[]{:S(2)}) collective-permute-start(f32[4,32,256]{2,1,0:T(8,128)S(1)} %get-tuple-element.46.ends_ref.after_ref), channel_id=1, source_target_pairs={{0,4},{4,0},{8,12},{12,8},{16,20},{20,16},{24,28},{28,24},{1,5},{5... | collective-permute-start | bytes 393224 | tf_op jit(solution)/shard_map/ppermute | solution.py:696
  36.3 8.3 %collective-permute-start.15 = (f32[4,32,256]{2,1,0:T(8,128)S(1)}, f32[4,32,256]{2,1,0:T(8,128)S(1)}, u32[]{:S(2)}, u32[]{:S(2)}) collective-permute-start(f32[4,32,256]{2,1,0:T(8,128)S(1)} %join_ends.7), channel_id=1, source_target_pairs={{0,16},{4,20},{8,24},{12,28},{16,0},{20,4},{24,8},{28,12},{1,17},{... | collective-permute-start | bytes 393224 | tf_op jit(solution)/shard_map/ppermute | solution.py:696
  40.7 7.3 %collective-permute-start.9 = (f32[4,32,256]{2,1,0:T(8,128)S(1)}, f32[4,32,256]{2,1,0:T(8,128)S(1)}, u32[]{:S(2)}, u32[]{:S(2)}) collective-permute-start(f32[4,32,256]{2,1,0:T(8,128)S(1)} %join_ends.4.ends_ref), channel_id=1, source_target_pairs={{0,8},{4,12},{8,0},{12,4},{16,24},{20,28},{24,16},{28,20},{1,9},{5... | collective-permute-start | bytes 393224 | tf_op jit(solution)/shard_map/ppermute | solution.py:696
  46.5 14.0 %collective-permute-start.19 = (f32[32,2048]{1,0:T(8,128)S(1)}, f32[32,2048]{1,0:T(8,128)S(1)}, u32[]{:S(2)}, u32[]{:S(2)}) collective-permute-start(f32[32,2048]{1,0:T(8,128)S(1)} %get-tuple-element.59), channel_id=1, source_target_pairs={{0,1},{1,0},{2,3},{3,2},{4,5},{5,4},{6,7},{7,6},{8,9},{9,8},{10,11... | collective-permute-start | bytes 786440 | tf_op jit(solution)/shard_map/ppermute | solution.py:655
  48.6 8.4 %collective-permute-start.10 = (f32[4,32,256]{2,1,0:T(8,128)S(1)}, f32[4,32,256]{2,1,0:T(8,128)S(1)}, u32[]{:S(2)}, u32[]{:S(2)}) collective-permute-start(f32[4,32,256]{2,1,0:T(8,128)S(1)} %join_ends.5), channel_id=1, source_target_pairs={{0,16},{4,20},{8,24},{12,28},{16,0},{20,4},{24,8},{28,12},{1,17},{... | collective-permute-start | bytes 393224 | tf_op jit(solution)/shard_map/ppermute | solution.py:696
  50.1 18.8 %collective-permute-start.20 = (f32[32,2048]{1,0:T(8,128)S(1)}, f32[32,2048]{1,0:T(8,128)S(1)}, u32[]{:S(2)}, u32[]{:S(2)}) collective-permute-start(f32[32,2048]{1,0:T(8,128)S(1)} %get-tuple-element.60), channel_id=1, source_target_pairs={{0,2},{1,3},{2,0},{3,1},{4,6},{5,7},{6,4},{7,5},{8,10},{9,11},{10,... | collective-permute-start | bytes 786440 | tf_op jit(solution)/shard_map/ppermute | solution.py:655
  50.3 18.6 %collective-permute-start.21 = (f32[32,2048]{1,0:T(8,128)S(1)}, f32[32,2048]{1,0:T(8,128)S(1)}, u32[]{:S(2)}, u32[]{:S(2)}) collective-permute-start(f32[32,2048]{1,0:T(8,128)S(1)} %get-tuple-element.61), channel_id=1, source_target_pairs={{0,3},{1,2},{2,1},{3,0},{4,7},{5,6},{6,5},{7,4},{8,11},{9,10},{10,... | collective-permute-start | bytes 786440 | tf_op jit(solution)/shard_map/ppermute | solution.py:655
  58.9 13.6 %collective-permute-start.16 = (f32[32,2048]{1,0:T(8,128)S(1)}, f32[32,2048]{1,0:T(8,128)S(1)}, u32[]{:S(2)}, u32[]{:S(2)}) collective-permute-start(f32[32,2048]{1,0:T(8,128)S(1)} %get-tuple-element.55), channel_id=1, source_target_pairs={{0,1},{1,0},{2,3},{3,2},{4,5},{5,4},{6,7},{7,6},{8,9},{9,8},{10,11... | collective-permute-start | bytes 786440 | tf_op jit(solution)/shard_map/ppermute | solution.py:655
  60.2 12.3 %collective-permute-start.17 = (f32[32,2048]{1,0:T(8,128)S(1)}, f32[32,2048]{1,0:T(8,128)S(1)}, u32[]{:S(2)}, u32[]{:S(2)}) collective-permute-start(f32[32,2048]{1,0:T(8,128)S(1)} %get-tuple-element.56), channel_id=1, source_target_pairs={{0,2},{1,3},{2,0},{3,1},{4,6},{5,7},{6,4},{7,5},{8,10},{9,11},{10,... | collective-permute-start | bytes 786440 | tf_op jit(solution)/shard_map/ppermute | solution.py:655
  60.5 14.5 %collective-permute-start.18 = (f32[32,2048]{1,0:T(8,128)S(1)}, f32[32,2048]{1,0:T(8,128)S(1)}, u32[]{:S(2)}, u32[]{:S(2)}) collective-permute-start(f32[32,2048]{1,0:T(8,128)S(1)} %get-tuple-element.57), channel_id=1, source_target_pairs={{0,3},{1,2},{2,1},{3,0},{4,7},{5,6},{6,5},{7,4},{8,11},{9,10},{10,... | collective-permute-start | bytes 786440 | tf_op jit(solution)/shard_map/ppermute | solution.py:655
